TPU v7x, 128 devices: a whole 4x4x4 slice. The times are simulated.
128 devices in a mesh: ckpt: 4 (over z_hi, core), fsdp: 32 (over x, y, z_lo).
Axes of the slice: x: 4, y: 4, z: 4 (z_hi: 2, z_lo: 2; z = z_hi * 2 + z_lo), core: 2. Of those that a mesh axis runs over, the one named last changes fastest.
Arguments:
- train_acts: bfloat16 [4, 4096, 4096], P('ckpt', 'fsdp'), may hold values from -6 to 6
- train_len: int32 [32, 2], replicated, may hold values from 16 to 64
- query_acts: bfloat16 [4, 256, 4096], P('ckpt', 'fsdp'), may hold values from -6 to 6
- query_len: int32 [2, 2], replicated, may hold values from 16 to 64
- norm_gain: bfloat16 [4, 4096], P('ckpt'), may hold values from 0.099609375 to 1.8984375
- up_weight: bfloat16 [4, 4096, 20480], P('ckpt', None, 'fsdp'), may hold values from -0.09375 to 0.09375
- readout: bfloat16 [4, 20480], P('ckpt', 'fsdp'), may hold values from -0.4 to 0.4
- lr_weight: float32 [4], P('ckpt'), may hold values from 0.25 to 1
Outputs:
- influence: float32 [32, 2], P('fsdp')
All inputs are finite; a program needn't handle non-finite values.
Results may differ from a plain program's by a relative error of at most 0.0055.
Values may be sent and summed in bfloat16 or wider, within the bound.
No kernel may reach another device: no remote copies, remote signals or barrier semaphores. Data moves between devices by JAX's collectives and lax.ppermute only.
A program may use at most 128 MiB of HBM per device.

v0:
```python
import jax
import jax.numpy as jnp
from jax import lax
from jax.sharding import PartitionSpec as P

LEN = 64
PAIR_DEV = 1
QPAIRS = 2


def normalize(values_in, gain_row):
    values = values_in.astype(jnp.float32)
    scale = lax.rsqrt(jnp.mean(values * values, axis=-1, keepdims=True) + 1e-05)
    return (values * scale * gain_row.astype(jnp.float32)).astype(jnp.bfloat16)


def token_weights(lengths):
    positions = jnp.arange(LEN, dtype=jnp.int32)
    live = (positions[None, None, :] < lengths[:, :, None]).astype(jnp.float32)
    return (live / lengths[:, :, None].astype(jnp.float32)).reshape(-1)


def seq_rewards(hidden, head, weights, count):
    terms = jnp.dot(jax.nn.silu(hidden), head.astype(jnp.float32), precision=lax.Precision.HIGHEST)
    return (terms * weights).reshape(count, 2, LEN).sum(axis=-1)


def token_slopes(rewards):
    slope = jax.nn.sigmoid(rewards[:, 1] - rewards[:, 0])
    signed = jnp.stack([-slope, slope], axis=1)
    return (signed[:, :, None] * jnp.ones((1, 1, LEN), jnp.float32)).reshape(-1)


def out_grads(hidden, head, factor):
    sig = jax.nn.sigmoid(hidden)
    deriv = sig * (1.0 + hidden * (1.0 - sig))
    return (factor[:, None] * head.astype(jnp.float32)[None, :] * deriv).astype(jnp.bfloat16)


def pair_scores(input_gram, output_gram, count):
    return (input_gram * output_gram).reshape(count, 2 * LEN, QPAIRS, 2 * LEN).sum(axis=(1, 3))


def local(train_acts, train_len, query_acts, query_len, norm_gain, up_weight, readout, lr_weight):
    pairs = train_len.shape[0]
    weight = up_weight[0]
    head = readout[0]
    normed_own = normalize(train_acts[0], norm_gain[0])
    query_own = normalize(query_acts[0], norm_gain[0])
    query_normed = lax.all_gather(query_own, "fsdp", axis=0, tiled=True)
    joined = jnp.dot(
        lax.all_gather(normed_own, "fsdp", axis=0, tiled=True),
        weight,
        preferred_element_type=jnp.float32,
    )
    query_hidden = jnp.dot(query_normed, weight, preferred_element_type=jnp.float32)
    train_weight = token_weights(train_len)
    query_weight = token_weights(query_len)
    train_part = seq_rewards(joined, head, train_weight, pairs)
    query_part = seq_rewards(query_hidden, head, query_weight, QPAIRS)
    train_reward, query_reward = lax.psum((train_part, query_part), "fsdp")
    grad_out = out_grads(joined, head, token_slopes(train_reward) * train_weight)
    query_grad = out_grads(query_hidden, head, token_slopes(query_reward) * query_weight)
    output_gram = lax.psum_scatter(
        jnp.dot(grad_out, query_grad.T, preferred_element_type=jnp.float32),
        "fsdp",
        scatter_dimension=0,
        tiled=True,
    )
    input_gram = jnp.dot(normed_own, query_normed.T, preferred_element_type=jnp.float32)
    own_scores = lr_weight[0] * pair_scores(input_gram, output_gram, PAIR_DEV)
    return lax.psum(own_scores, "ckpt")


def solution(mesh):
    return jax.shard_map(
        local,
        mesh=mesh,
        in_specs=(
            P("ckpt", "fsdp", None),
            P(),
            P("ckpt", "fsdp", None),
            P(),
            P("ckpt", None),
            P("ckpt", None, "fsdp"),
            P("ckpt", "fsdp"),
            P("ckpt"),
        ),
        out_specs=P("fsdp", None),
        check_vma=False,
    )
```

profile of v0, /device:TPU:1, one launch (start us, length us, event | category | flops | bytes accessed | tf_op | source)
XLA Modules:
  0.0 1189.3 jit_solution(1793512890996540077)
XLA Ops:
  6.5 0.7 mul.185
  7.3 1.0 fusion.18
  8.3 1.5 fusion.20
  9.9 1.5 fusion.8
  11.4 2.5 fusion.10
  14.0 0.7 convert_element_type.65
  14.7 0.8 copy.17
  15.5 0.1 copy.18
  15.6 0.1 fusion.21
  15.7 0.1 div.67
  15.8 0.7 convert_element_type.68
  16.5 0.8 fusion.24
  17.3 0.7 reduce.3
  18.0 127.3 %all-gather.3.cloned.1.call-done = bf16[256,4096]{1,0:T(8,128)(2,1)} async-done(((bf16[8,4096]{1,0:T(8,128)(2,1)}), bf16[256,4096]{1,0:T(8,128)(2,1)}) %all-gather.3.cloned.1.call-update) | async-done | bytes 2097168 | tf_op jit(solution)/shard_map/all_gather | solution.py:50
  145.3 4.9 fusion.2
  150.3 0.5 fusion.12
  150.7 0.3 copy-done.3
  151.2 0.1 reduce_sum.55
  151.3 725.6 %all-gather.5.cloned.1.call-done = bf16[4096,4096]{1,0:T(8,128)(2,1)} async-done(((bf16[128,4096]{1,0:T(8,128)(2,1)}), bf16[4096,4096]{1,0:T(8,128)(2,1)}) %all-gather.5.cloned.1.call-update) | async-done | bytes 33554448 | tf_op jit(solution)/shard_map/all_gather | solution.py:52
  876.8 31.5 %fusion.4 = f32[4096,640]{1,0:T(8,128)S(1)} fusion(bf16[4096,4096]{1,0:T(8,128)(2,1)} %all-gather.5.cloned.1.call-done, bf16[1,4096,640]{2,1,0:T(8,128)(2,1)} %param.13), kind=kOutput, calls=%fused_computation.6 | convolution fusion | flops 21474836480 | bytes 49283072 | tf_op jit(solution)/shard_map/dot_general | solution.py:51
  908.4 7.0 fusion
  915.4 0.1 reshape.107
  915.5 0.1 reduce_sum.54
  915.7 68.0 %all-reduce = (f32[32,2]{0,1:T(2,128)S(1)}, f32[2,2]{1,0:T(2,128)S(1)}) all-reduce(f32[32,2]{0,1:T(2,128)S(1)} %copy.21, f32[2,2]{1,0:T(2,128)S(1)} %reduce_sum.55), channel_id=1, replica_groups=mesh['ckpt'=4,'fsdp'=32] {'fsdp'}, use_global_device_ids=true, to_apply=%region_3.4 | all-reduce | flops 68 | bytes 544 | tf_op jit(solution)/shard_map/psum | solution.py:61
  984.0 0.1 copy.20
  984.1 0.1 mul.163
  984.2 0.1 reshape.108
  984.3 9.0 fusion.7
  994.1 155.7 %reduce-scatter.2.cloned.1.call-done = f32[128,256]{1,0:T(8,128)} async-done(((f32[4096,256]{1,0:T(8,128)}), f32[128,256]{1,0:T(8,128)}) %reduce-scatter.2.cloned.1.call-update) | async-done | bytes 131088 | tf_op jit(solution)/shard_map/reduce_scatter | solution.py:64
  1149.7 1.8 fusion.11
  1151.5 0.1 bitcast_reduce_fusion
  1151.6 31.1 %psum.23 = f32[1,2]{1,0:T(1,128)} all-reduce(f32[1,2]{1,0:T(1,128)S(1)} %multiply_bitcast_fusion), channel_id=1, replica_groups=mesh['ckpt'=4,'fsdp'=32] {'ckpt'}, use_global_device_ids=true, to_apply=%region_9.10 | all-reduce | flops 2 | bytes 16 | tf_op jit(solution)/shard_map/psum | solution.py:72
  (32 shorter events, 0.8 us)
Async XLA Ops:
  6.5 143.7 %copy-start.2 = (bf16[1,640]{1,0:T(2,128)(2,1)S(1)}, bf16[1,640]{1,0:T(2,128)(2,1)}, u32[]{:S(2)}) copy-start(bf16[1,640]{1,0:T(2,128)(2,1)} %param.14) | copy-start | bytes 3844
  6.5 138.8 %all-gather.3.cloned.1.call-start = ((), (), s32[]{:S(2)}) async-start(), calls=%async_computation.1 | async-start | bytes 2162688 | tf_op jit(solution)/shard_map/all_gather | solution.py:50
  9.9 867.0 %all-gather.5.cloned.1.call-start = ((), (), s32[]{:S(2)}) async-start(), calls=%async_computation.2 | async-start | bytes 34603008 | tf_op jit(solution)/shard_map/all_gather | solution.py:52
  14.0 1135.7 %reduce-scatter.2.cloned.1.call-start = ((), (), s32[]{:S(2)}) async-start(), calls=%async_computation.3 | async-start | bytes 4325376 | tf_op jit(solution)/shard_map/reduce_scatter | solution.py:64
  150.3 0.8 copy-start.3
  908.3 7.0 copy-start.4
  984.3 165.4 %copy-start = (bf16[128,4096]{1,0:T(8,128)(2,1)S(1)}, bf16[128,4096]{1,0:T(8,128)(2,1)}, u32[]{:S(2)}) copy-start(bf16[128,4096]{1,0:T(8,128)(2,1)} %fusion.10) | copy-start | bytes 3145732
  984.3 165.4 %copy-start.1 = (bf16[256,4096]{1,0:T(8,128)(2,1)S(1)}, bf16[256,4096]{1,0:T(8,128)(2,1)}, u32[]{:S(2)}) copy-start(bf16[256,4096]{1,0:T(8,128)(2,1)} %all-gather.3.cloned.1.call-done) | copy-start | bytes 6291460
Sparse Core Ops, SparseCore 0:
  10.0 135.2 all-gather.2
  147.0 729.8 all-gather.4
  993.5 156.1 reduce-scatter.1
where the time goes:
time: 1190 us
  waiting for transfers between devices  1010 us (85%)
  blocking collectives  99.1 us (8%)
  matrix products  54.7 us (5%)
  between operations  13.9 us (1%)
    all_gather x1, waiting for transfers between devices, local(): lax.all_gather(normed_own, 'fsdp', axis=0, tiled=True)  726 us
    reduce_scatter x1, waiting for transfers between devices, local(): lax.psum_scatter(jnp.dot(grad_out, query_grad.T, preferred_element_type=j...  156 us
    all_gather x1, waiting for transfers between devices, local(): query_normed = lax.all_gather(query_own, 'fsdp', axis=0, tiled=True)  127 us
    psum x1, blocking collectives, local(): train_reward, query_reward = lax.psum((train_part, query_part), 'fsdp')  68 us
    dot_general x1, matrix products, local(): jnp.dot(lax.all_gather(normed_own, 'fsdp', axis=0, tiled=True), weight, p...  31.5 us
    psum x1, blocking collectives, local(): return lax.psum(own_scores, 'ckpt')  31.1 us
  transfers between devices with their start and end apart: 3, of which 3 were waited for; matrix products, arithmetic and copies ran while one was open for 1% of the time, Pallas kernels for 0%

commit v1 on v0

v1 whole, which is shorter than its diff:
```python
import functools

import jax
import jax.numpy as jnp
from jax import lax
from jax.experimental import pallas as pl
from jax.experimental.pallas import tpu as pltpu
from jax.sharding import Mesh
from jax.sharding import PartitionSpec as P

LEN = 64
D = 4096
FD = 640
TILES = 5
NQ = 256
OFFS = (0, -1, 1, 2)
F32 = jnp.float32
BF16 = jnp.bfloat16


def ring(step):
    return [(i, (i + step) % 4) for i in range(4)]


def normalize(values_in, gain_row):
    values = values_in.astype(F32)
    scale = lax.rsqrt(jnp.mean(values * values, axis=-1, keepdims=True) + 1e-05)
    return (values * scale * gain_row.astype(F32)).astype(BF16)


def start_weights(wt, we, ws, sems):
    copies = []
    for j in range(TILES):
        cols = pl.ds(128 * j, 128)
        a = pltpu.make_async_copy(wt.at[:, cols], ws.at[j, :, pl.ds(0, 128)], sems.at[j, 0])
        b = pltpu.make_async_copy(we.at[:, cols], ws.at[j, :, pl.ds(128, 128)], sems.at[j, 1])
        a.start()
        b.start()
        copies.append((a, b))
    return copies


def activations(h):
    sig = 0.5 * jnp.tanh(0.5 * h) + 0.5
    act = h * sig
    return act, sig + act * (1.0 - sig)


def query_kernel(qa, qb, wt, we, head, qg_out, terms_out, xs, ws, acc, xsem, wsem):
    ca = pltpu.make_async_copy(qa, xs.at[pl.ds(0, 128)], xsem.at[0])
    cb = pltpu.make_async_copy(qb, xs.at[pl.ds(128, 128)], xsem.at[1])
    ca.start()
    cb.start()
    copies = start_weights(wt, we, ws, wsem)
    ca.wait()
    cb.wait()
    acc[...] = jnp.zeros_like(acc)
    for j in range(TILES):
        copies[j][0].wait()
        copies[j][1].wait()
        h = jnp.dot(xs[...], ws[j], preferred_element_type=F32)
        act, deriv = activations(h)
        row = head[:, 256 * j:256 * (j + 1)]
        acc[...] += act * row
        qg_out[:, 256 * j:256 * (j + 1)] = (row * row * deriv).astype(BF16)
    terms_out[...] = jnp.sum(acc[...], axis=1, keepdims=True)


def train_kernel(rows, *refs):
    n = len(rows)
    total = sum(rows)
    xin = refs[:n]
    lens, wt, we, qa, qb, qg, head, r_out, z_out, xs, qs, ws, acc, gram, xsem, qsem, wsem = refs[n:]
    xcopies = []
    at = 0
    for i in range(n):
        c = pltpu.make_async_copy(xin[i], xs.at[pl.ds(at, rows[i])], xsem.at[i])
        c.start()
        xcopies.append(c)
        at += rows[i]
    copies = start_weights(wt, we, ws, wsem)
    ca = pltpu.make_async_copy(qa, qs.at[pl.ds(0, 128)], qsem.at[0])
    cb = pltpu.make_async_copy(qb, qs.at[pl.ds(128, 128)], qsem.at[1])
    ca.start()
    cb.start()
    for c in xcopies:
        c.wait()
    acc[...] = jnp.zeros_like(acc)
    gram[...] = jnp.zeros_like(gram)
    for j in range(TILES):
        copies[j][0].wait()
        copies[j][1].wait()
        row = head[:, 256 * j:256 * (j + 1)]

        @pl.loop(0, total // 256)
        def _(k, j=j, row=row):
            part = pl.ds(pl.multiple_of(k * 256, 256), 256)
            h = jnp.dot(xs[part, :], ws[j], preferred_element_type=F32)
            act, deriv = activations(h)
            acc[part, :] += act * row
            gram[part, :] += lax.dot_general(
                deriv.astype(BF16), qg[:, 256 * j:256 * (j + 1)], (((1,), (1,)), ((), ())), preferred_element_type=F32
            )
    ca.wait()
    cb.wait()

    @pl.loop(0, total // 256)
    def _(k):
        part = pl.ds(pl.multiple_of(k * 256, 256), 256)
        gram[part, :] = gram[part, :] * lax.dot_general(
            xs[part, :], qs[...], (((1,), (1,)), ((), ())), preferred_element_type=F32
        )

    position = lax.broadcasted_iota(jnp.int32, (LEN, 1), 0)
    for s in range(total // LEN):
        length = lens[s]
        weight = jnp.where(position < length, 1.0 / length.astype(F32), 0.0)
        r_out[s:s + 1, :] = jnp.sum(acc[LEN * s:LEN * (s + 1), :] * weight, axis=0, keepdims=True)
        z_out[s:s + 1, :] = jnp.sum(gram[LEN * s:LEN * (s + 1), :] * weight, axis=0, keepdims=True)


ANY = pl.BlockSpec(memory_space=pl.ANY)
VM = pl.BlockSpec(memory_space=pltpu.VMEM)
SM = pl.BlockSpec(memory_space=pltpu.SMEM)


def query_call(qa, qb, wt, we, head):
    return pl.pallas_call(
        query_kernel,
        out_shape=(jax.ShapeDtypeStruct((NQ, 2 * FD), BF16), jax.ShapeDtypeStruct((NQ, 1), F32)),
        in_specs=[ANY, ANY, ANY, ANY, VM],
        out_specs=(VM, VM),
        scratch_shapes=[
            pltpu.VMEM((NQ, D), BF16),
            pltpu.VMEM((TILES, D, 256), BF16),
            pltpu.VMEM((NQ, 256), F32),
            pltpu.SemaphoreType.DMA((2,)),
            pltpu.SemaphoreType.DMA((TILES, 2)),
        ],
        compiler_params=pltpu.CompilerParams(vmem_limit_bytes=40 * 2**20),
        cost_estimate=pl.CostEstimate(flops=2 * NQ * D * 2 * FD, bytes_accessed=13 * 2**20, transcendentals=NQ * 2 * FD),
        name="query_side",
    )(qa, qb, wt, we, head)


def train_call(xin, lens, wt, we, qa, qb, qg, head):
    rows = tuple(x.shape[0] for x in xin)
    total = sum(rows)
    return pl.pallas_call(
        functools.partial(train_kernel, rows),
        out_shape=(jax.ShapeDtypeStruct((total // LEN, 256), F32),) * 2,
        in_specs=[ANY] * len(rows) + [SM, ANY, ANY, ANY, ANY, VM, VM],
        out_specs=(VM, VM),
        scratch_shapes=[
            pltpu.VMEM((total, D), BF16),
            pltpu.VMEM((NQ, D), BF16),
            pltpu.VMEM((TILES, D, 256), BF16),
            pltpu.VMEM((total, 256), F32),
            pltpu.VMEM((total, 256), F32),
            pltpu.SemaphoreType.DMA((len(rows),)),
            pltpu.SemaphoreType.DMA((2,)),
            pltpu.SemaphoreType.DMA((TILES, 2)),
        ],
        compiler_params=pltpu.CompilerParams(vmem_limit_bytes=40 * 2**20),
        cost_estimate=pl.CostEstimate(
            flops=2 * total * D * (2 * FD + NQ), bytes_accessed=13 * 2**20 + total * D * 2, transcendentals=total * 2 * FD
        ),
        name="train_side",
    )(*xin, lens, wt, we, qa, qb, qg, head)


def ring_gather_start(block, axis):
    low = lax.ppermute(block, axis, ring(1))
    high = lax.ppermute(block, axis, ring(-1))
    return low, high


def ring_gather_finish(low, high, axis):
    half = low.shape[0] // 2
    far_a = lax.ppermute(low[:half], axis, ring(1))
    far_b = lax.ppermute(high[half:], axis, ring(-1))
    return far_a, far_b


def local(train_acts, train_len, query_acts, query_len, norm_gain, up_weight, readout, lr_weight):
    core = lax.axis_index("c")
    turn = functools.partial(lax.ppermute, axis_name=("c", "zl"), perm=[(0, 0), (1, 2), (2, 1), (3, 3)])
    swap = functools.partial(lax.ppermute, axis_name="c", perm=[(0, 1), (1, 0)])

    normed = normalize(train_acts[0], norm_gain[0])
    query_own = normalize(query_acts[0], norm_gain[0])
    own = turn(normed)
    query_turned = turn(query_own)
    small = jnp.concatenate([readout[0].astype(F32), lr_weight, jnp.zeros((127,), F32)]).reshape(1, FD + 128)
    small = turn(small)
    small_other = swap(small)
    lr = small[0, FD]
    head = jnp.stack(
        [small[0, :FD].reshape(TILES, 128), small_other[0, :FD].reshape(TILES, 128)], axis=1
    ).reshape(1, 2 * FD)

    weight_in, own = lax.optimization_barrier((up_weight[0], own))
    wt = turn(weight_in)
    we = swap(wt)
    qa = lax.all_gather(query_turned, ("x", "y"), axis=0, tiled=True)
    qb = swap(qa)

    one, two = own[:LEN], own[LEN:]
    one_low, one_high = ring_gather_start(one, "x")
    two_low, two_high = ring_gather_start(two, "y")
    one_a, one_b = ring_gather_finish(one_low, one_high, "x")
    two_a, two_b = ring_gather_finish(two_low, two_high, "y")
    g1 = jnp.concatenate([one, one_low, one_high, one_a, one_b], axis=0)
    g2 = jnp.concatenate([two, two_low, two_high, two_a, two_b], axis=0)
    g1_low, g1_high = ring_gather_start(g1, "y")
    g2_low, g2_high = ring_gather_start(g2, "x")
    g1_a, g1_b = ring_gather_finish(g1_low, g1_high, "y")
    g2_a, g2_b = ring_gather_finish(g2_low, g2_high, "x")

    lens = lax.dynamic_index_in_dim(train_len.reshape(4, 4, 2, 2), core, 2, keepdims=False)
    places = jnp.array(OFFS, jnp.int32)
    lens = jnp.take(lens, (places + lax.axis_index("x")) % 4, axis=0)
    lens = jnp.take(lens, (places + lax.axis_index("y")) % 4, axis=1)

    i = jnp.arange(NQ, dtype=jnp.int32)
    side = jnp.where(i < 128, core, 1 - core)
    inner = i % 128
    qseq = inner // 32
    qpos = 16 * ((inner // 8) % 4) + 8 * side + inner % 8
    qlen = jnp.take(query_len.reshape(-1), qseq)
    qw = jnp.where(qpos < qlen, 1.0 / qlen.astype(F32), 0.0)
    pick = (qseq[:, None] == jnp.arange(4)[None, :]).astype(F32) * qw[:, None]

    qg, qterms = query_call(qa, qb, wt, we, head)
    qreward = jnp.sum(qterms * pick, axis=0)

    run = lambda xin, ls: train_call(xin, ls, wt, we, qa, qb, qg, head)
    r_c, z_c = run((g1, g2), jnp.concatenate([lens[:, 0, 0], lens[0, :, 1]]))
    r_1, z_1 = run((g1_low, g1_high), jnp.concatenate([lens[:, 1, 0], lens[:, 2, 0]]))
    r_2, z_2 = run((g2_low, g2_high), jnp.concatenate([lens[1, :, 1], lens[2, :, 1]]))
    r_f, z_f = run((g1_a, g1_b, g2_a, g2_b), jnp.concatenate([lens[:, 3, 0], lens[3, :, 1]]))
    order = lambda c, a, b, f: jnp.stack(
        [
            jnp.stack([c[:4], a[:4], a[4:], f[:4]], axis=1),
            jnp.stack([c[4:], b[:4], b[4:], f[4:]], axis=0),
        ]
    )
    rewards = jnp.sum(order(r_c, r_1, r_2, r_f), axis=-1, keepdims=True)
    scores = jnp.sum(order(z_c, z_1, z_2, z_f)[..., None] * pick, axis=-2)
    values = jnp.concatenate([rewards, scores], axis=-1)

    def spread(parts, query, axis):
        sent = [jnp.concatenate([p.reshape(1, -1), query.reshape(1, -1)], axis=1) for p in parts]
        total = sent[0]
        for k in (1, 2, 3):
            total = total + lax.ppermute(sent[k], axis, ring(OFFS[k]))
        return total[0, :-4].reshape(parts[0].shape), total[0, -4:]

    values, qreward = spread([values[:, k] for k in range(4)], qreward, "x")
    values, qreward = spread([values[:, k] for k in range(4)], qreward, "y")

    slope = jax.nn.sigmoid(values[1, 0] - values[0, 0])
    qr = qreward.reshape(2, 2)
    qslope = jax.nn.sigmoid(qr[:, 1] - qr[:, 0])
    by_query = (slope * (values[1, 1:] - values[0, 1:])).reshape(2, 2)
    mine = lr * qslope * (by_query[:, 1] - by_query[:, 0])
    mine = jnp.concatenate([mine, jnp.zeros((126,), F32)]).reshape(1, 128)
    total = jnp.zeros((1, 128), F32)
    for a in (0, 1):
        for b in (0, 1):
            perm = []
            for zh in (0, 1):
                for q in (0, 1):
                    for c in (0, 1):
                        perm.append((4 * (zh ^ a) + 2 * q + (c ^ b), 4 * zh + 2 * c + q))
            total = total + lax.ppermute(mine, ("zh", "c", "zl"), perm)
    return total[:, :2]


def solution(mesh):
    full = Mesh(mesh.devices.reshape(2, 2, 4, 4, 2), ("zh", "c", "x", "y", "zl"))
    ckpt, fsdp = ("zh", "c"), ("x", "y", "zl")
    return jax.shard_map(
        local,
        mesh=full,
        in_specs=(
            P(ckpt, fsdp, None),
            P(),
            P(ckpt, fsdp, None),
            P(),
            P(ckpt, None),
            P(ckpt, None, fsdp),
            P(ckpt, fsdp),
            P(ckpt),
        ),
        out_specs=P(fsdp, None),
        check_vma=False,
    )
```

time: 1190 us -> 294 us (0.25)
  waiting for transfers between devices: 1010 us -> 125 us
  blocking collectives: 99.1 us -> 0 us
  Pallas kernels: 0 us -> 66.1 us
  matrix products: 54.7 us -> 0 us
  starting transfers between devices: 0.09 us -> 53.3 us
  local copies, waits for them, and re-layouts: 2.06 us -> 20.5 us
    all_gather x2 -> x1, waiting for transfers between devices: 853 us -> 14.5 us  [local(): qa = lax.all_gather(query_turned, ('x', 'y'), axis=0, tiled=True)]
    reduce_scatter x1 -> x0, waiting for transfers between devices: 156 us -> none  [local(): lax.psum_scatter(jnp.dot(grad_out, query_grad.T, preferred_element_type=j...]
    ppermute x0 -> x33, waiting for transfers between devices: none -> 111 us  [the longest x1 46.8 us: local(): small = turn(small)]
    psum x2 -> x0, blocking collectives: 99.1 us -> none  [the longest x1 68 us: local(): train_reward, query_reward = lax.psum((train_part, query_part), 'fsdp')]
    pallas_call x0 -> x5, Pallas kernels: none -> 66.1 us  [the longest x4 58.4 us: train_call(): pl.pallas_call(functools.partial(train_kernel, rows), out_shape=(jax.Shap...]
    dot_general x6 -> x0, matrix products: 54.7 us -> none  [the longest x1 31.5 us: local(): jnp.dot(lax.all_gather(normed_own, 'fsdp', axis=0, tiled=True), weight, p...]
    ppermute x0 -> x33, starting transfers between devices: none -> 53.3 us  [the longest x4 11.8 us: local(): total = total + lax.ppermute(mine, ('zh', 'c', 'zl'), perm)]
  transfers between devices with their start and end apart: 3 -> 34, of which waited for: 3 -> 13; matrix products, arithmetic and copies ran while one was open for 1% -> 8% of each run, Pallas kernels for 0% -> 8%
where the time goes in v1:
time: 294 us; the launch traced here: 291 us
  waiting for transfers between devices  125 us (43%)
  Pallas kernels  66.1 us (22%)
  starting transfers between devices  53.3 us (18%)
  local copies, waits for them, and re-layouts  20.5 us (7%)
  between operations  16.1 us (5%)
  other arithmetic  9.47 us (3%)
    pallas_call x4, Pallas kernels, train_call(): pl.pallas_call(functools.partial(train_kernel, rows), out_shape=(jax.Shap...  58.4 us
    ppermute x1, waiting for transfers between devices, local(): small = turn(small)  46.8 us
    ppermute x4, waiting for transfers between devices, ring_gather_start(): high = lax.ppermute(block, axis, ring(-1))  30 us
    all_gather x1, waiting for transfers between devices, local(): qa = lax.all_gather(query_turned, ('x', 'y'), axis=0, tiled=True)  14.5 us
    ppermute x1, waiting for transfers between devices, local(): own = turn(normed)  12.5 us
    ppermute x4, starting transfers between devices, local(): total = total + lax.ppermute(mine, ('zh', 'c', 'zl'), perm)  11.8 us
    ppermute x4, starting transfers between devices, ring_gather_start(): high = lax.ppermute(block, axis, ring(-1))  9.41 us
    ppermute x4, starting transfers between devices, ring_gather_finish(): far_b = lax.ppermute(high[half:], axis, ring(-1))  8.15 us
  transfers between devices with their start and end apart: 34, of which 13 were waited for; matrix products, arithmetic and copies ran while one was open for 8% of the time, Pallas kernels for 8%

profile of v1, /device:TPU:1, one launch (start us, length us, event | category | flops | bytes accessed | tf_op | source)
XLA Modules:
  0.0 290.5 jit_solution(10505835129439116961)
XLA Ops:
  10.4 4.9 %collective-permute-start.1 = (bf16[128,4096]{1,0:T(8,128)(2,1)S(1)}, bf16[128,4096]{1,0:T(8,128)(2,1)S(1)}, u32[]{:S(2)}, u32[]{:S(2)}) collective-permute-start(bf16[128,4096]{1,0:T(8,128)(2,1)S(1)} %fusion.2), channel_id=1, source_target_pairs={{0,0},{1,32},{32,1},{33,33},{2,2},{3,34},{34,3},{35,35},{4,4},{5,3... | collective-permute-start | bytes 3145736 | tf_op jit(solution)/shard_map/ppermute | solution.py:192
  15.4 12.5 %collective-permute-done.1 = bf16[128,4096]{1,0:T(8,128)(2,1)S(1)} collective-permute-done((bf16[128,4096]{1,0:T(8,128)(2,1)S(1)}, bf16[128,4096]{1,0:T(8,128)(2,1)S(1)}, u32[]{:S(2)}, u32[]{:S(2)}) %collective-permute-start.1) | collective-permute-done | bytes 1048608 | tf_op jit(solution)/shard_map/ppermute | solution.py:192
  27.8 3.6 %collective-permute-start.10 = (bf16[4096,640]{1,0:T(8,128)(2,1)}, bf16[4096,640]{1,0:T(8,128)(2,1)}, u32[]{:S(2)}, u32[]{:S(2)}) collective-permute-start(bf16[4096,640]{1,0:T(8,128)(2,1)} %bitcast.76), channel_id=1, source_target_pairs={{0,0},{1,32},{32,1},{33,33},{2,2},{3,34},{34,3},{35,35},{4,4},{5,3... | collective-permute-start | bytes 15728648 | tf_op jit(solution)/shard_map/ppermute | solution.py:203
  32.2 1.9 collective-permute-start
  34.4 3.6 %collective-permute-start.12 = (bf16[8,4096]{1,0:T(8,128)(2,1)S(1)}, bf16[8,4096]{1,0:T(8,128)(2,1)S(1)}, u32[]{:S(2)}, u32[]{:S(2)}) collective-permute-start(bf16[8,4096]{1,0:T(8,128)(2,1)S(1)} %fusion.5), channel_id=1, source_target_pairs={{0,0},{1,32},{32,1},{33,33},{2,2},{3,34},{34,3},{35,35},{4,4},{5,3... | collective-permute-start | bytes 196616 | tf_op jit(solution)/shard_map/ppermute | solution.py:193
  39.7 2.7 collective-permute-start.7
  42.4 46.8 %collective-permute-done = f32[1,768]{1,0:T(1,128)S(1)} collective-permute-done((f32[1,768]{1,0:T(1,128)S(1)}, f32[1,768]{1,0:T(1,128)S(1)}, u32[]{:S(2)}, u32[]{:S(2)}) %collective-permute-start) | collective-permute-done | bytes 3104 | tf_op jit(solution)/shard_map/ppermute | solution.py:195
  89.2 2.5 collective-permute-start.3
  93.2 2.8 collective-permute-start.9
  97.0 4.2 %collective-permute-done.2 = bf16[64,4096]{1,0:T(8,128)(2,1)} collective-permute-done((bf16[64,4096]{1,0:T(8,128)(2,1)}, bf16[64,4096]{1,0:T(8,128)(2,1)}, u32[]{:S(2)}, u32[]{:S(2)}) %collective-permute-start.2) | collective-permute-done | bytes 524320 | tf_op jit(solution)/shard_map/ppermute | solution.py:173
  104.8 2.3 constant_dynamic-update-slice_fusion.3
  108.0 2.7 collective-permute-done.4
  111.4 6.2 %collective-permute-done.5 = bf16[32,4096]{1,0:T(8,128)(2,1)S(1)} collective-permute-done((bf16[32,4096]{1,0:T(8,128)(2,1)S(1)}, bf16[32,4096]{1,0:T(8,128)(2,1)S(1)}, u32[]{:S(2)}, u32[]{:S(2)}) %collective-permute-start.5) | collective-permute-done | bytes 262176 | tf_op jit(solution)/shard_map/ppermute | solution.py:181
  122.3 2.5 collective-permute-start.21
  125.6 14.5 %all-gather.2.cloned.1.call-done.qa.refs_5_.refs_7_ = bf16[128,4096]{1,0:T(8,128)(2,1)} async-done(((bf16[8,4096]{1,0:T(8,128)(2,1)}), bf16[128,4096]{1,0:T(8,128)(2,1)}) %all-gather.2.cloned.1.call-update) | async-done | bytes 1048592 | tf_op jit(solution)/shard_map/all_gather | solution.py:205
  140.0 30.0 %collective-permute-done.16.refs_1_ = bf16[256,4096]{1,0:T(8,128)(2,1)S(1)} collective-permute-done((bf16[256,4096]{1,0:T(8,128)(2,1)}, bf16[256,4096]{1,0:T(8,128)(2,1)S(1)}, u32[]{:S(2)}, u32[]{:S(2)}) %collective-permute-start.16) | collective-permute-done | bytes 2097184 | tf_op jit(solution)/shard_map/ppermute | solution.py:174
  171.6 2.5 compare_select_fusion.1
  174.8 2.9 %collective-permute-start.18 = (bf16[128,4096]{1,0:T(8,128)(2,1)S(1)}, bf16[128,4096]{1,0:T(8,128)(2,1)S(1)}, u32[]{:S(2)}, u32[]{:S(2)}) collective-permute-start(bf16[128,4096]{1,0:T(8,128)(2,1)S(1)} %slice.253), channel_id=1, source_target_pairs={{0,6},{2,0},{4,2},{6,4},{1,7},{3,1},{5,3},{7,5},{8,14},{10,8},{12,... | collective-permute-start | bytes 3145736 | tf_op jit(solution)/shard_map/ppermute | solution.py:181
  180.5 2.4 collective-permute-start.22
  184.5 7.8 %query_side.1 = (bf16[256,1280]{1,0:T(8,128)(2,1)S(1)}, f32[256,1]{1,0:T(8,128)S(1)}) custom-call(bf16[128,4096]{1,0:T(8,128)(2,1)S(1)} %copy-done, bf16[128,4096]{1,0:T(8,128)(2,1)S(1)} %collective-permute-done.13.qb.refs_6_.refs_8_, bf16[4096,640]{1,0:T(8,128)(2,1)} %collective-permute-done.10.wt.refs_3_.refs_5_, ...), custom_call_target="tpu_custom_call" | custom-call | flops 2684354560 | bytes 13631488 | tf_op jit(solution)/shard_map/query_side/pallas_call | solution.py:128
  192.2 16.9 %train_side.7 = (f32[8,256]{1,0:T(8,128)S(1)}, f32[8,256]{1,0:T(8,128)S(1)}) custom-call(bf16[256,4096]{1,0:T(8,128)(2,1)} %collective-permute-done.19.refs_0_, bf16[256,4096]{1,0:T(8,128)(2,1)} %collective-permute-done.21.refs_1_, s32[8]{0:T(128)S(1)} %pad_add_fusion.3.refs_2_, bf16[4096,640]{1,0:T(8,128)(2,1)} %collective-permute-done.10.wt.refs_3_.refs_5_, ...), custom_call_target="tpu_custom_call" | custom-call | flops 6442450944 | bytes 17825792 | tf_op jit(solution)/shard_map/train_side/pallas_call | solution.py:149
  209.8 13.6 %train_side.6 = (f32[8,256]{1,0:T(8,128)S(1)}, f32[8,256]{1,0:T(8,128)S(1)}) custom-call(bf16[128,4096]{1,0:T(8,128)(2,1)S(1)} %collective-permute-done.17.refs_0_, bf16[128,4096]{1,0:T(8,128)(2,1)S(1)} %collective-permute-done.18.refs_1_, bf16[128,4096]{1,0:T(8,128)(2,1)S(1)} %collective-permute-done.20.refs_2_, ...), custom_call_target="tpu_custom_call" | custom-call | flops 6442450944 | bytes 17825792 | tf_op jit(solution)/shard_map/train_side/pallas_call | solution.py:149
  223.4 14.0 %train_side.5 = (f32[8,256]{1,0:T(8,128)S(1)}, f32[8,256]{1,0:T(8,128)S(1)}) custom-call(bf16[256,4096]{1,0:T(8,128)(2,1)} %collective-permute-done.15.refs_0_, bf16[256,4096]{1,0:T(8,128)(2,1)S(1)} %collective-permute-done.16.refs_1_, s32[8]{0:T(128)S(1)} %pad_add_fusion.1.refs_2_, bf16[4096,640]{1,0:T(8,128)(2,1)} %collective-permute-done.10.wt.refs_3_.refs_5_, ...), custom_call_target="tpu_custom_call" | custom-call | flops 6442450944 | bytes 17825792 | tf_op jit(solution)/shard_map/train_side/pallas_call | solution.py:149
  237.4 13.9 %train_side.4 = (f32[8,256]{1,0:T(8,128)S(1)}, f32[8,256]{1,0:T(8,128)S(1)}) custom-call(bf16[256,4096]{1,0:T(8,128)(2,1)} %constant_dynamic-update-slice_fusion.refs_0_, bf16[256,4096]{1,0:T(8,128)(2,1)S(1)} %copy-done.2, s32[8]{0:T(128)S(1)} %pad_add_fusion.refs_2_, bf16[4096,640]{1,0:T(8,128)(2,1)} %collective-permute-done.10.wt.refs_3_.refs_5_, ...), custom_call_target="tpu_custom_call" | custom-call | flops 6442450944 | bytes 17825792 | tf_op jit(solution)/shard_map/train_side/pallas_call | solution.py:149
  252.6 2.1 collective-permute-start.23
  256.0 2.2 collective-permute-done.24
  259.3 2.6 collective-permute-start.26
  263.1 2.3 collective-permute-done.27
  269.0 4.5 %collective-permute-start.32 = (f32[1,128]{1,0:T(1,128)S(1)}, f32[1,128]{1,0:T(1,128)S(1)}, u32[]{:S(2)}, u32[]{:S(2)}) collective-permute-start(f32[1,128]{1,0:T(1,128)S(1)} %pad_bitcast_fusion), channel_id=1, source_target_pairs={{65,0},{64,32},{97,1},{96,33},{1,64},{0,96},{33,65},{32,97},{67,2}... | collective-permute-start | bytes 1544 | tf_op jit(solution)/shard_map/ppermute | solution.py:276
  273.5 4.0 %collective-permute-start.31 = (f32[1,128]{1,0:T(1,128)S(1)}, f32[1,128]{1,0:T(1,128)S(1)}, u32[]{:S(2)}, u32[]{:S(2)}) collective-permute-start(f32[1,128]{1,0:T(1,128)S(1)} %pad_bitcast_fusion), channel_id=1, source_target_pairs={{64,0},{65,32},{96,1},{97,33},{0,64},{1,96},{32,65},{33,97},{66,2}... | collective-permute-start | bytes 1544 | tf_op jit(solution)/shard_map/ppermute | solution.py:276
  278.3 2.5 collective-permute-start.29
  280.8 2.4 collective-permute-done.29
  (166 shorter events, 34.2 us)
Async XLA Ops:
  6.5 133.5 %all-gather.2.cloned.1.call-start = ((), (), s32[]{:S(2)}) async-start(), calls=%async_computation | async-start | bytes 1114112 | tf_op jit(solution)/shard_map/all_gather | solution.py:205
  10.4 17.4 %collective-permute-start.1 = (bf16[128,4096]{1,0:T(8,128)(2,1)S(1)}, bf16[128,4096]{1,0:T(8,128)(2,1)S(1)}, u32[]{:S(2)}, u32[]{:S(2)}) collective-permute-start(bf16[128,4096]{1,0:T(8,128)(2,1)S(1)} %fusion.2), channel_id=1, source_target_pairs={{0,0},{1,32},{32,1},{33,33},{2,2},{3,34},{34,3},{35,35},{4,4},{5,3... | collective-permute-start | bytes 3145736 | tf_op jit(solution)/shard_map/ppermute | solution.py:192
  27.8 76.9 %collective-permute-start.10 = (bf16[4096,640]{1,0:T(8,128)(2,1)}, bf16[4096,640]{1,0:T(8,128)(2,1)}, u32[]{:S(2)}, u32[]{:S(2)}) collective-permute-start(bf16[4096,640]{1,0:T(8,128)(2,1)} %bitcast.76), channel_id=1, source_target_pairs={{0,0},{1,32},{32,1},{33,33},{2,2},{3,34},{34,3},{35,35},{4,4},{5,3... | collective-permute-start | bytes 15728648 | tf_op jit(solution)/shard_map/ppermute | solution.py:203
  32.2 57.0 %collective-permute-start = (f32[1,768]{1,0:T(1,128)S(1)}, f32[1,768]{1,0:T(1,128)S(1)}, u32[]{:S(2)}, u32[]{:S(2)}) collective-permute-start(f32[1,768]{1,0:T(1,128)S(1)} %reshape.238), channel_id=1, source_target_pairs={{0,0},{1,32},{32,1},{33,33},{2,2},{3,34},{34,3},{35,35},{4,4},{5,3... | collective-permute-start | bytes 9224 | tf_op jit(solution)/shard_map/ppermute | solution.py:195
  34.4 57.3 %collective-permute-start.12 = (bf16[8,4096]{1,0:T(8,128)(2,1)S(1)}, bf16[8,4096]{1,0:T(8,128)(2,1)S(1)}, u32[]{:S(2)}, u32[]{:S(2)}) collective-permute-start(bf16[8,4096]{1,0:T(8,128)(2,1)S(1)} %fusion.5), channel_id=1, source_target_pairs={{0,0},{1,32},{32,1},{33,33},{2,2},{3,34},{34,3},{35,35},{4,4},{5,3... | collective-permute-start | bytes 196616 | tf_op jit(solution)/shard_map/ppermute | solution.py:193
  39.7 53.4 %collective-permute-start.7 = (bf16[64,4096]{1,0:T(8,128)(2,1)}, bf16[64,4096]{1,0:T(8,128)(2,1)S(1)}, u32[]{:S(2)}, u32[]{:S(2)}) collective-permute-start(bf16[64,4096]{1,0:T(8,128)(2,1)} %get-tuple-element.41), channel_id=1, source_target_pairs={{0,6},{2,0},{4,2},{6,4},{1,7},{3,1},{5,3},{7,5},{8,14},{10,8},{12,... | collective-permute-start | bytes 1572872 | tf_op jit(solution)/shard_map/ppermute | solution.py:174
  42.4 50.8 %collective-permute-start.6 = (bf16[64,4096]{1,0:T(8,128)(2,1)}, bf16[64,4096]{1,0:T(8,128)(2,1)}, u32[]{:S(2)}, u32[]{:S(2)}) collective-permute-start(bf16[64,4096]{1,0:T(8,128)(2,1)} %get-tuple-element.41), channel_id=1, source_target_pairs={{0,2},{2,4},{4,6},{6,0},{1,3},{3,5},{5,7},{7,1},{8,10},{10,12},{12... | collective-permute-start | bytes 1572872 | tf_op jit(solution)/shard_map/ppermute | solution.py:173
  89.2 14.3 %collective-permute-start.3 = (bf16[64,4096]{1,0:T(8,128)(2,1)}, bf16[64,4096]{1,0:T(8,128)(2,1)S(1)}, u32[]{:S(2)}, u32[]{:S(2)}) collective-permute-start(bf16[64,4096]{1,0:T(8,128)(2,1)} %get-tuple-element.44), channel_id=1, source_target_pairs={{0,24},{8,0},{16,8},{24,16},{1,25},{9,1},{17,9},{25,17},{2,26},{10... | collective-permute-start | bytes 1572872 | tf_op jit(solution)/shard_map/ppermute | solution.py:174
  91.7 9.6 %collective-permute-start.2 = (bf16[64,4096]{1,0:T(8,128)(2,1)}, bf16[64,4096]{1,0:T(8,128)(2,1)}, u32[]{:S(2)}, u32[]{:S(2)}) collective-permute-start(bf16[64,4096]{1,0:T(8,128)(2,1)} %get-tuple-element.44), channel_id=1, source_target_pairs={{0,8},{8,16},{16,24},{24,0},{1,9},{9,17},{17,25},{25,1},{2,10},{10... | collective-permute-start | bytes 1572872 | tf_op jit(solution)/shard_map/ppermute | solution.py:173
  93.1 31.7 %collective-permute-start.14 = (f32[1,768]{1,0:T(1,128)S(1)}, f32[1,768]{1,0:T(1,128)S(1)}, u32[]{:S(2)}, u32[]{:S(2)}) collective-permute-start(f32[1,768]{1,0:T(1,128)S(1)} %collective-permute-done), channel_id=1, source_target_pairs={{0,32},{32,0},{1,33},{33,1},{2,34},{34,2},{3,35},{35,3},{4,36},{36... | collective-permute-start | bytes 9224 | tf_op jit(solution)/shard_map/ppermute | solution.py:196
  93.2 28.4 %collective-permute-start.9 = (bf16[32,4096]{1,0:T(8,128)(2,1)S(1)}, bf16[32,4096]{1,0:T(8,128)(2,1)S(1)}, u32[]{:S(2)}, u32[]{:S(2)}) collective-permute-start(bf16[32,4096]{1,0:T(8,128)(2,1)S(1)} %slice.245), channel_id=1, source_target_pairs={{0,6},{2,0},{4,2},{6,4},{1,7},{3,1},{5,3},{7,5},{8,14},{10,8},{12,... | collective-permute-start | bytes 786440 | tf_op jit(solution)/shard_map/ppermute | solution.py:181
  101.2 19.6 %collective-permute-start.8 = (bf16[32,4096]{1,0:T(8,128)(2,1)S(1)}, bf16[32,4096]{1,0:T(8,128)(2,1)S(1)}, u32[]{:S(2)}, u32[]{:S(2)}) collective-permute-start(bf16[32,4096]{1,0:T(8,128)(2,1)S(1)} %slice.244), channel_id=1, source_target_pairs={{0,2},{2,4},{4,6},{6,0},{1,3},{3,5},{5,7},{7,1},{8,10},{10,12},{12... | collective-permute-start | bytes 786440 | tf_op jit(solution)/shard_map/ppermute | solution.py:180
  103.5 7.1 %collective-permute-start.4 = (bf16[32,4096]{1,0:T(8,128)(2,1)S(1)}, bf16[32,4096]{1,0:T(8,128)(2,1)S(1)}, u32[]{:S(2)}, u32[]{:S(2)}) collective-permute-start(bf16[32,4096]{1,0:T(8,128)(2,1)S(1)} %slice.242), channel_id=1, source_target_pairs={{0,8},{8,16},{16,24},{24,0},{1,9},{9,17},{17,25},{25,1},{2,10},{10... | collective-permute-start | bytes 786440 | tf_op jit(solution)/shard_map/ppermute | solution.py:180
  104.7 79.7 %collective-permute-start.11 = (bf16[4096,640]{1,0:T(8,128)(2,1)}, bf16[4096,640]{1,0:T(8,128)(2,1)}, u32[]{:S(2)}, u32[]{:S(2)}) collective-permute-start(bf16[4096,640]{1,0:T(8,128)(2,1)} %collective-permute-done.10.wt.refs_3_.refs_5_), channel_id=1, source_target_pairs={{0,32},{32,0},{1,33},{33,1},{2,34},{34,2},{3,35},{35,3},{4,36},{36... | collective-permute-start | bytes 15728648 | tf_op jit(solution)/shard_map/ppermute | solution.py:204
  110.6 7.0 %collective-permute-start.5 = (bf16[32,4096]{1,0:T(8,128)(2,1)S(1)}, bf16[32,4096]{1,0:T(8,128)(2,1)S(1)}, u32[]{:S(2)}, u32[]{:S(2)}) collective-permute-start(bf16[32,4096]{1,0:T(8,128)(2,1)S(1)} %slice.243), channel_id=1, source_target_pairs={{0,24},{8,0},{16,8},{24,16},{1,25},{9,1},{17,9},{25,17},{2,26},{10... | collective-permute-start | bytes 786440 | tf_op jit(solution)/shard_map/ppermute | solution.py:181
  118.3 51.7 %collective-permute-start.16 = (bf16[256,4096]{1,0:T(8,128)(2,1)}, bf16[256,4096]{1,0:T(8,128)(2,1)S(1)}, u32[]{:S(2)}, u32[]{:S(2)}) collective-permute-start(bf16[256,4096]{1,0:T(8,128)(2,1)} %constant_dynamic-update-slice_fusion.refs_0_), channel_id=1, source_target_pairs={{0,6},{2,0},{4,2},{6,4},{1,7},{3,1},{5,3},{7,5},{8,14},{10,8},{12,... | collective-permute-start | bytes 6291464 | tf_op jit(solution)/shard_map/ppermute | solution.py:174
  120.9 53.9 %collective-permute-start.15 = (bf16[256,4096]{1,0:T(8,128)(2,1)}, bf16[256,4096]{1,0:T(8,128)(2,1)}, u32[]{:S(2)}, u32[]{:S(2)}) collective-permute-start(bf16[256,4096]{1,0:T(8,128)(2,1)} %constant_dynamic-update-slice_fusion.refs_0_), channel_id=1, source_target_pairs={{0,2},{2,4},{4,6},{6,0},{1,3},{3,5},{5,7},{7,1},{8,10},{10,12},{12... | collective-permute-start | bytes 6291464 | tf_op jit(solution)/shard_map/ppermute | solution.py:173
  122.3 56.7 %collective-permute-start.21 = (bf16[256,4096]{1,0:T(8,128)(2,1)}, bf16[256,4096]{1,0:T(8,128)(2,1)}, u32[]{:S(2)}, u32[]{:S(2)}) collective-permute-start(bf16[256,4096]{1,0:T(8,128)(2,1)} %constant_dynamic-update-slice_fusion.5.refs_1_), channel_id=1, source_target_pairs={{0,24},{8,0},{16,8},{24,16},{1,25},{9,1},{17,9},{25,17},{2,26},{10... | collective-permute-start | bytes 6291464 | tf_op jit(solution)/shard_map/ppermute | solution.py:174
  124.8 55.6 %collective-permute-start.19 = (bf16[256,4096]{1,0:T(8,128)(2,1)}, bf16[256,4096]{1,0:T(8,128)(2,1)}, u32[]{:S(2)}, u32[]{:S(2)}) collective-permute-start(bf16[256,4096]{1,0:T(8,128)(2,1)} %constant_dynamic-update-slice_fusion.5.refs_1_), channel_id=1, source_target_pairs={{0,8},{8,16},{16,24},{24,0},{1,9},{9,17},{17,25},{25,1},{2,10},{10... | collective-permute-start | bytes 6291464 | tf_op jit(solution)/shard_map/ppermute | solution.py:173
  170.1 14.1 %collective-permute-start.13 = (bf16[128,4096]{1,0:T(8,128)(2,1)}, bf16[128,4096]{1,0:T(8,128)(2,1)S(1)}, u32[]{:S(2)}, u32[]{:S(2)}) collective-permute-start(bf16[128,4096]{1,0:T(8,128)(2,1)} %all-gather.2.cloned.1.call-done.qa.refs_5_.refs_7_), channel_id=1, source_target_pairs={{0,32},{32,0},{1,33},{33,1},{2,34},{34,2},{3,35},{35,3},{4,36},{36... | collective-permute-start | bytes 3145736 | tf_op jit(solution)/shard_map/ppermute | solution.py:206
  174.8 34.4 %collective-permute-start.18 = (bf16[128,4096]{1,0:T(8,128)(2,1)S(1)}, bf16[128,4096]{1,0:T(8,128)(2,1)S(1)}, u32[]{:S(2)}, u32[]{:S(2)}) collective-permute-start(bf16[128,4096]{1,0:T(8,128)(2,1)S(1)} %slice.253), channel_id=1, source_target_pairs={{0,6},{2,0},{4,2},{6,4},{1,7},{3,1},{5,3},{7,5},{8,14},{10,8},{12,... | collective-permute-start | bytes 3145736 | tf_op jit(solution)/shard_map/ppermute | solution.py:181
  179.0 30.2 %collective-permute-start.17 = (bf16[128,4096]{1,0:T(8,128)(2,1)S(1)}, bf16[128,4096]{1,0:T(8,128)(2,1)S(1)}, u32[]{:S(2)}, u32[]{:S(2)}) collective-permute-start(bf16[128,4096]{1,0:T(8,128)(2,1)S(1)} %slice.252), channel_id=1, source_target_pairs={{0,2},{2,4},{4,6},{6,0},{1,3},{3,5},{5,7},{7,1},{8,10},{10,12},{12... | collective-permute-start | bytes 3145736 | tf_op jit(solution)/shard_map/ppermute | solution.py:180
  180.5 28.7 %collective-permute-start.22 = (bf16[128,4096]{1,0:T(8,128)(2,1)S(1)}, bf16[128,4096]{1,0:T(8,128)(2,1)S(1)}, u32[]{:S(2)}, u32[]{:S(2)}) collective-permute-start(bf16[128,4096]{1,0:T(8,128)(2,1)S(1)} %slice.255), channel_id=1, source_target_pairs={{0,24},{8,0},{16,8},{24,16},{1,25},{9,1},{17,9},{25,17},{2,26},{10... | collective-permute-start | bytes 3145736 | tf_op jit(solution)/shard_map/ppermute | solution.py:181
  184.2 25.6 %collective-permute-start.20 = (bf16[128,4096]{1,0:T(8,128)(2,1)S(1)}, bf16[128,4096]{1,0:T(8,128)(2,1)S(1)}, u32[]{:S(2)}, u32[]{:S(2)}) collective-permute-start(bf16[128,4096]{1,0:T(8,128)(2,1)S(1)} %slice.254), channel_id=1, source_target_pairs={{0,8},{8,16},{16,24},{24,0},{1,9},{9,17},{17,25},{25,1},{2,10},{10... | collective-permute-start | bytes 3145736 | tf_op jit(solution)/shard_map/ppermute | solution.py:180
  254.7 3.6 %collective-permute-start.24 = (f32[1,44]{1,0:T(1,128)S(1)}, f32[1,44]{1,0:T(1,128)S(1)}, u32[]{:S(2)}, u32[]{:S(2)}) collective-permute-start(f32[1,44]{1,0:T(1,128)S(1)} %get-tuple-element.77), channel_id=1, source_target_pairs={{0,8},{8,16},{16,24},{24,0},{1,9},{9,17},{17,25},{25,1},{2,10},{10... | collective-permute-start | bytes 536 | tf_op jit(solution)/shard_map/ppermute | solution.py:256
  254.7 3.9 %collective-permute-start.25 = (f32[1,44]{1,0:T(1,128)S(1)}, f32[1,44]{1,0:T(1,128)S(1)}, u32[]{:S(2)}, u32[]{:S(2)}) collective-permute-start(f32[1,44]{1,0:T(1,128)S(1)} %get-tuple-element.78), channel_id=1, source_target_pairs={{0,16},{8,24},{16,0},{24,8},{1,17},{9,25},{17,1},{25,9},{2,18},{10... | collective-permute-start | bytes 536 | tf_op jit(solution)/shard_map/ppermute | solution.py:256
  259.3 3.9 %collective-permute-start.26 = (f32[1,14]{1,0:T(1,128)S(1)}, f32[1,14]{1,0:T(1,128)S(1)}, u32[]{:S(2)}, u32[]{:S(2)}) collective-permute-start(f32[1,14]{1,0:T(1,128)S(1)} %get-tuple-element.73), channel_id=1, source_target_pairs={{0,6},{2,0},{4,2},{6,4},{1,7},{3,1},{5,3},{7,5},{8,14},{10,8},{12,... | collective-permute-start | bytes 176 | tf_op jit(solution)/shard_map/ppermute | solution.py:256
  261.9 3.6 %collective-permute-start.27 = (f32[1,14]{1,0:T(1,128)S(1)}, f32[1,14]{1,0:T(1,128)S(1)}, u32[]{:S(2)}, u32[]{:S(2)}) collective-permute-start(f32[1,14]{1,0:T(1,128)S(1)} %get-tuple-element.74), channel_id=1, source_target_pairs={{0,2},{2,4},{4,6},{6,0},{1,3},{3,5},{5,7},{7,1},{8,10},{10,12},{12... | collective-permute-start | bytes 176 | tf_op jit(solution)/shard_map/ppermute | solution.py:256
  261.9 3.9 %collective-permute-start.28 = (f32[1,14]{1,0:T(1,128)S(1)}, f32[1,14]{1,0:T(1,128)S(1)}, u32[]{:S(2)}, u32[]{:S(2)}) collective-permute-start(f32[1,14]{1,0:T(1,128)S(1)} %get-tuple-element.75), channel_id=1, source_target_pairs={{0,4},{2,6},{4,0},{6,2},{1,5},{3,7},{5,1},{7,3},{8,12},{10,14},{12... | collective-permute-start | bytes 176 | tf_op jit(solution)/shard_map/ppermute | solution.py:256
  269.0 11.8 %collective-permute-start.32 = (f32[1,128]{1,0:T(1,128)S(1)}, f32[1,128]{1,0:T(1,128)S(1)}, u32[]{:S(2)}, u32[]{:S(2)}) collective-permute-start(f32[1,128]{1,0:T(1,128)S(1)} %pad_bitcast_fusion), channel_id=1, source_target_pairs={{65,0},{64,32},{97,1},{96,33},{1,64},{0,96},{33,65},{32,97},{67,2}... | collective-permute-start | bytes 1544 | tf_op jit(solution)/shard_map/ppermute | solution.py:276
  273.5 7.3 %collective-permute-start.31 = (f32[1,128]{1,0:T(1,128)S(1)}, f32[1,128]{1,0:T(1,128)S(1)}, u32[]{:S(2)}, u32[]{:S(2)}) collective-permute-start(f32[1,128]{1,0:T(1,128)S(1)} %pad_bitcast_fusion), channel_id=1, source_target_pairs={{64,0},{65,32},{96,1},{97,33},{0,64},{1,96},{32,65},{33,97},{66,2}... | collective-permute-start | bytes 1544 | tf_op jit(solution)/shard_map/ppermute | solution.py:276
  278.3 4.8 %collective-permute-start.29 = (f32[1,128]{1,0:T(1,128)S(1)}, f32[1,128]{1,0:T(1,128)S(1)}, u32[]{:S(2)}, u32[]{:S(2)}) collective-permute-start(f32[1,128]{1,0:T(1,128)S(1)} %pad_bitcast_fusion), channel_id=1, source_target_pairs={{0,0},{1,32},{32,1},{33,33},{64,64},{65,96},{96,65},{97,97},{2,2},... | collective-permute-start | bytes 1544 | tf_op jit(solution)/shard_map/ppermute | solution.py:276
  (11 other events, 270.4 us)
Sparse Core Ops, SparseCore 0:
  93.2 46.7 all-gather.1

commit v2 on v0

v2 whole, which is shorter than its diff:
```python
import functools

import jax
import jax.numpy as jnp
from jax import lax
from jax.experimental import pallas as pl
from jax.experimental.pallas import tpu as pltpu
from jax.sharding import Mesh
from jax.sharding import PartitionSpec as P

LEN = 64
D = 4096
FD = 640
TILES = 5
NQ = 256
OFFS = (0, -1, 1, 2)
F32 = jnp.float32
BF16 = jnp.bfloat16
NT = (((1,), (1,)), ((), ()))
HIGHEST = lax.Precision.HIGHEST
CP = 48
HEAD = LEN - CP
REWARD, SECOND, QUERY, RATE = 4, 8, 16, 20


def ring(step):
    return [(i, (i + step) % 4) for i in range(4)]


def activations(h):
    sig = 0.5 * jnp.tanh(0.5 * h) + 0.5
    act = h * sig
    return act, sig + act * (1.0 - sig)


def fold(v):
    return v[:, :128] + v[:, 128:]


def norm_kernel(acts, query, gain, one, two, rest, qown):
    def norm(v):
        v = v.astype(F32)
        scale = lax.rsqrt(jnp.mean(v * v, axis=-1, keepdims=True) + 1e-05)
        return (v * scale * gain[...].astype(F32)).astype(BF16)

    one[...] = norm(acts[HEAD:LEN, :])
    two[...] = norm(acts[LEN + HEAD:, :])
    rest[0:HEAD, :] = norm(acts[:HEAD, :])
    rest[HEAD:2 * HEAD, :] = norm(acts[LEN:LEN + HEAD, :])
    qown[...] = norm(query[...])


def norm_call(acts, query, gain):
    return pl.pallas_call(
        norm_kernel,
        out_shape=tuple(jax.ShapeDtypeStruct((n, D), BF16) for n in (CP, CP, 2 * HEAD, 8)),
        in_specs=[VM] * 3,
        out_specs=(VM,) * 4,
        cost_estimate=pl.CostEstimate(flops=4 * 136 * D, bytes_accessed=4 * 2**20, transcendentals=136),
        name="norm_rows",
    )(acts, query, gain)


def copy_kernel(moves, n, m, *refs):
    src, dst, sem = refs[:n], refs[n:n + m], refs[n + m]
    copies = [
        pltpu.make_async_copy(src[i].at[pl.ds(s, k)], dst[o].at[pl.ds(d, k)], sem.at[c])
        for c, (i, s, o, d, k) in enumerate(moves)
    ]
    for c in copies:
        c.start()
    for c in copies:
        c.wait()


def copy_call(parts, rows, moves, name):
    return pl.pallas_call(
        functools.partial(copy_kernel, moves, len(parts), len(rows)),
        out_shape=tuple(jax.ShapeDtypeStruct((n, D), BF16) for n in rows),
        in_specs=[ANY] * len(parts),
        out_specs=(VM,) * len(rows),
        scratch_shapes=[pltpu.SemaphoreType.DMA((len(moves),))],
        cost_estimate=pl.CostEstimate(flops=0, bytes_accessed=sum(rows) * D * 4, transcendentals=0),
        name=name,
    )(*parts)


def rows_kernel(shapes, block, with_queries, *refs):
    n = len(shapes)
    xin = refs[:n]
    info, train_len, query_len, queries, own, first, second = refs[n:n + 7]
    if with_queries:
        small, small_first, small_second, out, qg, heads = refs[n + 7:n + 13]
    else:
        before, qg, heads, out = refs[n + 7:n + 11]
    xs, qs, ws, dv, acc, gram, sums_r, sums_z, xsem, qsem, wsem = refs[-11:]
    straight = info[0] == 1
    x, y, core = info[1], info[2], info[3]

    starts, at = [], 0
    for rows, _ in shapes:
        starts.append(at)
        at += rows
    total = at
    xloads = [
        pltpu.make_async_copy(xin[i], xs.at[pl.ds(starts[i], shapes[i][0])], xsem.at[i]) for i in range(n)
    ]

    u = lax.broadcasted_iota(jnp.int32, (NQ, 128), 0)
    lane = lax.broadcasted_iota(jnp.int32, (NQ, 128), 1)
    qx, qy = (u >> 5) & 3, (u >> 3) & 3
    position = 8 * (2 * qy + jnp.where(u < 128, 1, 0)) + (u & 7)
    length = jnp.zeros((NQ, 128), jnp.int32)
    for k in range(4):
        length = jnp.where(qx == k, query_len[k // 2, k % 2], length)
    weight = jnp.where(position < length, 1.0 / jnp.maximum(length, 1).astype(F32), 0.0)

    def pick(at):
        return jnp.where(qx == lane - at, weight, 0.0)

    qload = pltpu.make_async_copy(queries, qs, qsem)

    def tiles(a, b):
        moves = []
        for j in range(TILES):
            cols = pl.ds(128 * j, 128)
            for h, side in enumerate((a, b)):
                dst = ws.at[j, :, pl.ds(128 * h, 128)]
                moves.append(pltpu.make_async_copy(side.at[:, cols], dst, wsem.at[j, h]))
        return moves

    def start_tiles():
        @pl.when(straight)
        def _():
            for c in tiles(own, first):
                c.start()

        @pl.when(jnp.logical_not(straight))
        def _():
            for c in tiles(first, second):
                c.start()

    def wait_tiles():
        for c in tiles(first, second):
            c.wait()

    qload.start()
    if with_queries:
        start_tiles()
        for j in range(TILES):
            cols = slice(128 * j, 128 * (j + 1))
            heads[:, 256 * j:256 * j + 128] = jnp.where(straight, small[:, cols], small_first[:, cols])
            heads[:, 256 * j + 128:256 * j + 256] = jnp.where(straight, small_first[:, cols], small_second[:, cols])
        qload.wait()
        wait_tiles()
        for c in xloads:
            c.start()
        query_total = None
        for j in range(TILES):
            row = heads[:, 256 * j:256 * (j + 1)]
            act, deriv = activations(jnp.dot(qs[...], ws[j], preferred_element_type=F32))
            part = fold(act * row)
            query_total = part if j == 0 else query_total + part
            qg[:, 256 * j:256 * (j + 1)] = (row * row * deriv).astype(BF16)
        common = jnp.sum(jnp.sum(query_total, axis=1, keepdims=True) * pick(QUERY), axis=0, keepdims=True)
        common += jnp.where(straight, small[:, FD:], small_first[:, FD:])
        out[...] = jnp.broadcast_to(common, (16, 128))
        for c in xloads:
            c.wait()
    else:
        for c in xloads:
            c.start()
        out[...] = before[...]
        qload.wait()
        for c in xloads:
            c.wait()
        start_tiles()

    @pl.loop(0, total // block)
    def _(b):
        at = pl.ds(pl.multiple_of(b * block, block), block)
        gram[at, :] = lax.dot_general(xs[at, :], qs[...], NT, preferred_element_type=F32)

    if not with_queries:
        wait_tiles()

    @pl.loop(0, total // block)
    def _(b):
        at = pl.ds(pl.multiple_of(b * block, block), block)
        for j in range(TILES):
            cols = slice(256 * j, 256 * (j + 1))
            act, deriv = activations(jnp.dot(xs[at, :], ws[j], preferred_element_type=F32))
            part = fold(act * heads[:, cols])
            if j == 0:
                acc[at, :] = part
            else:
                acc[at, :] += part
            dv[:, cols] = deriv.astype(BF16)
        gram[at, :] = gram[at, :] * lax.dot_general(dv[...], qg[...], NT, preferred_element_type=F32)

    runs = []
    for i, (_, found) in enumerate(shapes):
        for row, count, side, relative, gx, gy, slot in found:
            place = lax.rem(x + gx + 4, 4) * 4 + lax.rem(y + gy + 4, 4) if relative else 4 * gx + gy
            runs.append((starts[i] + row, count, side, place, slot))
    for k, (row, count, side, place, slot) in enumerate(runs):
        length = train_len[place * 2 + 1 - core, side]
        live = lax.broadcasted_iota(jnp.int32, (count, 1), 0) + slot < length
        live = jnp.where(live, 1.0 / jnp.maximum(length, 1).astype(F32), 0.0)
        sums_r[k:k + 1, :] = jnp.sum(acc[row:row + count, :] * live, axis=0, keepdims=True)
        sums_z[k:k + 1, :] = jnp.sum(gram[row:row + count, :] * live, axis=0, keepdims=True)
    reward = jnp.sum(sums_r[...], axis=1, keepdims=True)
    lanes = lax.broadcasted_iota(jnp.int32, (len(runs), 128), 1)
    tables = []
    for at in (0, SECOND):
        scores = jnp.dot(sums_z[...], pick(at), precision=HIGHEST, preferred_element_type=F32)
        tables.append(scores + jnp.where(lanes == at + REWARD, reward, 0.0))
    for k, (_, _, side, place, _) in enumerate(runs):
        at = pl.ds(place, 1)
        out[at, :] = out[at, :] + tables[side][k:k + 1, :]


ANY = pl.BlockSpec(memory_space=pl.ANY)
HBM = pl.BlockSpec(memory_space=pltpu.HBM)
VM = pl.BlockSpec(memory_space=pltpu.VMEM)
SM = pl.BlockSpec(memory_space=pltpu.SMEM)


def rows_call(rows, block, name, given, with_queries):
    xin = [r[0] for r in rows]
    shapes = tuple((v.shape[0], found) for v, found in rows)
    n, total = len(rows), sum(v.shape[0] for v in xin)
    runs = sum(len(found) for _, found in rows)
    out_shape = [jax.ShapeDtypeStruct((16, 128), F32)]
    if with_queries:
        out_shape += [jax.ShapeDtypeStruct((NQ, 2 * FD), BF16), jax.ShapeDtypeStruct((1, 2 * FD), F32)]
    return pl.pallas_call(
        functools.partial(rows_kernel, shapes, block, with_queries),
        out_shape=tuple(out_shape),
        in_specs=[HBM] * n + [SM] * 3 + [HBM] * 4 + [VM] * 3,
        out_specs=(VM,) * len(out_shape),
        scratch_shapes=[
            pltpu.VMEM((total, D), BF16),
            pltpu.VMEM((NQ, D), BF16),
            pltpu.VMEM((TILES, D, 256), BF16),
            pltpu.VMEM((block, 2 * FD), BF16),
            pltpu.VMEM((total, 128), F32),
            pltpu.VMEM((total, 256), F32),
            pltpu.VMEM((runs, 128), F32),
            pltpu.VMEM((runs, 256), F32),
            pltpu.SemaphoreType.DMA((n,)),
            pltpu.SemaphoreType.DMA,
            pltpu.SemaphoreType.DMA((TILES, 2)),
        ],
        compiler_params=pltpu.CompilerParams(vmem_limit_bytes=56 * 2**20),
        cost_estimate=pl.CostEstimate(flops=1, bytes_accessed=1, transcendentals=0),
        name=name,
    )(*xin, *given)


def final_kernel(plane, got, out):
    rows = lax.broadcasted_iota(jnp.int32, (32, 128), 0)
    parts = []
    for zh in (0, 1):
        at = pl.ds(pl.multiple_of(64 * zh + 32 * (1 - plane[0]), 32), 32)
        v = got[at, :]
        for p in (0, 1):
            parts.append(jnp.sum(jnp.where((rows & 1) == p, v, 0.0), axis=0, keepdims=True))
    total = jnp.concatenate(parts, axis=0)
    lanes = lax.broadcasted_iota(jnp.int32, (4, 128), 1)
    at = lambda k: jnp.sum(jnp.where(lanes == k, total, 0.0), axis=1, keepdims=True)
    sigmoid = lambda v: 0.5 * jnp.tanh(0.5 * v) + 0.5
    factor = at(RATE) * (1.0 / 16.0) * sigmoid(at(SECOND + REWARD) - at(REWARD))
    for i in (0, 1):
        scores = [at(SECOND + 2 * i + k) - at(2 * i + k) for k in (0, 1)]
        value = factor * sigmoid(at(QUERY + 2 * i + 1) - at(QUERY + 2 * i)) * (scores[1] - scores[0])
        out[:, i:i + 1] = jnp.sum(value, axis=0, keepdims=True)


def final_call(plane, got):
    return pl.pallas_call(
        final_kernel,
        out_shape=jax.ShapeDtypeStruct((1, 2), F32),
        in_specs=[SM, VM],
        out_specs=VM,
        name="influence",
    )(plane, got)


def local(train_acts, train_len, query_acts, query_len, norm_gain, up_weight, readout, lr_weight):
    core, plane = lax.axis_index("c"), lax.axis_index("zl")
    x, y = lax.axis_index("x"), lax.axis_index("y")
    straight = core == plane
    turn = functools.partial(lax.ppermute, axis_name=("c", "zl"), perm=[(0, 2), (2, 3), (3, 1), (1, 0)])
    swap = functools.partial(lax.ppermute, axis_name="c", perm=[(0, 1), (1, 0)])
    low = lambda v, axis: lax.ppermute(v, axis, ring(1))
    high = lambda v, axis: lax.ppermute(v, axis, ring(-1))

    one, two, rest, qown = norm_call(train_acts[0], query_acts[0], norm_gain)
    small = jnp.concatenate(
        [readout[0].astype(F32), jnp.zeros((RATE,), F32), lr_weight, jnp.zeros((127 - RATE,), F32)]
    ).reshape(1, FD + 128)
    qown, small_first, one, two, rest = turn(qown), turn(small), turn(one), turn(two), turn(rest)
    weight_own, qown, small_first, one, two, rest = lax.optimization_barrier(
        (up_weight[0], qown, small_first, one, two, rest)
    )
    weight_first = turn(weight_own)
    small_second = swap(small_first)
    queries = lax.all_gather(qown, ("c", "x", "y"), axis=0, tiled=True)
    some = lax.all_gather(rest, ("x", "y"), axis=0, tiled=True)

    one_low, one_high = low(one, "x"), high(one, "x")
    two_low, two_high = low(two, "y"), high(two, "y")
    one_a, one_b = low(one_low[:32], "x"), high(one_high[32:], "x")
    two_a, two_b = low(two_low[:32], "y"), high(two_high[32:], "y")
    moves = []
    for g in (0, 1):
        moves += [(5 * g, 0, 2 * g, 0, CP), (5 * g + 1, 0, 2 * g, CP, CP), (5 * g + 2, 0, 2 * g + 1, 0, CP),
                  (5 * g + 3, 0, 2 * g + 1, CP, 32), (5 * g + 4, 0, 2 * g + 1, CP + 32, 16)]
    a1, b1, a2, b2 = copy_call(
        (one, one_low, one_high, one_a, one_b, two, two_low, two_high, two_a, two_b), (2 * CP,) * 4, moves, "join_rows"
    )
    a1_low, b1_high = low(a1, "y"), high(b1, "y")
    a2_low, b2_high = low(a2, "x"), high(b2, "x")
    weight_first, a1_low, b1_high, a2_low, b2_high = lax.optimization_barrier(
        (weight_first, a1_low, b1_high, a2_low, b2_high)
    )
    weight_second = swap(weight_first)
    b1_low, a1_high = low(b1, "y"), high(a1, "y")
    b2_low, a2_high = low(b2, "x"), high(a2, "x")
    a1_far, b1_far = low(a1_low, "y"), high(b1_high, "y")
    a2_far, b2_far = low(a2_low, "x"), high(b2_high, "x")

    def group(side, g, ks):
        found = []
        for i, k in enumerate(ks):
            gx, gy = (OFFS[k], OFFS[g]) if side == 0 else (OFFS[g], OFFS[k])
            found.append((CP * i, CP, side, True, gx, gy, HEAD))
        return tuple(found)

    gathered_runs = tuple(
        (HEAD * (2 * p + side), HEAD, side, False, p // 4, p % 4, 0) for p in range(16) for side in (0, 1)
    )
    near, rest = (0, 1), (2, 3)
    info = jnp.stack([straight.astype(jnp.int32), x, y, core])
    given = (info, train_len, query_len, queries, weight_own, weight_first, weight_second)
    sums, *kept = rows_call(
        [(a1, group(0, 0, near)), (b1, group(0, 0, rest)), (a2, group(1, 0, near)), (b2, group(1, 0, rest))],
        192, "first_rows", (*given, small, small_first, small_second), True,
    )
    (sums,) = rows_call(
        [(a1_low, group(0, 1, near)), (b1_high, group(0, 2, rest)), (a2_low, group(1, 1, near)), (b2_high, group(1, 2, rest)),
         (b1_low, group(0, 1, rest)), (a1_high, group(0, 2, near)), (b2_low, group(1, 1, rest)), (a2_high, group(1, 2, near)),
         (some, gathered_runs)],
        256, "next_rows", (*given, sums, *kept), False,
    )
    (sums,) = rows_call(
        [(a1_far, group(0, 3, near)), (b1_far, group(0, 3, rest)), (a2_far, group(1, 3, near)), (b2_far, group(1, 3, rest))],
        192, "last_rows", (*given, sums, *kept), False,
    )
    message = jnp.broadcast_to(sums.reshape(1, 16, 1, 128), (4, 16, 2, 128)).reshape(128, 128)
    got = lax.all_to_all(message, ("zh", "c", "x", "y", "zl"), split_axis=0, concat_axis=0, tiled=True)
    return final_call(plane.reshape(1), got)


def solution(mesh):
    full = Mesh(mesh.devices.reshape(2, 2, 4, 4, 2), ("zh", "c", "x", "y", "zl"))
    ckpt, fsdp = ("zh", "c"), ("x", "y", "zl")
    return jax.shard_map(
        local,
        mesh=full,
        in_specs=(
            P(ckpt, fsdp, None),
            P(),
            P(ckpt, fsdp, None),
            P(),
            P(ckpt, None),
            P(ckpt, None, fsdp),
            P(ckpt, fsdp),
            P(ckpt),
        ),
        out_specs=P(fsdp, None),
        check_vma=False,
    )
```

time: 1190 us -> 218 us (0.18)
  waiting for transfers between devices: 1010 us -> 72 us
  blocking collectives: 99.1 us -> 18.9 us
  Pallas kernels: 0 us -> 66.7 us
  matrix products: 54.7 us -> 0 us
  starting transfers between devices: 0.09 us -> 38.8 us
    all_gather x2, waiting for transfers between devices: 853 us -> 9.93 us  [the longest x1 9.92 us: local(): some = lax.all_gather(rest, ('x', 'y'), axis=0, tiled=True)]
    reduce_scatter x1 -> x0, waiting for transfers between devices: 156 us -> none  [local(): lax.psum_scatter(jnp.dot(grad_out, query_grad.T, preferred_element_type=j...]
    psum x2 -> x0, blocking collectives: 99.1 us -> none  [the longest x1 68 us: local(): train_reward, query_reward = lax.psum((train_part, query_part), 'fsdp')]
    pallas_call x0 -> x6, Pallas kernels: none -> 66.7 us  [the longest x3 58.9 us: rows_call(): pl.pallas_call(functools.partial(rows_kernel, shapes, block, with_queries...]
    ppermute x0 -> x28, waiting for transfers between devices: none -> 62.1 us  [the longest x10 39.6 us: local(): low = lambda v, axis: lax.ppermute(v, axis, ring(1))]
    dot_general x6 -> x0, matrix products: 54.7 us -> none  [the longest x1 31.5 us: local(): jnp.dot(lax.all_gather(normed_own, 'fsdp', axis=0, tiled=True), weight, p...]
    ppermute x0 -> x28, starting transfers between devices: none -> 38.8 us  [the longest x10 19.3 us: local(): high = lambda v, axis: lax.ppermute(v, axis, ring(-1))]
    all_to_all x0 -> x1, blocking collectives: none -> 18.9 us  [local(): lax.all_to_all(message, ('zh', 'c', 'x', 'y', 'zl'), split_axis=0, concat...]
  transfers between devices with their start and end apart: 3 -> 30, of which waited for: 3 -> 12; matrix products, arithmetic and copies ran while one was open for 1% -> 1% of each run, Pallas kernels for 0% -> 22%
where the time goes in v2:
time: 218 us
  waiting for transfers between devices  72 us (33%)
  Pallas kernels  66.7 us (31%)
  starting transfers between devices  38.8 us (18%)
  blocking collectives  18.9 us (9%)
  between operations  14.4 us (7%)
  local copies, waits for them, and re-layouts  5.75 us (3%)
    pallas_call x3, Pallas kernels, rows_call(): pl.pallas_call(functools.partial(rows_kernel, shapes, block, with_queries...  58.9 us
    ppermute x10, waiting for transfers between devices, local(): low = lambda v, axis: lax.ppermute(v, axis, ring(1))  39.6 us
    ppermute x10, starting transfers between devices, local(): high = lambda v, axis: lax.ppermute(v, axis, ring(-1))  19.3 us
    all_to_all x1, blocking collectives, local(): lax.all_to_all(message, ('zh', 'c', 'x', 'y', 'zl'), split_axis=0, concat...  18.9 us
    all_gather x1, waiting for transfers between devices, local(): some = lax.all_gather(rest, ('x', 'y'), axis=0, tiled=True)  9.92 us
    ppermute x1, waiting for transfers between devices, local(): turn(small)  8.99 us
    ppermute x10, starting transfers between devices, local(): low = lambda v, axis: lax.ppermute(v, axis, ring(1))  8.83 us
    ppermute x1, waiting for transfers between devices, local(): weight_first = turn(weight_own)  6.74 us
  transfers between devices with their start and end apart: 30, of which 12 were waited for; matrix products, arithmetic and copies ran while one was open for 1% of the time, Pallas kernels for 22%

profile of v2, /device:TPU:1, one launch (start us, length us, event | category | flops | bytes accessed | tf_op | source)
XLA Modules:
  0.0 218.0 jit_solution(13284526820424595160)
XLA Ops:
  6.5 2.7 %norm_rows.1 = (bf16[48,4096]{1,0:T(8,128)(2,1)}, bf16[48,4096]{1,0:T(8,128)(2,1)}, bf16[32,4096]{1,0:T(8,128)(2,1)}, bf16[8,4096]{1,0:T(8,128)(2,1)}) custom-call(bf16[128,4096]{1,0:T(8,128)(2,1)} %bitcast.14, bf16[8,4096]{1,0:T(8,128)(2,1)} %bitcast.17, bf16[1,4096]{1,0:T(2,128)(2,1)} %gain.1), custom_call_target="tpu_custom_call" | custom-call | flops 2228224 | bytes 4194304 | tf_op jit(solution)/shard_map/norm_rows/pallas_call | solution.py:54
  9.2 2.5 %collective-permute-start.2 = (bf16[48,4096]{1,0:T(8,128)(2,1)}, bf16[48,4096]{1,0:T(8,128)(2,1)S(1)}, u32[]{:S(2)}, u32[]{:S(2)}) collective-permute-start(bf16[48,4096]{1,0:T(8,128)(2,1)} %get-tuple-element.28), channel_id=1, source_target_pairs={{0,32},{32,33},{33,1},{1,0},{2,34},{34,35},{35,3},{3,2},{4,36},{36... | collective-permute-start | bytes 1179656 | tf_op jit(solution)/shard_map/ppermute | solution.py:303
  13.9 1.5 collective-permute-start.1
  15.5 9.0 %collective-permute-done.1.refs_12_ = f32[1,768]{1,0:T(1,128)S(1)} collective-permute-done((f32[1,768]{1,0:T(1,128)S(1)}, f32[1,768]{1,0:T(1,128)S(1)}, u32[]{:S(2)}, u32[]{:S(2)}) %collective-permute-start.1) | collective-permute-done | bytes 3104 | tf_op jit(solution)/shard_map/ppermute | solution.py:303
  25.2 1.9 collective-permute-start.5
  27.1 1.4 collective-permute-start.10
  29.7 1.5 collective-permute-start.11
  31.2 1.5 collective-permute-start.7
  32.7 5.8 %collective-permute-done.10.refs_6_ = bf16[48,4096]{1,0:T(8,128)(2,1)S(1)} collective-permute-done((bf16[48,4096]{1,0:T(8,128)(2,1)S(1)}, bf16[48,4096]{1,0:T(8,128)(2,1)S(1)}, u32[]{:S(2)}, u32[]{:S(2)}) %collective-permute-start.10) | collective-permute-done | bytes 393248 | tf_op jit(solution)/shard_map/ppermute | solution.py:296
  39.8 2.7 %collective-permute-start.13 = (bf16[16,4096]{1,0:T(8,128)(2,1)S(1)}, bf16[16,4096]{1,0:T(8,128)(2,1)S(1)}, u32[]{:S(2)}, u32[]{:S(2)}) collective-permute-start(bf16[16,4096]{1,0:T(8,128)(2,1)S(1)} %slice.19), channel_id=1, source_target_pairs={{0,6},{2,0},{4,2},{6,4},{1,7},{3,1},{5,3},{7,5},{8,14},{10,8},{12,... | collective-permute-start | bytes 393224 | tf_op jit(solution)/shard_map/ppermute | solution.py:297
  42.5 1.6 collective-permute-start.9
  44.6 2.5 %collective-permute-done.9.refs_4_ = bf16[16,4096]{1,0:T(8,128)(2,1)S(1)} collective-permute-done((bf16[16,4096]{1,0:T(8,128)(2,1)S(1)}, bf16[16,4096]{1,0:T(8,128)(2,1)S(1)}, u32[]{:S(2)}, u32[]{:S(2)}) %collective-permute-start.9) | collective-permute-done | bytes 131104 | tf_op jit(solution)/shard_map/ppermute | solution.py:297
  48.6 3.6 %join_rows.1 = (bf16[96,4096]{1,0:T(8,128)(2,1)}, bf16[96,4096]{1,0:T(8,128)(2,1)}, bf16[96,4096]{1,0:T(8,128)(2,1)}, bf16[96,4096]{1,0:T(8,128)(2,1)}) custom-call(bf16[48,4096]{1,0:T(8,128)(2,1)} %copy-done.11, bf16[48,4096]{1,0:T(8,128)(2,1)} %copy-done.1, bf16[48,4096]{1,0:T(8,128)(2,1)} %copy-done.10, bf16[32,4096]{1,0:T(8,128)(2,1)} %copy-done.14, ...), custom_call_target="tpu_custom_call" | custom-call | bytes 6291456 | tf_op jit(solution)/shard_map/join_rows/pallas_call | solution.py:77
  52.9 2.1 collective-permute-start.15
  56.2 1.5 collective-permute-start.17
  57.7 16.3 %collective-permute-done.14.refs_0_ = bf16[96,4096]{1,0:T(8,128)(2,1)} collective-permute-done((bf16[96,4096]{1,0:T(8,128)(2,1)}, bf16[96,4096]{1,0:T(8,128)(2,1)}, u32[]{:S(2)}, u32[]{:S(2)}) %collective-permute-start.14) | collective-permute-done | bytes 786464 | tf_op jit(solution)/shard_map/ppermute | solution.py:296
  74.0 3.1 %collective-permute-done.16.refs_2_ = bf16[96,4096]{1,0:T(8,128)(2,1)} collective-permute-done((bf16[96,4096]{1,0:T(8,128)(2,1)}, bf16[96,4096]{1,0:T(8,128)(2,1)}, u32[]{:S(2)}, u32[]{:S(2)}) %collective-permute-start.16) | collective-permute-done | bytes 786464 | tf_op jit(solution)/shard_map/ppermute | solution.py:296
  77.3 6.7 %collective-permute-done.5.refs_9_.refs_14_ = bf16[4096,640]{1,0:T(8,128)(2,1)} collective-permute-done((bf16[4096,640]{1,0:T(8,128)(2,1)}, bf16[4096,640]{1,0:T(8,128)(2,1)}, u32[]{:S(2)}, u32[]{:S(2)}) %collective-permute-start.5) | collective-permute-done | bytes 5242912 | tf_op jit(solution)/shard_map/ppermute | solution.py:307
  84.1 3.2 %collective-permute-start.22 = (bf16[4096,640]{1,0:T(8,128)(2,1)}, bf16[4096,640]{1,0:T(8,128)(2,1)}, u32[]{:S(2)}, u32[]{:S(2)}) collective-permute-start(bf16[4096,640]{1,0:T(8,128)(2,1)} %collective-permute-done.5.refs_9_.refs_14_), channel_id=1, source_target_pairs={{0,32},{32,0},{1,33},{33,1},{2,34},{34,2},{3,35},{35,3},{4,36},{36... | collective-permute-start | bytes 15728648 | tf_op jit(solution)/shard_map/ppermute | solution.py:328
  87.2 1.4 collective-permute-start.23
  88.6 1.4 collective-permute-start.24
  92.0 3.5 %collective-permute-done.27.refs_13_ = f32[1,768]{1,0:T(1,128)S(1)} collective-permute-done((f32[1,768]{1,0:T(1,128)S(1)}, f32[1,768]{1,0:T(1,128)S(1)}, u32[]{:S(2)}, u32[]{:S(2)}) %collective-permute-start.27) | collective-permute-done | bytes 3104 | tf_op jit(solution)/shard_map/ppermute | solution.py:308
  95.5 2.6 %collective-permute-start.26 = (bf16[96,4096]{1,0:T(8,128)(2,1)}, bf16[96,4096]{1,0:T(8,128)(2,1)}, u32[]{:S(2)}, u32[]{:S(2)}) collective-permute-start(bf16[96,4096]{1,0:T(8,128)(2,1)} %get-tuple-element.36.refs_2_), channel_id=1, source_target_pairs={{0,24},{8,0},{16,8},{24,16},{1,25},{9,1},{17,9},{25,17},{2,26},{10... | collective-permute-start | bytes 2359304 | tf_op jit(solution)/shard_map/ppermute | solution.py:297
  98.1 13.8 %collective-permute-done.23.refs_4_ = bf16[96,4096]{1,0:T(8,128)(2,1)S(1)} collective-permute-done((bf16[96,4096]{1,0:T(8,128)(2,1)}, bf16[96,4096]{1,0:T(8,128)(2,1)S(1)}, u32[]{:S(2)}, u32[]{:S(2)}) %collective-permute-start.23) | collective-permute-done | bytes 786464 | tf_op jit(solution)/shard_map/ppermute | solution.py:296
  111.9 2.7 %collective-permute-start.19 = (bf16[96,4096]{1,0:T(8,128)(2,1)}, bf16[96,4096]{1,0:T(8,128)(2,1)S(1)}, u32[]{:S(2)}, u32[]{:S(2)}) collective-permute-start(bf16[96,4096]{1,0:T(8,128)(2,1)} %collective-permute-done.15.refs_1_), channel_id=1, source_target_pairs={{0,6},{2,0},{4,2},{6,4},{1,7},{3,1},{5,3},{7,5},{8,14},{10,8},{12,... | collective-permute-start | bytes 2359304 | tf_op jit(solution)/shard_map/ppermute | solution.py:297
  115.7 1.8 collective-permute-start.21
  118.8 17.4 %first_rows.1 = (f32[16,128]{1,0:T(8,128)}, bf16[256,1280]{1,0:T(8,128)(2,1)}, f32[1,1280]{1,0:T(1,128)}) custom-call(bf16[96,4096]{1,0:T(8,128)(2,1)} %get-tuple-element.34.refs_0_, bf16[96,4096]{1,0:T(8,128)(2,1)} %get-tuple-element.35.refs_1_, bf16[96,4096]{1,0:T(8,128)(2,1)} %get-tuple-element.36.refs_2_, bf16[96,4096]{1,0:T(8,128)(2,1)} %get-tuple-element.37.refs_3_, ...), custom_call_target="tpu_custom_call" | custom-call | flops 1 | bytes 1 | tf_op jit(solution)/shard_map/first_rows/pallas_call | solution.py:237
  136.2 9.9 %all-gather.5.cloned.1.call-done.refs_8_ = bf16[512,4096]{1,0:T(8,128)(2,1)} async-done(((bf16[32,4096]{1,0:T(8,128)(2,1)}), bf16[512,4096]{1,0:T(8,128)(2,1)}) %all-gather.5.cloned.1.call-update) | async-done | bytes 4194320 | tf_op jit(solution)/shard_map/all_gather | solution.py:310
  146.1 27.7 %next_rows.1.refs_11_ = f32[16,128]{1,0:T(8,128)} custom-call(bf16[96,4096]{1,0:T(8,128)(2,1)} %collective-permute-done.14.refs_0_, bf16[96,4096]{1,0:T(8,128)(2,1)} %collective-permute-done.15.refs_1_, bf16[96,4096]{1,0:T(8,128)(2,1)} %collective-permute-done.16.refs_2_, bf16[96,4096]{1,0:T(8,128)(2,1)} %collective-permute-done.17.refs_3_, ...), custom_call_target="tpu_custom_call" | custom-call | flops 1 | bytes 1 | tf_op jit(solution)/shard_map/next_rows/pallas_call | solution.py:237
  176.2 13.9 %last_rows.1 = f32[16,128]{1,0:T(8,128)} custom-call(bf16[96,4096]{1,0:T(8,128)(2,1)} %copy-done.2, bf16[96,4096]{1,0:T(8,128)(2,1)} %copy-done.3, bf16[96,4096]{1,0:T(8,128)(2,1)} %copy-done.4, bf16[96,4096]{1,0:T(8,128)(2,1)} %copy-done.5, s32[4]{0:T(128)} %pad_add_fusion.refs_4_.refs_9_, s32[32,2]{1,0:T(8,128)} %copy.14.refs_5_.refs_10_, s32[2,2]{1,0:T(2,128)} %refs_6_.3, ...), custom_call_target="tpu_custom_call" | custom-call | flops 1 | bytes 1 | tf_op jit(solution)/shard_map/last_rows/pallas_call | solution.py:237
  190.8 18.9 %all_to_all.11 = f32[128,1,128]{2,1,0:T(1,128)} all-to-all(f32[128,1,128]{2,1,0:T(1,128)S(1)} %bitcast.16), channel_id=1, replica_groups=mesh['zh'=2,'c'=2,'x'=4,'y'=4,'zl'=2] {'zh','c','x','y','zl'}, dimensions={0} | all-to-all | bytes 131072 | tf_op jit(solution)/shard_map/all_to_all | solution.py:362
  209.7 1.5 influence.1
  (95 shorter events, 16.3 us)
Async XLA Ops:
  6.5 110.9 %copy-start.22 = (s32[32,2]{0,1:T(2,128)S(1)}, s32[32,2]{0,1:T(2,128)}, u32[]{:S(2)}) copy-start(s32[32,2]{0,1:T(2,128)} %param.9) | copy-start | bytes 772
  6.5 112.3 %all-gather.3.cloned.1.call-start = ((), (), s32[]{:S(2)}) async-start(), calls=%async_computation.1 | async-start | bytes 2162688 | tf_op jit(solution)/shard_map/all_gather | solution.py:309
  9.2 15.3 %collective-permute-start.2 = (bf16[48,4096]{1,0:T(8,128)(2,1)}, bf16[48,4096]{1,0:T(8,128)(2,1)S(1)}, u32[]{:S(2)}, u32[]{:S(2)}) collective-permute-start(bf16[48,4096]{1,0:T(8,128)(2,1)} %get-tuple-element.28), channel_id=1, source_target_pairs={{0,32},{32,33},{33,1},{1,0},{2,34},{34,35},{35,3},{3,2},{4,36},{36... | collective-permute-start | bytes 1179656 | tf_op jit(solution)/shard_map/ppermute | solution.py:303
  11.7 12.8 %collective-permute-start.3 = (bf16[48,4096]{1,0:T(8,128)(2,1)}, bf16[48,4096]{1,0:T(8,128)(2,1)S(1)}, u32[]{:S(2)}, u32[]{:S(2)}) collective-permute-start(bf16[48,4096]{1,0:T(8,128)(2,1)} %get-tuple-element.29), channel_id=1, source_target_pairs={{0,32},{32,33},{33,1},{1,0},{2,34},{34,35},{35,3},{3,2},{4,36},{36... | collective-permute-start | bytes 1179656 | tf_op jit(solution)/shard_map/ppermute | solution.py:303
  12.4 12.1 %collective-permute-start.4 = (bf16[32,4096]{1,0:T(8,128)(2,1)}, bf16[32,4096]{1,0:T(8,128)(2,1)S(1)}, u32[]{:S(2)}, u32[]{:S(2)}) collective-permute-start(bf16[32,4096]{1,0:T(8,128)(2,1)} %get-tuple-element.30), channel_id=1, source_target_pairs={{0,32},{32,33},{33,1},{1,0},{2,34},{34,35},{35,3},{3,2},{4,36},{36... | collective-permute-start | bytes 786440 | tf_op jit(solution)/shard_map/ppermute | solution.py:303
  12.4 12.1 %collective-permute-start = (bf16[8,4096]{1,0:T(8,128)(2,1)}, bf16[8,4096]{1,0:T(8,128)(2,1)S(1)}, u32[]{:S(2)}, u32[]{:S(2)}) collective-permute-start(bf16[8,4096]{1,0:T(8,128)(2,1)} %get-tuple-element.27), channel_id=1, source_target_pairs={{0,32},{32,33},{33,1},{1,0},{2,34},{34,35},{35,3},{3,2},{4,36},{36... | collective-permute-start | bytes 196616 | tf_op jit(solution)/shard_map/ppermute | solution.py:303
  13.9 104.9 %copy-start.19 = (f32[1,768]{1,0:T(1,128)}, f32[1,768]{1,0:T(1,128)S(1)}, u32[]{:S(2)}) copy-start(f32[1,768]{1,0:T(1,128)S(1)} %reshape.15.refs_11_) | copy-start | bytes 9220
  13.9 10.5 %collective-permute-start.1 = (f32[1,768]{1,0:T(1,128)S(1)}, f32[1,768]{1,0:T(1,128)S(1)}, u32[]{:S(2)}, u32[]{:S(2)}) collective-permute-start(f32[1,768]{1,0:T(1,128)S(1)} %reshape.15.refs_11_), channel_id=1, source_target_pairs={{0,32},{32,33},{33,1},{1,0},{2,34},{34,35},{35,3},{3,2},{4,36},{36... | collective-permute-start | bytes 9224 | tf_op jit(solution)/shard_map/ppermute | solution.py:303
  25.1 121.0 %all-gather.5.cloned.1.call-start = ((), (), s32[]{:S(2)}) async-start(), calls=%async_computation.2 | async-start | bytes 4456448 | tf_op jit(solution)/shard_map/all_gather | solution.py:310
  25.2 58.9 %collective-permute-start.5 = (bf16[4096,640]{1,0:T(8,128)(2,1)}, bf16[4096,640]{1,0:T(8,128)(2,1)}, u32[]{:S(2)}, u32[]{:S(2)}) collective-permute-start(bf16[4096,640]{1,0:T(8,128)(2,1)} %bitcast.10), channel_id=1, source_target_pairs={{0,32},{32,33},{33,1},{1,0},{2,34},{34,35},{35,3},{3,2},{4,36},{36... | collective-permute-start | bytes 15728648 | tf_op jit(solution)/shard_map/ppermute | solution.py:307
  27.1 11.4 %collective-permute-start.10 = (bf16[48,4096]{1,0:T(8,128)(2,1)S(1)}, bf16[48,4096]{1,0:T(8,128)(2,1)S(1)}, u32[]{:S(2)}, u32[]{:S(2)}) collective-permute-start(bf16[48,4096]{1,0:T(8,128)(2,1)S(1)} %collective-permute-done.3.refs_5_), channel_id=1, source_target_pairs={{0,2},{2,4},{4,6},{6,0},{1,3},{3,5},{5,7},{7,1},{8,10},{10,12},{12... | collective-permute-start | bytes 1179656 | tf_op jit(solution)/shard_map/ppermute | solution.py:296
  28.5 10.7 %collective-permute-start.6 = (bf16[48,4096]{1,0:T(8,128)(2,1)S(1)}, bf16[48,4096]{1,0:T(8,128)(2,1)S(1)}, u32[]{:S(2)}, u32[]{:S(2)}) collective-permute-start(bf16[48,4096]{1,0:T(8,128)(2,1)S(1)} %collective-permute-done.2.refs_0_), channel_id=1, source_target_pairs={{0,8},{8,16},{16,24},{24,0},{1,9},{9,17},{17,25},{25,1},{2,10},{10... | collective-permute-start | bytes 1179656 | tf_op jit(solution)/shard_map/ppermute | solution.py:296
  29.7 10.1 %collective-permute-start.11 = (bf16[48,4096]{1,0:T(8,128)(2,1)S(1)}, bf16[48,4096]{1,0:T(8,128)(2,1)S(1)}, u32[]{:S(2)}, u32[]{:S(2)}) collective-permute-start(bf16[48,4096]{1,0:T(8,128)(2,1)S(1)} %collective-permute-done.3.refs_5_), channel_id=1, source_target_pairs={{0,6},{2,0},{4,2},{6,4},{1,7},{3,1},{5,3},{7,5},{8,14},{10,8},{12,... | collective-permute-start | bytes 1179656 | tf_op jit(solution)/shard_map/ppermute | solution.py:297
  31.2 11.3 %collective-permute-start.7 = (bf16[48,4096]{1,0:T(8,128)(2,1)S(1)}, bf16[48,4096]{1,0:T(8,128)(2,1)S(1)}, u32[]{:S(2)}, u32[]{:S(2)}) collective-permute-start(bf16[48,4096]{1,0:T(8,128)(2,1)S(1)} %collective-permute-done.2.refs_0_), channel_id=1, source_target_pairs={{0,24},{8,0},{16,8},{24,16},{1,25},{9,1},{17,9},{25,17},{2,26},{10... | collective-permute-start | bytes 1179656 | tf_op jit(solution)/shard_map/ppermute | solution.py:297
  38.5 8.6 %collective-permute-start.12 = (bf16[32,4096]{1,0:T(8,128)(2,1)S(1)}, bf16[32,4096]{1,0:T(8,128)(2,1)S(1)}, u32[]{:S(2)}, u32[]{:S(2)}) collective-permute-start(bf16[32,4096]{1,0:T(8,128)(2,1)S(1)} %slice.18), channel_id=1, source_target_pairs={{0,2},{2,4},{4,6},{6,0},{1,3},{3,5},{5,7},{7,1},{8,10},{10,12},{12... | collective-permute-start | bytes 786440 | tf_op jit(solution)/shard_map/ppermute | solution.py:296
  39.2 7.9 %collective-permute-start.8 = (bf16[32,4096]{1,0:T(8,128)(2,1)S(1)}, bf16[32,4096]{1,0:T(8,128)(2,1)S(1)}, u32[]{:S(2)}, u32[]{:S(2)}) collective-permute-start(bf16[32,4096]{1,0:T(8,128)(2,1)S(1)} %slice.16), channel_id=1, source_target_pairs={{0,8},{8,16},{16,24},{24,0},{1,9},{9,17},{17,25},{25,1},{2,10},{10... | collective-permute-start | bytes 786440 | tf_op jit(solution)/shard_map/ppermute | solution.py:296
  39.8 4.8 %collective-permute-start.13 = (bf16[16,4096]{1,0:T(8,128)(2,1)S(1)}, bf16[16,4096]{1,0:T(8,128)(2,1)S(1)}, u32[]{:S(2)}, u32[]{:S(2)}) collective-permute-start(bf16[16,4096]{1,0:T(8,128)(2,1)S(1)} %slice.19), channel_id=1, source_target_pairs={{0,6},{2,0},{4,2},{6,4},{1,7},{3,1},{5,3},{7,5},{8,14},{10,8},{12,... | collective-permute-start | bytes 393224 | tf_op jit(solution)/shard_map/ppermute | solution.py:297
  42.5 4.6 %collective-permute-start.9 = (bf16[16,4096]{1,0:T(8,128)(2,1)S(1)}, bf16[16,4096]{1,0:T(8,128)(2,1)S(1)}, u32[]{:S(2)}, u32[]{:S(2)}) collective-permute-start(bf16[16,4096]{1,0:T(8,128)(2,1)S(1)} %slice.17), channel_id=1, source_target_pairs={{0,24},{8,0},{16,8},{24,16},{1,25},{9,1},{17,9},{25,17},{2,26},{10... | collective-permute-start | bytes 393224 | tf_op jit(solution)/shard_map/ppermute | solution.py:297
  52.2 21.8 %collective-permute-start.14 = (bf16[96,4096]{1,0:T(8,128)(2,1)}, bf16[96,4096]{1,0:T(8,128)(2,1)}, u32[]{:S(2)}, u32[]{:S(2)}) collective-permute-start(bf16[96,4096]{1,0:T(8,128)(2,1)} %get-tuple-element.34.refs_0_), channel_id=1, source_target_pairs={{0,2},{2,4},{4,6},{6,0},{1,3},{3,5},{5,7},{7,1},{8,10},{10,12},{12... | collective-permute-start | bytes 2359304 | tf_op jit(solution)/shard_map/ppermute | solution.py:296
  52.9 21.1 %collective-permute-start.15 = (bf16[96,4096]{1,0:T(8,128)(2,1)}, bf16[96,4096]{1,0:T(8,128)(2,1)}, u32[]{:S(2)}, u32[]{:S(2)}) collective-permute-start(bf16[96,4096]{1,0:T(8,128)(2,1)} %get-tuple-element.35.refs_1_), channel_id=1, source_target_pairs={{0,6},{2,0},{4,2},{6,4},{1,7},{3,1},{5,3},{7,5},{8,14},{10,8},{12,... | collective-permute-start | bytes 2359304 | tf_op jit(solution)/shard_map/ppermute | solution.py:297
  55.0 22.1 %collective-permute-start.16 = (bf16[96,4096]{1,0:T(8,128)(2,1)}, bf16[96,4096]{1,0:T(8,128)(2,1)}, u32[]{:S(2)}, u32[]{:S(2)}) collective-permute-start(bf16[96,4096]{1,0:T(8,128)(2,1)} %get-tuple-element.36.refs_2_), channel_id=1, source_target_pairs={{0,8},{8,16},{16,24},{24,0},{1,9},{9,17},{17,25},{25,1},{2,10},{10... | collective-permute-start | bytes 2359304 | tf_op jit(solution)/shard_map/ppermute | solution.py:296
  56.2 21.1 %collective-permute-start.17 = (bf16[96,4096]{1,0:T(8,128)(2,1)}, bf16[96,4096]{1,0:T(8,128)(2,1)}, u32[]{:S(2)}, u32[]{:S(2)}) collective-permute-start(bf16[96,4096]{1,0:T(8,128)(2,1)} %get-tuple-element.37.refs_3_), channel_id=1, source_target_pairs={{0,24},{8,0},{16,8},{24,16},{1,25},{9,1},{17,9},{25,17},{2,26},{10... | collective-permute-start | bytes 2359304 | tf_op jit(solution)/shard_map/ppermute | solution.py:297
  84.1 31.6 %collective-permute-start.22 = (bf16[4096,640]{1,0:T(8,128)(2,1)}, bf16[4096,640]{1,0:T(8,128)(2,1)}, u32[]{:S(2)}, u32[]{:S(2)}) collective-permute-start(bf16[4096,640]{1,0:T(8,128)(2,1)} %collective-permute-done.5.refs_9_.refs_14_), channel_id=1, source_target_pairs={{0,32},{32,0},{1,33},{33,1},{2,34},{34,2},{3,35},{35,3},{4,36},{36... | collective-permute-start | bytes 15728648 | tf_op jit(solution)/shard_map/ppermute | solution.py:328
  87.2 24.6 %collective-permute-start.23 = (bf16[96,4096]{1,0:T(8,128)(2,1)}, bf16[96,4096]{1,0:T(8,128)(2,1)S(1)}, u32[]{:S(2)}, u32[]{:S(2)}) collective-permute-start(bf16[96,4096]{1,0:T(8,128)(2,1)} %get-tuple-element.35.refs_1_), channel_id=1, source_target_pairs={{0,2},{2,4},{4,6},{6,0},{1,3},{3,5},{5,7},{7,1},{8,10},{10,12},{12... | collective-permute-start | bytes 2359304 | tf_op jit(solution)/shard_map/ppermute | solution.py:296
  88.6 23.2 %collective-permute-start.24 = (bf16[96,4096]{1,0:T(8,128)(2,1)}, bf16[96,4096]{1,0:T(8,128)(2,1)S(1)}, u32[]{:S(2)}, u32[]{:S(2)}) collective-permute-start(bf16[96,4096]{1,0:T(8,128)(2,1)} %get-tuple-element.34.refs_0_), channel_id=1, source_target_pairs={{0,6},{2,0},{4,2},{6,4},{1,7},{3,1},{5,3},{7,5},{8,14},{10,8},{12,... | collective-permute-start | bytes 2359304 | tf_op jit(solution)/shard_map/ppermute | solution.py:297
  90.0 24.5 %collective-permute-start.25 = (bf16[96,4096]{1,0:T(8,128)(2,1)}, bf16[96,4096]{1,0:T(8,128)(2,1)S(1)}, u32[]{:S(2)}, u32[]{:S(2)}) collective-permute-start(bf16[96,4096]{1,0:T(8,128)(2,1)} %get-tuple-element.37.refs_3_), channel_id=1, source_target_pairs={{0,8},{8,16},{16,24},{24,0},{1,9},{9,17},{17,25},{25,1},{2,10},{10... | collective-permute-start | bytes 2359304 | tf_op jit(solution)/shard_map/ppermute | solution.py:296
  91.3 4.3 %collective-permute-start.27 = (f32[1,768]{1,0:T(1,128)S(1)}, f32[1,768]{1,0:T(1,128)S(1)}, u32[]{:S(2)}, u32[]{:S(2)}) collective-permute-start(f32[1,768]{1,0:T(1,128)S(1)} %collective-permute-done.1.refs_12_), channel_id=1, source_target_pairs={{0,32},{32,0},{1,33},{33,1},{2,34},{34,2},{3,35},{35,3},{4,36},{36... | collective-permute-start | bytes 9224 | tf_op jit(solution)/shard_map/ppermute | solution.py:308
  95.5 40.7 %collective-permute-start.26 = (bf16[96,4096]{1,0:T(8,128)(2,1)}, bf16[96,4096]{1,0:T(8,128)(2,1)}, u32[]{:S(2)}, u32[]{:S(2)}) collective-permute-start(bf16[96,4096]{1,0:T(8,128)(2,1)} %get-tuple-element.36.refs_2_), channel_id=1, source_target_pairs={{0,24},{8,0},{16,8},{24,16},{1,25},{9,1},{17,9},{25,17},{2,26},{10... | collective-permute-start | bytes 2359304 | tf_op jit(solution)/shard_map/ppermute | solution.py:297
  111.8 62.0 %collective-permute-start.18 = (bf16[96,4096]{1,0:T(8,128)(2,1)}, bf16[96,4096]{1,0:T(8,128)(2,1)S(1)}, u32[]{:S(2)}, u32[]{:S(2)}) collective-permute-start(bf16[96,4096]{1,0:T(8,128)(2,1)} %collective-permute-done.14.refs_0_), channel_id=1, source_target_pairs={{0,2},{2,4},{4,6},{6,0},{1,3},{3,5},{5,7},{7,1},{8,10},{10,12},{12... | collective-permute-start | bytes 2359304 | tf_op jit(solution)/shard_map/ppermute | solution.py:296
  111.9 62.0 %collective-permute-start.19 = (bf16[96,4096]{1,0:T(8,128)(2,1)}, bf16[96,4096]{1,0:T(8,128)(2,1)S(1)}, u32[]{:S(2)}, u32[]{:S(2)}) collective-permute-start(bf16[96,4096]{1,0:T(8,128)(2,1)} %collective-permute-done.15.refs_1_), channel_id=1, source_target_pairs={{0,6},{2,0},{4,2},{6,4},{1,7},{3,1},{5,3},{7,5},{8,14},{10,8},{12,... | collective-permute-start | bytes 2359304 | tf_op jit(solution)/shard_map/ppermute | solution.py:297
  114.5 59.3 %collective-permute-start.20 = (bf16[96,4096]{1,0:T(8,128)(2,1)}, bf16[96,4096]{1,0:T(8,128)(2,1)S(1)}, u32[]{:S(2)}, u32[]{:S(2)}) collective-permute-start(bf16[96,4096]{1,0:T(8,128)(2,1)} %collective-permute-done.16.refs_2_), channel_id=1, source_target_pairs={{0,8},{8,16},{16,24},{24,0},{1,9},{9,17},{17,25},{25,1},{2,10},{10... | collective-permute-start | bytes 2359304 | tf_op jit(solution)/shard_map/ppermute | solution.py:296
  115.7 58.2 %collective-permute-start.21 = (bf16[96,4096]{1,0:T(8,128)(2,1)}, bf16[96,4096]{1,0:T(8,128)(2,1)S(1)}, u32[]{:S(2)}, u32[]{:S(2)}) collective-permute-start(bf16[96,4096]{1,0:T(8,128)(2,1)} %collective-permute-done.17.refs_3_), channel_id=1, source_target_pairs={{0,24},{8,0},{16,8},{24,16},{1,25},{9,1},{17,9},{25,17},{2,26},{10... | collective-permute-start | bytes 2359304 | tf_op jit(solution)/shard_map/ppermute | solution.py:297
  (21 other events, 214.4 us)
Sparse Core Ops, SparseCore 0:
  25.2 50.1 all-gather.2
  77.6 68.4 all-gather.4

commit v3 on v2

--- a/solution.py
+++ b/solution.py
@@ -37,28 +37,32 @@
     return v[:, :128] + v[:, 128:]
 
 
-def norm_kernel(acts, query, gain, one, two, rest, qown):
-    def norm(v):
-        v = v.astype(F32)
-        scale = lax.rsqrt(jnp.mean(v * v, axis=-1, keepdims=True) + 1e-05)
-        return (v * scale * gain[...].astype(F32)).astype(BF16)
-
-    one[...] = norm(acts[HEAD:LEN, :])
-    two[...] = norm(acts[LEN + HEAD:, :])
-    rest[0:HEAD, :] = norm(acts[:HEAD, :])
-    rest[HEAD:2 * HEAD, :] = norm(acts[LEN:LEN + HEAD, :])
-    qown[...] = norm(query[...])
-
-
-def norm_call(acts, query, gain):
+def norm(v, gain):
+    v = v.astype(F32)
+    scale = lax.rsqrt(jnp.mean(v * v, axis=-1, keepdims=True) + 1e-05)
+    return (v * scale * gain[...].astype(F32)).astype(BF16)
+
+
+def query_norm_kernel(query, gain, out):
+    out[...] = norm(query[...], gain)
+
+
+def norm_kernel(acts, gain, one, two, rest):
+    one[...] = norm(acts[HEAD:LEN, :], gain)
+    two[...] = norm(acts[LEN + HEAD:, :], gain)
+    rest[0:HEAD, :] = norm(acts[:HEAD, :], gain)
+    rest[HEAD:, :] = norm(acts[LEN:LEN + HEAD, :], gain)
+
+
+def norm_call(body, rows, acts, gain):
     return pl.pallas_call(
-        norm_kernel,
-        out_shape=tuple(jax.ShapeDtypeStruct((n, D), BF16) for n in (CP, CP, 2 * HEAD, 8)),
-        in_specs=[VM] * 3,
-        out_specs=(VM,) * 4,
-        cost_estimate=pl.CostEstimate(flops=4 * 136 * D, bytes_accessed=4 * 2**20, transcendentals=136),
+        body,
+        out_shape=tuple(jax.ShapeDtypeStruct((n, D), BF16) for n in rows),
+        in_specs=[VM] * 2,
+        out_specs=(VM,) * len(rows),
+        cost_estimate=pl.CostEstimate(flops=4 * sum(rows) * D, bytes_accessed=4 * sum(rows) * D, transcendentals=sum(rows)),
         name="norm_rows",
-    )(acts, query, gain)
+    )(acts, gain)
 
 
 def copy_kernel(moves, n, m, *refs):
@@ -88,23 +92,21 @@
 def rows_kernel(shapes, block, with_queries, *refs):
     n = len(shapes)
     xin = refs[:n]
-    info, train_len, query_len, queries, own, first, second = refs[n:n + 7]
+    info, queries, own, first, second = refs[n:n + 5]
     if with_queries:
-        small, small_first, small_second, out, qg, heads = refs[n + 7:n + 13]
+        small, small_first, small_second, out, qg, heads = refs[n + 5:n + 11]
     else:
-        before, qg, heads, out = refs[n + 7:n + 11]
+        qg, heads, out = refs[n + 5:n + 8]
     xs, qs, ws, dv, acc, gram, sums_r, sums_z, xsem, qsem, wsem = refs[-11:]
     straight = info[0] == 1
     x, y, core = info[1], info[2], info[3]
 
-    starts, at = [], 0
-    for rows, _ in shapes:
+    starts, xloads, at = [], [], 0
+    for i, (shape, _) in enumerate(shapes):
         starts.append(at)
-        at += rows
+        xloads.append(pltpu.make_async_copy(xin[i], xs.at[pl.ds(at, shape[0])], xsem.at[i]))
+        at += shape[0]
     total = at
-    xloads = [
-        pltpu.make_async_copy(xin[i], xs.at[pl.ds(starts[i], shapes[i][0])], xsem.at[i]) for i in range(n)
-    ]
 
     u = lax.broadcasted_iota(jnp.int32, (NQ, 128), 0)
     lane = lax.broadcasted_iota(jnp.int32, (NQ, 128), 1)
@@ -112,7 +114,7 @@
     position = 8 * (2 * qy + jnp.where(u < 128, 1, 0)) + (u & 7)
     length = jnp.zeros((NQ, 128), jnp.int32)
     for k in range(4):
-        length = jnp.where(qx == k, query_len[k // 2, k % 2], length)
+        length = jnp.where(qx == k, info[4 + k], length)
     weight = jnp.where(position < length, 1.0 / jnp.maximum(length, 1).astype(F32), 0.0)
 
     def pick(at):
@@ -170,23 +172,27 @@
     else:
         for c in xloads:
             c.start()
-        out[...] = before[...]
+        out[...] = jnp.zeros_like(out)
         qload.wait()
         for c in xloads:
             c.wait()
         start_tiles()
 
+    def input_gram(at):
+        gram[at, :] = lax.dot_general(xs[at, :], qs[...], NT, preferred_element_type=F32)
+
+    if not with_queries:
+        @pl.loop(0, total // block)
+        def _(b):
+            input_gram(pl.ds(pl.multiple_of(b * block, block), block))
+
+        wait_tiles()
+
     @pl.loop(0, total // block)
     def _(b):
         at = pl.ds(pl.multiple_of(b * block, block), block)
-        gram[at, :] = lax.dot_general(xs[at, :], qs[...], NT, preferred_element_type=F32)
-
-    if not with_queries:
-        wait_tiles()
-
-    @pl.loop(0, total // block)
-    def _(b):
-        at = pl.ds(pl.multiple_of(b * block, block), block)
+        if with_queries:
+            input_gram(at)
         for j in range(TILES):
             cols = slice(256 * j, 256 * (j + 1))
             act, deriv = activations(jnp.dot(xs[at, :], ws[j], preferred_element_type=F32))
@@ -204,7 +210,7 @@
             place = lax.rem(x + gx + 4, 4) * 4 + lax.rem(y + gy + 4, 4) if relative else 4 * gx + gy
             runs.append((starts[i] + row, count, side, place, slot))
     for k, (row, count, side, place, slot) in enumerate(runs):
-        length = train_len[place * 2 + 1 - core, side]
+        length = info[8 + 2 * (place * 2 + 1 - core) + side]
         live = lax.broadcasted_iota(jnp.int32, (count, 1), 0) + slot < length
         live = jnp.where(live, 1.0 / jnp.maximum(length, 1).astype(F32), 0.0)
         sums_r[k:k + 1, :] = jnp.sum(acc[row:row + count, :] * live, axis=0, keepdims=True)
@@ -228,8 +234,9 @@
 
 def rows_call(rows, block, name, given, with_queries):
     xin = [r[0] for r in rows]
-    shapes = tuple((v.shape[0], found) for v, found in rows)
-    n, total = len(rows), sum(v.shape[0] for v in xin)
+    shapes = tuple((v.shape, found) for v, found in rows)
+    n = len(rows)
+    total = sum(v.shape[0] for v in xin)
     runs = sum(len(found) for _, found in rows)
     out_shape = [jax.ShapeDtypeStruct((16, 128), F32)]
     if with_queries:
@@ -237,7 +244,7 @@
     return pl.pallas_call(
         functools.partial(rows_kernel, shapes, block, with_queries),
         out_shape=tuple(out_shape),
-        in_specs=[HBM] * n + [SM] * 3 + [HBM] * 4 + [VM] * 3,
+        in_specs=[HBM] * n + [SM] + [HBM] * 4 + [VM] * (3 if with_queries else 2),
         out_specs=(VM,) * len(out_shape),
         scratch_shapes=[
             pltpu.VMEM((total, D), BF16),
@@ -296,23 +303,25 @@
     low = lambda v, axis: lax.ppermute(v, axis, ring(1))
     high = lambda v, axis: lax.ppermute(v, axis, ring(-1))
 
-    one, two, rest, qown = norm_call(train_acts[0], query_acts[0], norm_gain)
+    (query,) = norm_call(query_norm_kernel, (8,), query_acts[0], norm_gain)
+    query_turned = turn(query)
+    acts, _ = lax.optimization_barrier((train_acts[0], query))
+    one, two, rest = norm_call(norm_kernel, (CP, CP, 2 * HEAD), acts, norm_gain)
     small = jnp.concatenate(
         [readout[0].astype(F32), jnp.zeros((RATE,), F32), lr_weight, jnp.zeros((127 - RATE,), F32)]
     ).reshape(1, FD + 128)
-    qown, small_first, one, two, rest = turn(qown), turn(small), turn(one), turn(two), turn(rest)
-    weight_own, qown, small_first, one, two, rest = lax.optimization_barrier(
-        (up_weight[0], qown, small_first, one, two, rest)
-    )
+    query_turned, one = lax.optimization_barrier((query_turned, one))
+    small_first, one, two, rest = turn(small), turn(one), turn(two), turn(rest)
+    weight_own, small_first, one, two, rest = lax.optimization_barrier((up_weight[0], small_first, one, two, rest))
     weight_first = turn(weight_own)
-    small_second = swap(small_first)
-    queries = lax.all_gather(qown, ("c", "x", "y"), axis=0, tiled=True)
+    queries = lax.all_gather(query_turned, ("c", "x", "y"), axis=0, tiled=True)
     some = lax.all_gather(rest, ("x", "y"), axis=0, tiled=True)
 
     one_low, one_high = low(one, "x"), high(one, "x")
     two_low, two_high = low(two, "y"), high(two, "y")
     one_a, one_b = low(one_low[:32], "x"), high(one_high[32:], "x")
     two_a, two_b = low(two_low[:32], "y"), high(two_high[32:], "y")
+    one_low, small_second = lax.optimization_barrier((one_low, swap(small_first)))
     moves = []
     for g in (0, 1):
         moves += [(5 * g, 0, 2 * g, 0, CP), (5 * g + 1, 0, 2 * g, CP, CP), (5 * g + 2, 0, 2 * g + 1, 0, CP),
@@ -328,36 +337,43 @@
     weight_second = swap(weight_first)
     b1_low, a1_high = low(b1, "y"), high(a1, "y")
     b2_low, a2_high = low(b2, "x"), high(a2, "x")
-    a1_far, b1_far = low(a1_low, "y"), high(b1_high, "y")
-    a2_far, b2_far = low(a2_low, "x"), high(b2_high, "x")
-
-    def group(side, g, ks):
+
+    def group(*halves):
         found = []
-        for i, k in enumerate(ks):
-            gx, gy = (OFFS[k], OFFS[g]) if side == 0 else (OFFS[g], OFFS[k])
-            found.append((CP * i, CP, side, True, gx, gy, HEAD))
+        for side, g, ks in halves:
+            for k in ks:
+                gx, gy = (OFFS[k], OFFS[g]) if side == 0 else (OFFS[g], OFFS[k])
+                found.append((CP * len(found), CP, side, True, gx, gy, HEAD))
         return tuple(found)
 
     gathered_runs = tuple(
         (HEAD * (2 * p + side), HEAD, side, False, p // 4, p % 4, 0) for p in range(16) for side in (0, 1)
     )
-    near, rest = (0, 1), (2, 3)
-    info = jnp.stack([straight.astype(jnp.int32), x, y, core])
-    given = (info, train_len, query_len, queries, weight_own, weight_first, weight_second)
+    near, far = (0, 1), (2, 3)
+    info = jnp.concatenate([
+        jnp.stack([straight.astype(jnp.int32), x, y, core]), query_len.reshape(-1), train_len.reshape(-1)
+    ])
+    given = (info, queries, weight_own, weight_first, weight_second)
     sums, *kept = rows_call(
-        [(a1, group(0, 0, near)), (b1, group(0, 0, rest)), (a2, group(1, 0, near)), (b2, group(1, 0, rest))],
-        192, "first_rows", (*given, small, small_first, small_second), True,
-    )
-    (sums,) = rows_call(
-        [(a1_low, group(0, 1, near)), (b1_high, group(0, 2, rest)), (a2_low, group(1, 1, near)), (b2_high, group(1, 2, rest)),
-         (b1_low, group(0, 1, rest)), (a1_high, group(0, 2, near)), (b2_low, group(1, 1, rest)), (a2_high, group(1, 2, near)),
-         (some, gathered_runs)],
-        256, "next_rows", (*given, sums, *kept), False,
-    )
-    (sums,) = rows_call(
-        [(a1_far, group(0, 3, near)), (b1_far, group(0, 3, rest)), (a2_far, group(1, 3, near)), (b2_far, group(1, 3, rest))],
-        192, "last_rows", (*given, sums, *kept), False,
-    )
+        [(a1, group((0, 0, near))), (b1, group((0, 0, far))), (a2, group((1, 0, near))), (b2, group((1, 0, far))),
+         (a1_low, group((0, 1, near))), (b1_high, group((0, 2, far))),
+         (a2_low, group((1, 1, near))), (b2_high, group((1, 2, far)))],
+        256, "first_rows", (*given, small, small_first, small_second), True,
+    )
+    sums, a1_on, b1_on, a2_on, b2_on = lax.optimization_barrier((sums, a1_low, b1_high, a2_low, b2_high))
+    a1_far, b1_far = low(a1_on, "y"), high(b1_on, "y")
+    a2_far, b2_far = low(a2_on, "x"), high(b2_on, "x")
+    (more,) = rows_call(
+        [(b1_low, group((0, 1, far))), (a1_high, group((0, 2, near))),
+         (b2_low, group((1, 1, far))), (a2_high, group((1, 2, near))), (some, gathered_runs)],
+        224, "next_rows", (*given, *kept), False,
+    )
+    (last,) = rows_call(
+        [(a1_far, group((0, 3, near))), (b1_far, group((0, 3, far))),
+         (a2_far, group((1, 3, near))), (b2_far, group((1, 3, far)))],
+        192, "last_rows", (*given, *kept), False,
+    )
+    sums = sums + more + last
     message = jnp.broadcast_to(sums.reshape(1, 16, 1, 128), (4, 16, 2, 128)).reshape(128, 128)
     got = lax.all_to_all(message, ("zh", "c", "x", "y", "zl"), split_axis=0, concat_axis=0, tiled=True)
     return final_call(plane.reshape(1), got)

time: 218 us -> 198 us (0.908)
  waiting for transfers between devices: 72 us -> 48 us
  starting transfers between devices: 38.8 us -> 43 us
    ppermute x10, waiting for transfers between devices: 39.6 us -> 26.1 us  [local(): low = lambda v, axis: lax.ppermute(v, axis, ring(1))]
    all_gather x1, waiting for transfers between devices: 9.92 us -> 1.16 us  [local(): some = lax.all_gather(rest, ('x', 'y'), axis=0, tiled=True)]
    ppermute x2, starting transfers between devices: 0.83 us -> 5.42 us  [the longest x1 2.95 us: local(): swap(small_first)]
    ppermute x2, waiting for transfers between devices: 3.48 us -> 0.01 us  [the longest x1 0.01 us: local(): query_turned = turn(query)]
    ppermute x1, starting transfers between devices: 2.47 us -> 0.09 us  [local(): turn(one)]
    unnamed x47 -> x55, local copies, waits for them, and re-layouts: 4.97 us -> 4.41 us
  transfers between devices with their start and end apart: 30 -> 30, of which waited for: 12 -> 13; matrix products, arithmetic and copies ran while one was open for 1% -> 1% of each run, Pallas kernels for 22% -> 25%
where the time goes in v3:
time: 198 us; the launch traced here: 197 us
  Pallas kernels  66.6 us (34%)
  waiting for transfers between devices  48 us (24%)
  starting transfers between devices  43 us (22%)
  blocking collectives  18.3 us (9%)
  between operations  14.4 us (7%)
  local copies, waits for them, and re-layouts  5.37 us (3%)
    pallas_call x3, Pallas kernels, rows_call(): pl.pallas_call(functools.partial(rows_kernel, shapes, block, with_queries...  57.4 us
    ppermute x10, waiting for transfers between devices, local(): low = lambda v, axis: lax.ppermute(v, axis, ring(1))  26.1 us
    ppermute x10, starting transfers between devices, local(): high = lambda v, axis: lax.ppermute(v, axis, ring(-1))  18.6 us
    all_to_all x1, blocking collectives, local(): lax.all_to_all(message, ('zh', 'c', 'x', 'y', 'zl'), split_axis=0, concat...  18.3 us
    ppermute x10, starting transfers between devices, local(): low = lambda v, axis: lax.ppermute(v, axis, ring(1))  9.89 us
    ppermute x1, waiting for transfers between devices, local(): turn(small)  8.61 us
    ppermute x1, waiting for transfers between devices, local(): weight_first = turn(weight_own)  5.75 us
    unnamed x55, local copies, waits for them, and re-layouts  4.41 us
  transfers between devices with their start and end apart: 30, of which 13 were waited for; matrix products, arithmetic and copies ran while one was open for 1% of the time, Pallas kernels for 25%

profile of v3, /device:TPU:1, one launch (start us, length us, event | category | flops | bytes accessed | tf_op | source)
XLA Modules:
  0.0 197.2 jit_solution(2649180575191554156)
XLA Ops:
  6.5 1.6 norm_rows.2
  8.2 2.5 %collective-permute-start.1 = (bf16[8,4096]{1,0:T(8,128)(2,1)}, bf16[8,4096]{1,0:T(8,128)(2,1)S(1)}, u32[]{:S(2)}, u32[]{:S(2)}) collective-permute-start(bf16[8,4096]{1,0:T(8,128)(2,1)} %norm_rows.2), channel_id=1, source_target_pairs={{0,32},{32,33},{33,1},{1,0},{2,34},{34,35},{35,3},{3,2},{4,36},{36... | collective-permute-start | bytes 196616 | tf_op jit(solution)/shard_map/ppermute | solution.py:307
  10.6 2.6 %norm_rows.3 = (bf16[48,4096]{1,0:T(8,128)(2,1)}, bf16[48,4096]{1,0:T(8,128)(2,1)}, bf16[32,4096]{1,0:T(8,128)(2,1)}) custom-call(bf16[128,4096]{1,0:T(8,128)(2,1)} %bitcast.14, bf16[1,4096]{1,0:T(2,128)(2,1)} %gain.3), custom_call_target="tpu_custom_call" | custom-call | flops 2097152 | bytes 2097152 | tf_op jit(solution)/shard_map/norm_rows/pallas_call | solution.py:58
  14.8 1.8 collective-permute-start.4
  18.2 8.6 %collective-permute-done.refs_14_ = f32[1,768]{1,0:T(1,128)S(1)} collective-permute-done((f32[1,768]{1,0:T(1,128)S(1)}, f32[1,768]{1,0:T(1,128)S(1)}, u32[]{:S(2)}, u32[]{:S(2)}) %collective-permute-start) | collective-permute-done | bytes 3104 | tf_op jit(solution)/shard_map/ppermute | solution.py:314
  26.8 1.9 collective-permute-start.14
  31.3 1.5 collective-permute-start.7
  32.8 1.4 collective-permute-start.11
  34.2 5.4 %collective-permute-done.5.refs_1_ = bf16[48,4096]{1,0:T(8,128)(2,1)S(1)} collective-permute-done((bf16[48,4096]{1,0:T(8,128)(2,1)S(1)}, bf16[48,4096]{1,0:T(8,128)(2,1)S(1)}, u32[]{:S(2)}, u32[]{:S(2)}) %collective-permute-start.5) | collective-permute-done | bytes 393248 | tf_op jit(solution)/shard_map/ppermute | solution.py:303
  41.4 3.0 %collective-permute-start.6 = (f32[1,768]{1,0:T(1,128)S(1)}, f32[1,768]{1,0:T(1,128)S(1)}, u32[]{:S(2)}, u32[]{:S(2)}) collective-permute-start(f32[1,768]{1,0:T(1,128)S(1)} %collective-permute-done.refs_14_), channel_id=1, source_target_pairs={{0,32},{32,0},{1,33},{33,1},{2,34},{34,2},{3,35},{35,3},{4,36},{36... | collective-permute-start | bytes 9224 | tf_op jit(solution)/shard_map/ppermute | solution.py:324
  44.4 2.7 %collective-permute-start.9 = (bf16[16,4096]{1,0:T(8,128)(2,1)S(1)}, bf16[16,4096]{1,0:T(8,128)(2,1)S(1)}, u32[]{:S(2)}, u32[]{:S(2)}) collective-permute-start(bf16[16,4096]{1,0:T(8,128)(2,1)S(1)} %slice.17), channel_id=1, source_target_pairs={{0,24},{8,0},{16,8},{24,16},{1,25},{9,1},{17,9},{25,17},{2,26},{10... | collective-permute-start | bytes 393224 | tf_op jit(solution)/shard_map/ppermute | solution.py:304
  47.1 1.4 collective-permute-start.13
  48.5 1.7 collective-permute-done.9.refs_4_
  50.2 2.0 %collective-permute-done.13.refs_9_ = bf16[16,4096]{1,0:T(8,128)(2,1)S(1)} collective-permute-done((bf16[16,4096]{1,0:T(8,128)(2,1)S(1)}, bf16[16,4096]{1,0:T(8,128)(2,1)S(1)}, u32[]{:S(2)}, u32[]{:S(2)}) %collective-permute-start.13) | collective-permute-done | bytes 131104 | tf_op jit(solution)/shard_map/ppermute | solution.py:304
  53.7 3.6 %join_rows.1 = (bf16[96,4096]{1,0:T(8,128)(2,1)}, bf16[96,4096]{1,0:T(8,128)(2,1)}, bf16[96,4096]{1,0:T(8,128)(2,1)}, bf16[96,4096]{1,0:T(8,128)(2,1)}) custom-call(bf16[48,4096]{1,0:T(8,128)(2,1)} %copy-done.13, bf16[48,4096]{1,0:T(8,128)(2,1)} %copy-done, bf16[48,4096]{1,0:T(8,128)(2,1)} %copy-done.10, bf16[32,4096]{1,0:T(8,128)(2,1)} %copy-done.14, ...), custom_call_target="tpu_custom_call" | custom-call | bytes 6291456 | tf_op jit(solution)/shard_map/join_rows/pallas_call | solution.py:81
  60.1 2.7 %collective-permute-start.18 = (bf16[96,4096]{1,0:T(8,128)(2,1)}, bf16[96,4096]{1,0:T(8,128)(2,1)S(1)}, u32[]{:S(2)}, u32[]{:S(2)}) collective-permute-start(bf16[96,4096]{1,0:T(8,128)(2,1)} %get-tuple-element.47.refs_3_), channel_id=1, source_target_pairs={{0,24},{8,0},{16,8},{24,16},{1,25},{9,1},{17,9},{25,17},{2,26},{10... | collective-permute-start | bytes 2359304 | tf_op jit(solution)/shard_map/ppermute | solution.py:304
  62.8 13.6 %collective-permute-done.15.refs_4_ = bf16[96,4096]{1,0:T(8,128)(2,1)S(1)} collective-permute-done((bf16[96,4096]{1,0:T(8,128)(2,1)}, bf16[96,4096]{1,0:T(8,128)(2,1)S(1)}, u32[]{:S(2)}, u32[]{:S(2)}) %collective-permute-start.15) | collective-permute-done | bytes 786464 | tf_op jit(solution)/shard_map/ppermute | solution.py:303
  76.9 3.1 %collective-permute-done.17.refs_6_ = bf16[96,4096]{1,0:T(8,128)(2,1)S(1)} collective-permute-done((bf16[96,4096]{1,0:T(8,128)(2,1)}, bf16[96,4096]{1,0:T(8,128)(2,1)S(1)}, u32[]{:S(2)}, u32[]{:S(2)}) %collective-permute-start.17) | collective-permute-done | bytes 786464 | tf_op jit(solution)/shard_map/ppermute | solution.py:303
  80.0 5.8 %collective-permute-done.14.refs_11_.refs_8_.refs_7_ = bf16[4096,640]{1,0:T(8,128)(2,1)} collective-permute-done((bf16[4096,640]{1,0:T(8,128)(2,1)}, bf16[4096,640]{1,0:T(8,128)(2,1)}, u32[]{:S(2)}, u32[]{:S(2)}) %collective-permute-start.14) | collective-permute-done | bytes 5242912 | tf_op jit(solution)/shard_map/ppermute | solution.py:316
  85.7 4.3 %collective-permute-start.19 = (bf16[4096,640]{1,0:T(8,128)(2,1)}, bf16[4096,640]{1,0:T(8,128)(2,1)}, u32[]{:S(2)}, u32[]{:S(2)}) collective-permute-start(bf16[4096,640]{1,0:T(8,128)(2,1)} %collective-permute-done.14.refs_11_.refs_8_.refs_7_), channel_id=1, source_target_pairs={{0,32},{32,0},{1,33},{33,1},{2,34},{34,2},{3,35},{35,3},{4,36},{36... | collective-permute-start | bytes 15728648 | tf_op jit(solution)/shard_map/ppermute | solution.py:337
  91.4 1.4 collective-permute-start.21
  95.0 1.5 collective-permute-start.23
  96.5 2.2 %collective-permute-done.19.refs_12_.refs_9_.refs_8_ = bf16[4096,640]{1,0:T(8,128)(2,1)} collective-permute-done((bf16[4096,640]{1,0:T(8,128)(2,1)}, bf16[4096,640]{1,0:T(8,128)(2,1)}, u32[]{:S(2)}, u32[]{:S(2)}) %collective-permute-start.19) | collective-permute-done | bytes 5242912 | tf_op jit(solution)/shard_map/ppermute | solution.py:337
  98.7 21.5 %first_rows.1 = (f32[16,128]{1,0:T(8,128)}, bf16[256,1280]{1,0:T(8,128)(2,1)}, f32[1,1280]{1,0:T(1,128)}) custom-call(bf16[96,4096]{1,0:T(8,128)(2,1)} %get-tuple-element.44.refs_0_, bf16[96,4096]{1,0:T(8,128)(2,1)} %get-tuple-element.45.refs_1_, bf16[96,4096]{1,0:T(8,128)(2,1)} %get-tuple-element.46.refs_2_, bf16[96,4096]{1,0:T(8,128)(2,1)} %get-tuple-element.47.refs_3_, ...), custom_call_target="tpu_custom_call" | custom-call | flops 1 | bytes 1 | tf_op jit(solution)/shard_map/first_rows/pallas_call | solution.py:244
  120.2 1.5 collective-permute-start.24
  121.7 1.7 collective-permute-done.20.refs_0_
  123.4 2.3 %collective-permute-start.25 = (bf16[96,4096]{1,0:T(8,128)(2,1)}, bf16[96,4096]{1,0:T(8,128)(2,1)S(1)}, u32[]{:S(2)}, u32[]{:S(2)}) collective-permute-start(bf16[96,4096]{1,0:T(8,128)(2,1)} %copy-done.3), channel_id=1, source_target_pairs={{0,6},{2,0},{4,2},{6,4},{1,7},{3,1},{5,3},{7,5},{8,14},{10,8},{12,... | collective-permute-start | bytes 2359304 | tf_op jit(solution)/shard_map/ppermute | solution.py:304
  128.1 2.3 %collective-permute-start.27 = (bf16[96,4096]{1,0:T(8,128)(2,1)}, bf16[96,4096]{1,0:T(8,128)(2,1)S(1)}, u32[]{:S(2)}, u32[]{:S(2)}) collective-permute-start(bf16[96,4096]{1,0:T(8,128)(2,1)} %copy-done.5), channel_id=1, source_target_pairs={{0,24},{8,0},{16,8},{24,16},{1,25},{9,1},{17,9},{25,17},{2,26},{10... | collective-permute-start | bytes 2359304 | tf_op jit(solution)/shard_map/ppermute | solution.py:304
  131.6 21.9 %next_rows.1 = f32[16,128]{1,0:T(8,128)} custom-call(bf16[96,4096]{1,0:T(8,128)(2,1)} %collective-permute-done.20.refs_0_, bf16[96,4096]{1,0:T(8,128)(2,1)} %collective-permute-done.21.refs_1_, bf16[96,4096]{1,0:T(8,128)(2,1)} %collective-permute-done.22.refs_2_, bf16[96,4096]{1,0:T(8,128)(2,1)} %collective-permute-done.23.refs_3_, ...), custom_call_target="tpu_custom_call" | custom-call | flops 1 | bytes 1 | tf_op jit(solution)/shard_map/next_rows/pallas_call | solution.py:244
  155.9 13.9 %last_rows.1 = f32[16,128]{1,0:T(8,128)} custom-call(bf16[96,4096]{1,0:T(8,128)(2,1)} %copy-done.6, bf16[96,4096]{1,0:T(8,128)(2,1)} %copy-done.7, bf16[96,4096]{1,0:T(8,128)(2,1)} %copy-done.8, bf16[96,4096]{1,0:T(8,128)(2,1)} %copy-done.9, s32[72]{0:T(128)} %concatenate.7.refs_8_.refs_5_.refs_4_, ...), custom_call_target="tpu_custom_call" | custom-call | flops 1 | bytes 1 | tf_op jit(solution)/shard_map/last_rows/pallas_call | solution.py:244
  170.6 18.3 %all_to_all.11 = f32[128,1,128]{2,1,0:T(1,128)} all-to-all(f32[128,1,128]{2,1,0:T(1,128)S(1)} %bitcast.16), channel_id=1, replica_groups=mesh['zh'=2,'c'=2,'x'=4,'y'=4,'zl'=2] {'zh','c','x','y','zl'}, dimensions={0} | all-to-all | bytes 131072 | tf_op jit(solution)/shard_map/all_to_all | solution.py:378
  188.9 1.5 influence.1
  (107 shorter events, 21.7 us)
Async XLA Ops:
  6.5 87.5 %copy-start.26 = (s32[2,2]{1,0:T(2,128)S(1)}, s32[2,2]{1,0:T(2,128)}, u32[]{:S(2)}) copy-start(s32[2,2]{1,0:T(2,128)} %param.11) | copy-start | bytes 52
  6.5 87.6 %copy-start.25 = (s32[32,2]{0,1:T(2,128)S(1)}, s32[32,2]{0,1:T(2,128)}, u32[]{:S(2)}) copy-start(s32[32,2]{0,1:T(2,128)} %param.9) | copy-start | bytes 772
  6.5 90.0 %all-gather.3.cloned.1.call-start = ((), (), s32[]{:S(2)}) async-start(), calls=%async_computation.1 | async-start | bytes 2162688 | tf_op jit(solution)/shard_map/all_gather | solution.py:317
  8.2 5.0 %collective-permute-start.1 = (bf16[8,4096]{1,0:T(8,128)(2,1)}, bf16[8,4096]{1,0:T(8,128)(2,1)S(1)}, u32[]{:S(2)}, u32[]{:S(2)}) collective-permute-start(bf16[8,4096]{1,0:T(8,128)(2,1)} %norm_rows.2), channel_id=1, source_target_pairs={{0,32},{32,33},{33,1},{1,0},{2,34},{34,35},{35,3},{3,2},{4,36},{36... | collective-permute-start | bytes 196616 | tf_op jit(solution)/shard_map/ppermute | solution.py:307
  13.8 117.8 %all-gather.5.cloned.1.call-start = ((), (), s32[]{:S(2)}) async-start(), calls=%async_computation.2 | async-start | bytes 4456448 | tf_op jit(solution)/shard_map/all_gather | solution.py:318
  13.9 12.9 %collective-permute-start.3 = (bf16[48,4096]{1,0:T(8,128)(2,1)}, bf16[48,4096]{1,0:T(8,128)(2,1)S(1)}, u32[]{:S(2)}, u32[]{:S(2)}) collective-permute-start(bf16[48,4096]{1,0:T(8,128)(2,1)} %get-tuple-element.38), channel_id=1, source_target_pairs={{0,32},{32,33},{33,1},{1,0},{2,34},{34,35},{35,3},{3,2},{4,36},{36... | collective-permute-start | bytes 1179656 | tf_op jit(solution)/shard_map/ppermute | solution.py:314
  14.7 12.1 %collective-permute-start.2 = (bf16[48,4096]{1,0:T(8,128)(2,1)}, bf16[48,4096]{1,0:T(8,128)(2,1)S(1)}, u32[]{:S(2)}, u32[]{:S(2)}) collective-permute-start(bf16[48,4096]{1,0:T(8,128)(2,1)} %get-tuple-element.37), channel_id=1, source_target_pairs={{0,32},{32,33},{33,1},{1,0},{2,34},{34,35},{35,3},{3,2},{4,36},{36... | collective-permute-start | bytes 1179656 | tf_op jit(solution)/shard_map/ppermute | solution.py:314
  14.8 12.0 %collective-permute-start.4 = (bf16[32,4096]{1,0:T(8,128)(2,1)}, bf16[32,4096]{1,0:T(8,128)(2,1)S(1)}, u32[]{:S(2)}, u32[]{:S(2)}) collective-permute-start(bf16[32,4096]{1,0:T(8,128)(2,1)} %get-tuple-element.39), channel_id=1, source_target_pairs={{0,32},{32,33},{33,1},{1,0},{2,34},{34,35},{35,3},{3,2},{4,36},{36... | collective-permute-start | bytes 786440 | tf_op jit(solution)/shard_map/ppermute | solution.py:314
  18.0 8.7 %collective-permute-start = (f32[1,768]{1,0:T(1,128)S(1)}, f32[1,768]{1,0:T(1,128)S(1)}, u32[]{:S(2)}, u32[]{:S(2)}) collective-permute-start(f32[1,768]{1,0:T(1,128)S(1)} %reshape.21.refs_13_), channel_id=1, source_target_pairs={{0,32},{32,33},{33,1},{1,0},{2,34},{34,35},{35,3},{3,2},{4,36},{36... | collective-permute-start | bytes 9224 | tf_op jit(solution)/shard_map/ppermute | solution.py:314
  26.8 58.9 %collective-permute-start.14 = (bf16[4096,640]{1,0:T(8,128)(2,1)}, bf16[4096,640]{1,0:T(8,128)(2,1)}, u32[]{:S(2)}, u32[]{:S(2)}) collective-permute-start(bf16[4096,640]{1,0:T(8,128)(2,1)} %bitcast.10), channel_id=1, source_target_pairs={{0,32},{32,33},{33,1},{1,0},{2,34},{34,35},{35,3},{3,2},{4,36},{36... | collective-permute-start | bytes 15728648 | tf_op jit(solution)/shard_map/ppermute | solution.py:316
  28.8 10.9 %collective-permute-start.5 = (bf16[48,4096]{1,0:T(8,128)(2,1)S(1)}, bf16[48,4096]{1,0:T(8,128)(2,1)S(1)}, u32[]{:S(2)}, u32[]{:S(2)}) collective-permute-start(bf16[48,4096]{1,0:T(8,128)(2,1)S(1)} %collective-permute-done.2.refs_0_), channel_id=1, source_target_pairs={{0,8},{8,16},{16,24},{24,0},{1,9},{9,17},{17,25},{25,1},{2,10},{10... | collective-permute-start | bytes 1179656 | tf_op jit(solution)/shard_map/ppermute | solution.py:303
  30.0 10.9 %collective-permute-start.10 = (bf16[48,4096]{1,0:T(8,128)(2,1)S(1)}, bf16[48,4096]{1,0:T(8,128)(2,1)S(1)}, u32[]{:S(2)}, u32[]{:S(2)}) collective-permute-start(bf16[48,4096]{1,0:T(8,128)(2,1)S(1)} %collective-permute-done.3.refs_5_), channel_id=1, source_target_pairs={{0,2},{2,4},{4,6},{6,0},{1,3},{3,5},{5,7},{7,1},{8,10},{10,12},{12... | collective-permute-start | bytes 1179656 | tf_op jit(solution)/shard_map/ppermute | solution.py:303
  31.3 10.0 %collective-permute-start.7 = (bf16[48,4096]{1,0:T(8,128)(2,1)S(1)}, bf16[48,4096]{1,0:T(8,128)(2,1)S(1)}, u32[]{:S(2)}, u32[]{:S(2)}) collective-permute-start(bf16[48,4096]{1,0:T(8,128)(2,1)S(1)} %collective-permute-done.2.refs_0_), channel_id=1, source_target_pairs={{0,24},{8,0},{16,8},{24,16},{1,25},{9,1},{17,9},{25,17},{2,26},{10... | collective-permute-start | bytes 1179656 | tf_op jit(solution)/shard_map/ppermute | solution.py:304
  32.8 11.5 %collective-permute-start.11 = (bf16[48,4096]{1,0:T(8,128)(2,1)S(1)}, bf16[48,4096]{1,0:T(8,128)(2,1)S(1)}, u32[]{:S(2)}, u32[]{:S(2)}) collective-permute-start(bf16[48,4096]{1,0:T(8,128)(2,1)S(1)} %collective-permute-done.3.refs_5_), channel_id=1, source_target_pairs={{0,6},{2,0},{4,2},{6,4},{1,7},{3,1},{5,3},{7,5},{8,14},{10,8},{12,... | collective-permute-start | bytes 1179656 | tf_op jit(solution)/shard_map/ppermute | solution.py:304
  39.7 12.5 %collective-permute-start.8 = (bf16[32,4096]{1,0:T(8,128)(2,1)S(1)}, bf16[32,4096]{1,0:T(8,128)(2,1)S(1)}, u32[]{:S(2)}, u32[]{:S(2)}) collective-permute-start(bf16[32,4096]{1,0:T(8,128)(2,1)S(1)} %slice.16), channel_id=1, source_target_pairs={{0,8},{8,16},{16,24},{24,0},{1,9},{9,17},{17,25},{25,1},{2,10},{10... | collective-permute-start | bytes 786440 | tf_op jit(solution)/shard_map/ppermute | solution.py:303
  41.0 11.3 %collective-permute-start.12 = (bf16[32,4096]{1,0:T(8,128)(2,1)S(1)}, bf16[32,4096]{1,0:T(8,128)(2,1)S(1)}, u32[]{:S(2)}, u32[]{:S(2)}) collective-permute-start(bf16[32,4096]{1,0:T(8,128)(2,1)S(1)} %slice.18), channel_id=1, source_target_pairs={{0,2},{2,4},{4,6},{6,0},{1,3},{3,5},{5,7},{7,1},{8,10},{10,12},{12... | collective-permute-start | bytes 786440 | tf_op jit(solution)/shard_map/ppermute | solution.py:303
  41.4 5.7 %collective-permute-start.6 = (f32[1,768]{1,0:T(1,128)S(1)}, f32[1,768]{1,0:T(1,128)S(1)}, u32[]{:S(2)}, u32[]{:S(2)}) collective-permute-start(f32[1,768]{1,0:T(1,128)S(1)} %collective-permute-done.refs_14_), channel_id=1, source_target_pairs={{0,32},{32,0},{1,33},{33,1},{2,34},{34,2},{3,35},{35,3},{4,36},{36... | collective-permute-start | bytes 9224 | tf_op jit(solution)/shard_map/ppermute | solution.py:324
  44.4 5.8 %collective-permute-start.9 = (bf16[16,4096]{1,0:T(8,128)(2,1)S(1)}, bf16[16,4096]{1,0:T(8,128)(2,1)S(1)}, u32[]{:S(2)}, u32[]{:S(2)}) collective-permute-start(bf16[16,4096]{1,0:T(8,128)(2,1)S(1)} %slice.17), channel_id=1, source_target_pairs={{0,24},{8,0},{16,8},{24,16},{1,25},{9,1},{17,9},{25,17},{2,26},{10... | collective-permute-start | bytes 393224 | tf_op jit(solution)/shard_map/ppermute | solution.py:304
  47.1 5.2 %collective-permute-start.13 = (bf16[16,4096]{1,0:T(8,128)(2,1)S(1)}, bf16[16,4096]{1,0:T(8,128)(2,1)S(1)}, u32[]{:S(2)}, u32[]{:S(2)}) collective-permute-start(bf16[16,4096]{1,0:T(8,128)(2,1)S(1)} %slice.19), channel_id=1, source_target_pairs={{0,6},{2,0},{4,2},{6,4},{1,7},{3,1},{5,3},{7,5},{8,14},{10,8},{12,... | collective-permute-start | bytes 393224 | tf_op jit(solution)/shard_map/ppermute | solution.py:304
  57.4 19.0 %collective-permute-start.15 = (bf16[96,4096]{1,0:T(8,128)(2,1)}, bf16[96,4096]{1,0:T(8,128)(2,1)S(1)}, u32[]{:S(2)}, u32[]{:S(2)}) collective-permute-start(bf16[96,4096]{1,0:T(8,128)(2,1)} %get-tuple-element.44.refs_0_), channel_id=1, source_target_pairs={{0,2},{2,4},{4,6},{6,0},{1,3},{3,5},{5,7},{7,1},{8,10},{10,12},{12... | collective-permute-start | bytes 2359304 | tf_op jit(solution)/shard_map/ppermute | solution.py:303
  58.7 18.1 %collective-permute-start.16 = (bf16[96,4096]{1,0:T(8,128)(2,1)}, bf16[96,4096]{1,0:T(8,128)(2,1)S(1)}, u32[]{:S(2)}, u32[]{:S(2)}) collective-permute-start(bf16[96,4096]{1,0:T(8,128)(2,1)} %get-tuple-element.45.refs_1_), channel_id=1, source_target_pairs={{0,6},{2,0},{4,2},{6,4},{1,7},{3,1},{5,3},{7,5},{8,14},{10,8},{12,... | collective-permute-start | bytes 2359304 | tf_op jit(solution)/shard_map/ppermute | solution.py:304
  60.1 19.9 %collective-permute-start.17 = (bf16[96,4096]{1,0:T(8,128)(2,1)}, bf16[96,4096]{1,0:T(8,128)(2,1)S(1)}, u32[]{:S(2)}, u32[]{:S(2)}) collective-permute-start(bf16[96,4096]{1,0:T(8,128)(2,1)} %get-tuple-element.46.refs_2_), channel_id=1, source_target_pairs={{0,8},{8,16},{16,24},{24,0},{1,9},{9,17},{17,25},{25,1},{2,10},{10... | collective-permute-start | bytes 2359304 | tf_op jit(solution)/shard_map/ppermute | solution.py:303
  60.1 19.9 %collective-permute-start.18 = (bf16[96,4096]{1,0:T(8,128)(2,1)}, bf16[96,4096]{1,0:T(8,128)(2,1)S(1)}, u32[]{:S(2)}, u32[]{:S(2)}) collective-permute-start(bf16[96,4096]{1,0:T(8,128)(2,1)} %get-tuple-element.47.refs_3_), channel_id=1, source_target_pairs={{0,24},{8,0},{16,8},{24,16},{1,25},{9,1},{17,9},{25,17},{2,26},{10... | collective-permute-start | bytes 2359304 | tf_op jit(solution)/shard_map/ppermute | solution.py:304
  85.7 12.9 %collective-permute-start.19 = (bf16[4096,640]{1,0:T(8,128)(2,1)}, bf16[4096,640]{1,0:T(8,128)(2,1)}, u32[]{:S(2)}, u32[]{:S(2)}) collective-permute-start(bf16[4096,640]{1,0:T(8,128)(2,1)} %collective-permute-done.14.refs_11_.refs_8_.refs_7_), channel_id=1, source_target_pairs={{0,32},{32,0},{1,33},{33,1},{2,34},{34,2},{3,35},{35,3},{4,36},{36... | collective-permute-start | bytes 15728648 | tf_op jit(solution)/shard_map/ppermute | solution.py:337
  90.0 33.3 %collective-permute-start.20 = (bf16[96,4096]{1,0:T(8,128)(2,1)}, bf16[96,4096]{1,0:T(8,128)(2,1)}, u32[]{:S(2)}, u32[]{:S(2)}) collective-permute-start(bf16[96,4096]{1,0:T(8,128)(2,1)} %get-tuple-element.45.refs_1_), channel_id=1, source_target_pairs={{0,2},{2,4},{4,6},{6,0},{1,3},{3,5},{5,7},{7,1},{8,10},{10,12},{12... | collective-permute-start | bytes 2359304 | tf_op jit(solution)/shard_map/ppermute | solution.py:303
  91.4 34.2 %collective-permute-start.21 = (bf16[96,4096]{1,0:T(8,128)(2,1)}, bf16[96,4096]{1,0:T(8,128)(2,1)}, u32[]{:S(2)}, u32[]{:S(2)}) collective-permute-start(bf16[96,4096]{1,0:T(8,128)(2,1)} %get-tuple-element.44.refs_0_), channel_id=1, source_target_pairs={{0,6},{2,0},{4,2},{6,4},{1,7},{3,1},{5,3},{7,5},{8,14},{10,8},{12,... | collective-permute-start | bytes 2359304 | tf_op jit(solution)/shard_map/ppermute | solution.py:304
  92.9 35.3 %collective-permute-start.22 = (bf16[96,4096]{1,0:T(8,128)(2,1)}, bf16[96,4096]{1,0:T(8,128)(2,1)}, u32[]{:S(2)}, u32[]{:S(2)}) collective-permute-start(bf16[96,4096]{1,0:T(8,128)(2,1)} %get-tuple-element.47.refs_3_), channel_id=1, source_target_pairs={{0,8},{8,16},{16,24},{24,0},{1,9},{9,17},{17,25},{25,1},{2,10},{10... | collective-permute-start | bytes 2359304 | tf_op jit(solution)/shard_map/ppermute | solution.py:303
  95.0 35.4 %collective-permute-start.23 = (bf16[96,4096]{1,0:T(8,128)(2,1)}, bf16[96,4096]{1,0:T(8,128)(2,1)}, u32[]{:S(2)}, u32[]{:S(2)}) collective-permute-start(bf16[96,4096]{1,0:T(8,128)(2,1)} %get-tuple-element.46.refs_2_), channel_id=1, source_target_pairs={{0,24},{8,0},{16,8},{24,16},{1,25},{9,1},{17,9},{25,17},{2,26},{10... | collective-permute-start | bytes 2359304 | tf_op jit(solution)/shard_map/ppermute | solution.py:304
  120.2 33.4 %collective-permute-start.24 = (bf16[96,4096]{1,0:T(8,128)(2,1)}, bf16[96,4096]{1,0:T(8,128)(2,1)S(1)}, u32[]{:S(2)}, u32[]{:S(2)}) collective-permute-start(bf16[96,4096]{1,0:T(8,128)(2,1)} %copy-done.2), channel_id=1, source_target_pairs={{0,2},{2,4},{4,6},{6,0},{1,3},{3,5},{5,7},{7,1},{8,10},{10,12},{12... | collective-permute-start | bytes 2359304 | tf_op jit(solution)/shard_map/ppermute | solution.py:303
  123.4 30.2 %collective-permute-start.25 = (bf16[96,4096]{1,0:T(8,128)(2,1)}, bf16[96,4096]{1,0:T(8,128)(2,1)S(1)}, u32[]{:S(2)}, u32[]{:S(2)}) collective-permute-start(bf16[96,4096]{1,0:T(8,128)(2,1)} %copy-done.3), channel_id=1, source_target_pairs={{0,6},{2,0},{4,2},{6,4},{1,7},{3,1},{5,3},{7,5},{8,14},{10,8},{12,... | collective-permute-start | bytes 2359304 | tf_op jit(solution)/shard_map/ppermute | solution.py:304
  125.6 28.0 %collective-permute-start.26 = (bf16[96,4096]{1,0:T(8,128)(2,1)}, bf16[96,4096]{1,0:T(8,128)(2,1)S(1)}, u32[]{:S(2)}, u32[]{:S(2)}) collective-permute-start(bf16[96,4096]{1,0:T(8,128)(2,1)} %copy-done.4), channel_id=1, source_target_pairs={{0,8},{8,16},{16,24},{24,0},{1,9},{9,17},{17,25},{25,1},{2,10},{10... | collective-permute-start | bytes 2359304 | tf_op jit(solution)/shard_map/ppermute | solution.py:303
  128.1 25.5 %collective-permute-start.27 = (bf16[96,4096]{1,0:T(8,128)(2,1)}, bf16[96,4096]{1,0:T(8,128)(2,1)S(1)}, u32[]{:S(2)}, u32[]{:S(2)}) collective-permute-start(bf16[96,4096]{1,0:T(8,128)(2,1)} %copy-done.5), channel_id=1, source_target_pairs={{0,24},{8,0},{16,8},{24,16},{1,25},{9,1},{17,9},{25,17},{2,26},{10... | collective-permute-start | bytes 2359304 | tf_op jit(solution)/shard_map/ppermute | solution.py:304
  (25 other events, 423.1 us)
Sparse Core Ops, SparseCore 0:
  14.0 47.3 all-gather.2
  63.5 68.1 all-gather.4

commit v4 on v3

--- a/solution.py
+++ b/solution.py
@@ -47,9 +47,9 @@
     out[...] = norm(query[...], gain)
 
 
-def norm_kernel(acts, gain, one, two, rest):
-    one[...] = norm(acts[HEAD:LEN, :], gain)
-    two[...] = norm(acts[LEN + HEAD:, :], gain)
+def norm_kernel(acts, gain, both, rest):
+    both[:CP, :] = norm(acts[HEAD:LEN, :], gain)
+    both[CP:, :] = norm(acts[LEN + HEAD:, :], gain)
     rest[0:HEAD, :] = norm(acts[:HEAD, :], gain)
     rest[HEAD:, :] = norm(acts[LEN:LEN + HEAD, :], gain)
 
@@ -120,7 +120,9 @@
     def pick(at):
         return jnp.where(qx == lane - at, weight, 0.0)
 
-    qload = pltpu.make_async_copy(queries, qs, qsem)
+    qloads = [
+        pltpu.make_async_copy(queries.at[pl.ds(64 * i, 64)], qs.at[pl.ds(64 * i, 64)], qsem.at[i]) for i in range(4)
+    ]
 
     def tiles(a, b):
         moves = []
@@ -146,14 +148,16 @@
         for c in tiles(first, second):
             c.wait()
 
-    qload.start()
+    for c in qloads:
+        c.start()
     if with_queries:
         start_tiles()
         for j in range(TILES):
             cols = slice(128 * j, 128 * (j + 1))
             heads[:, 256 * j:256 * j + 128] = jnp.where(straight, small[:, cols], small_first[:, cols])
             heads[:, 256 * j + 128:256 * j + 256] = jnp.where(straight, small_first[:, cols], small_second[:, cols])
-        qload.wait()
+        for c in qloads:
+            c.wait()
         wait_tiles()
         for c in xloads:
             c.start()
@@ -173,8 +177,7 @@
         for c in xloads:
             c.start()
         out[...] = jnp.zeros_like(out)
-        qload.wait()
-        for c in xloads:
+        for c in qloads + xloads:
             c.wait()
         start_tiles()
 
@@ -232,7 +235,7 @@
 SM = pl.BlockSpec(memory_space=pltpu.SMEM)
 
 
-def rows_call(rows, block, name, given, with_queries):
+def rows_call(rows, block, name, given, with_queries, space=HBM, limit=56):
     xin = [r[0] for r in rows]
     shapes = tuple((v.shape, found) for v, found in rows)
     n = len(rows)
@@ -244,7 +247,7 @@
     return pl.pallas_call(
         functools.partial(rows_kernel, shapes, block, with_queries),
         out_shape=tuple(out_shape),
-        in_specs=[HBM] * n + [SM] + [HBM] * 4 + [VM] * (3 if with_queries else 2),
+        in_specs=[space] * n + [SM] + [HBM] * 4 + [VM] * (3 if with_queries else 2),
         out_specs=(VM,) * len(out_shape),
         scratch_shapes=[
             pltpu.VMEM((total, D), BF16),
@@ -256,10 +259,10 @@
             pltpu.VMEM((runs, 128), F32),
             pltpu.VMEM((runs, 256), F32),
             pltpu.SemaphoreType.DMA((n,)),
-            pltpu.SemaphoreType.DMA,
+            pltpu.SemaphoreType.DMA((4,)),
             pltpu.SemaphoreType.DMA((TILES, 2)),
         ],
-        compiler_params=pltpu.CompilerParams(vmem_limit_bytes=56 * 2**20),
+        compiler_params=pltpu.CompilerParams(vmem_limit_bytes=limit * 2**20),
         cost_estimate=pl.CostEstimate(flops=1, bytes_accessed=1, transcendentals=0),
         name=name,
     )(*xin, *given)
@@ -306,13 +309,14 @@
     (query,) = norm_call(query_norm_kernel, (8,), query_acts[0], norm_gain)
     query_turned = turn(query)
     acts, _ = lax.optimization_barrier((train_acts[0], query))
-    one, two, rest = norm_call(norm_kernel, (CP, CP, 2 * HEAD), acts, norm_gain)
+    both, rest = norm_call(norm_kernel, (2 * CP, 2 * HEAD), acts, norm_gain)
     small = jnp.concatenate(
         [readout[0].astype(F32), jnp.zeros((RATE,), F32), lr_weight, jnp.zeros((127 - RATE,), F32)]
     ).reshape(1, FD + 128)
-    query_turned, one = lax.optimization_barrier((query_turned, one))
-    small_first, one, two, rest = turn(small), turn(one), turn(two), turn(rest)
-    weight_own, small_first, one, two, rest = lax.optimization_barrier((up_weight[0], small_first, one, two, rest))
+    query_turned, both = lax.optimization_barrier((query_turned, both))
+    both, rest, small_first = turn(both), turn(rest), turn(small)
+    weight_own, small_first, both, rest = lax.optimization_barrier((up_weight[0], small_first, both, rest))
+    one, two = both[:CP], both[CP:]
     weight_first = turn(weight_own)
     queries = lax.all_gather(query_turned, ("c", "x", "y"), axis=0, tiled=True)
     some = lax.all_gather(rest, ("x", "y"), axis=0, tiled=True)
@@ -324,10 +328,10 @@
     one_low, small_second = lax.optimization_barrier((one_low, swap(small_first)))
     moves = []
     for g in (0, 1):
-        moves += [(5 * g, 0, 2 * g, 0, CP), (5 * g + 1, 0, 2 * g, CP, CP), (5 * g + 2, 0, 2 * g + 1, 0, CP),
-                  (5 * g + 3, 0, 2 * g + 1, CP, 32), (5 * g + 4, 0, 2 * g + 1, CP + 32, 16)]
+        moves += [(4 * 2, CP * g, 2 * g, 0, CP), (4 * g, 0, 2 * g, CP, CP), (4 * g + 1, 0, 2 * g + 1, 0, CP),
+                  (4 * g + 2, 0, 2 * g + 1, CP, 32), (4 * g + 3, 0, 2 * g + 1, CP + 32, 16)]
     a1, b1, a2, b2 = copy_call(
-        (one, one_low, one_high, one_a, one_b, two, two_low, two_high, two_a, two_b), (2 * CP,) * 4, moves, "join_rows"
+        (one_low, one_high, one_a, one_b, two_low, two_high, two_a, two_b, both), (2 * CP,) * 4, moves, "join_rows"
     )
     a1_low, b1_high = low(a1, "y"), high(b1, "y")
     a2_low, b2_high = low(a2, "x"), high(b2, "x")
@@ -371,7 +375,7 @@
     (last,) = rows_call(
         [(a1_far, group((0, 3, near))), (b1_far, group((0, 3, far))),
          (a2_far, group((1, 3, near))), (b2_far, group((1, 3, far)))],
-        192, "last_rows", (*given, *kept), False,
+        192, "last_rows", (*given, *kept), False, ANY, 30,
     )
     sums = sums + more + last
     message = jnp.broadcast_to(sums.reshape(1, 16, 1, 128), (4, 16, 2, 128)).reshape(128, 128)

time: 198 us -> 195 us (0.985)
    ppermute x4 -> x3, waiting for transfers between devices: 8.61 us -> 8.81 us  [local(): both, rest, small_first = (turn(both), turn(rest), turn(small))]
  transfers between devices with their start and end apart: 30 -> 29, of which waited for: 13 -> 14; matrix products, arithmetic and copies ran while one was open for 1% -> 1% of each run, Pallas kernels for 25% -> 26%
where the time goes in v4:
time: 195 us; the launch traced here: 194 us
  Pallas kernels  66.1 us (34%)
  waiting for transfers between devices  48.3 us (25%)
  starting transfers between devices  42.5 us (22%)
  blocking collectives  18.1 us (9%)
  between operations  14.4 us (7%)
  local copies, waits for them, and re-layouts  4.25 us (2%)
    pallas_call x3, Pallas kernels, rows_call(): pl.pallas_call(functools.partial(rows_kernel, shapes, block, with_queries...  56.6 us
    ppermute x10, waiting for transfers between devices, local(): low = lambda v, axis: lax.ppermute(v, axis, ring(1))  25.6 us
    ppermute x10, starting transfers between devices, local(): high = lambda v, axis: lax.ppermute(v, axis, ring(-1))  18.3 us
    all_to_all x1, blocking collectives, local(): lax.all_to_all(message, ('zh', 'c', 'x', 'y', 'zl'), split_axis=0, concat...  18.1 us
    ppermute x10, starting transfers between devices, local(): low = lambda v, axis: lax.ppermute(v, axis, ring(1))  10.2 us
    ppermute x3, waiting for transfers between devices, local(): both, rest, small_first = (turn(both), turn(rest), turn(small))  8.81 us
    ppermute x1, waiting for transfers between devices, local(): weight_first = turn(weight_own)  5.37 us
    ppermute x10, waiting for transfers between devices, local(): high = lambda v, axis: lax.ppermute(v, axis, ring(-1))  5.04 us
  transfers between devices with their start and end apart: 29, of which 14 were waited for; matrix products, arithmetic and copies ran while one was open for 1% of the time, Pallas kernels for 26%

profile of v4, /device:TPU:1, one launch (start us, length us, event | category | flops | bytes accessed | tf_op | source)
XLA Modules:
  0.0 194.4 jit_solution(8391090111143591284)
XLA Ops:
  6.5 1.6 norm_rows.2
  8.2 2.5 %collective-permute-start.1 = (bf16[8,4096]{1,0:T(8,128)(2,1)}, bf16[8,4096]{1,0:T(8,128)(2,1)S(1)}, u32[]{:S(2)}, u32[]{:S(2)}) collective-permute-start(bf16[8,4096]{1,0:T(8,128)(2,1)} %norm_rows.2), channel_id=1, source_target_pairs={{0,32},{32,33},{33,1},{1,0},{2,34},{34,35},{35,3},{3,2},{4,36},{36... | collective-permute-start | bytes 196616 | tf_op jit(solution)/shard_map/ppermute | solution.py:310
  10.6 2.8 %norm_rows.3 = (bf16[96,4096]{1,0:T(8,128)(2,1)}, bf16[32,4096]{1,0:T(8,128)(2,1)}) custom-call(bf16[128,4096]{1,0:T(8,128)(2,1)} %bitcast.16, bf16[1,4096]{1,0:T(2,128)(2,1)} %gain.3), custom_call_target="tpu_custom_call" | custom-call | flops 2097152 | bytes 2097152 | tf_op jit(solution)/shard_map/norm_rows/pallas_call | solution.py:58
  16.4 1.7 collective-permute-start
  18.1 8.8 %collective-permute-done.refs_14_ = f32[1,768]{1,0:T(1,128)S(1)} collective-permute-done((f32[1,768]{1,0:T(1,128)S(1)}, f32[1,768]{1,0:T(1,128)S(1)}, u32[]{:S(2)}, u32[]{:S(2)}) %collective-permute-start) | collective-permute-done | bytes 3104 | tf_op jit(solution)/shard_map/ppermute | solution.py:317
  26.9 1.9 collective-permute-start.13
  31.5 1.5 collective-permute-start.6
  34.4 5.5 %collective-permute-done.4.refs_0_ = bf16[48,4096]{1,0:T(8,128)(2,1)S(1)} collective-permute-done((bf16[48,4096]{1,0:T(8,128)(2,1)S(1)}, bf16[48,4096]{1,0:T(8,128)(2,1)S(1)}, u32[]{:S(2)}, u32[]{:S(2)}) %collective-permute-start.4) | collective-permute-done | bytes 393248 | tf_op jit(solution)/shard_map/ppermute | solution.py:306
  41.6 2.9 %collective-permute-start.5 = (f32[1,768]{1,0:T(1,128)S(1)}, f32[1,768]{1,0:T(1,128)S(1)}, u32[]{:S(2)}, u32[]{:S(2)}) collective-permute-start(f32[1,768]{1,0:T(1,128)S(1)} %collective-permute-done.refs_14_), channel_id=1, source_target_pairs={{0,32},{32,0},{1,33},{33,1},{2,34},{34,2},{3,35},{35,3},{4,36},{36... | collective-permute-start | bytes 9224 | tf_op jit(solution)/shard_map/ppermute | solution.py:328
  44.5 2.7 %collective-permute-start.8 = (bf16[16,4096]{1,0:T(8,128)(2,1)S(1)}, bf16[16,4096]{1,0:T(8,128)(2,1)S(1)}, u32[]{:S(2)}, u32[]{:S(2)}) collective-permute-start(bf16[16,4096]{1,0:T(8,128)(2,1)S(1)} %slice.25), channel_id=1, source_target_pairs={{0,24},{8,0},{16,8},{24,16},{1,25},{9,1},{17,9},{25,17},{2,26},{10... | collective-permute-start | bytes 393224 | tf_op jit(solution)/shard_map/ppermute | solution.py:307
  47.2 1.4 collective-permute-start.12
  48.7 1.8 collective-permute-done.8.refs_3_
  50.4 1.9 collective-permute-done.12.refs_7_
  53.9 3.6 %join_rows.1 = (bf16[96,4096]{1,0:T(8,128)(2,1)}, bf16[96,4096]{1,0:T(8,128)(2,1)}, bf16[96,4096]{1,0:T(8,128)(2,1)}, bf16[96,4096]{1,0:T(8,128)(2,1)}) custom-call(bf16[48,4096]{1,0:T(8,128)(2,1)} %copy-done.5, bf16[48,4096]{1,0:T(8,128)(2,1)} %copy-done.10, bf16[32,4096]{1,0:T(8,128)(2,1)} %copy-done.12, bf16[16,4096]{1,0:T(8,128)(2,1)} %copy-done.15, ...), custom_call_target="tpu_custom_call" | custom-call | bytes 6291456 | tf_op jit(solution)/shard_map/join_rows/pallas_call | solution.py:81
  57.5 1.5 collective-permute-start.14
  60.5 2.4 %collective-permute-start.17 = (bf16[96,4096]{1,0:T(8,128)(2,1)}, bf16[96,4096]{1,0:T(8,128)(2,1)}, u32[]{:S(2)}, u32[]{:S(2)}) collective-permute-start(bf16[96,4096]{1,0:T(8,128)(2,1)} %get-tuple-element.43.refs_3_), channel_id=1, source_target_pairs={{0,24},{8,0},{16,8},{24,16},{1,25},{9,1},{17,9},{25,17},{2,26},{10... | collective-permute-start | bytes 2359304 | tf_op jit(solution)/shard_map/ppermute | solution.py:307
  62.9 13.6 %collective-permute-done.14.refs_4_ = bf16[96,4096]{1,0:T(8,128)(2,1)S(1)} collective-permute-done((bf16[96,4096]{1,0:T(8,128)(2,1)}, bf16[96,4096]{1,0:T(8,128)(2,1)S(1)}, u32[]{:S(2)}, u32[]{:S(2)}) %collective-permute-start.14) | collective-permute-done | bytes 786464 | tf_op jit(solution)/shard_map/ppermute | solution.py:306
  77.6 2.8 %collective-permute-done.16.refs_6_ = bf16[96,4096]{1,0:T(8,128)(2,1)S(1)} collective-permute-done((bf16[96,4096]{1,0:T(8,128)(2,1)}, bf16[96,4096]{1,0:T(8,128)(2,1)S(1)}, u32[]{:S(2)}, u32[]{:S(2)}) %collective-permute-start.16) | collective-permute-done | bytes 786464 | tf_op jit(solution)/shard_map/ppermute | solution.py:306
  80.4 5.4 %collective-permute-done.13.refs_11_.refs_8_.refs_7_ = bf16[4096,640]{1,0:T(8,128)(2,1)} collective-permute-done((bf16[4096,640]{1,0:T(8,128)(2,1)}, bf16[4096,640]{1,0:T(8,128)(2,1)}, u32[]{:S(2)}, u32[]{:S(2)}) %collective-permute-start.13) | collective-permute-done | bytes 5242912 | tf_op jit(solution)/shard_map/ppermute | solution.py:320
  85.8 4.2 %collective-permute-start.18 = (bf16[4096,640]{1,0:T(8,128)(2,1)}, bf16[4096,640]{1,0:T(8,128)(2,1)}, u32[]{:S(2)}, u32[]{:S(2)}) collective-permute-start(bf16[4096,640]{1,0:T(8,128)(2,1)} %collective-permute-done.13.refs_11_.refs_8_.refs_7_), channel_id=1, source_target_pairs={{0,32},{32,0},{1,33},{33,1},{2,34},{34,2},{3,35},{35,3},{4,36},{36... | collective-permute-start | bytes 15728648 | tf_op jit(solution)/shard_map/ppermute | solution.py:341
  91.4 1.4 collective-permute-start.20
  95.0 1.5 collective-permute-start.22
  96.5 2.2 %collective-permute-done.18.refs_12_.refs_9_.refs_8_ = bf16[4096,640]{1,0:T(8,128)(2,1)} collective-permute-done((bf16[4096,640]{1,0:T(8,128)(2,1)}, bf16[4096,640]{1,0:T(8,128)(2,1)}, u32[]{:S(2)}, u32[]{:S(2)}) %collective-permute-start.18) | collective-permute-done | bytes 5242912 | tf_op jit(solution)/shard_map/ppermute | solution.py:341
  98.7 21.6 %first_rows.1 = (f32[16,128]{1,0:T(8,128)}, bf16[256,1280]{1,0:T(8,128)(2,1)}, f32[1,1280]{1,0:T(1,128)}) custom-call(bf16[96,4096]{1,0:T(8,128)(2,1)} %get-tuple-element.40.refs_0_, bf16[96,4096]{1,0:T(8,128)(2,1)} %get-tuple-element.41.refs_1_, bf16[96,4096]{1,0:T(8,128)(2,1)} %get-tuple-element.42.refs_2_, bf16[96,4096]{1,0:T(8,128)(2,1)} %get-tuple-element.43.refs_3_, ...), custom_call_target="tpu_custom_call" | custom-call | flops 1 | bytes 1 | tf_op jit(solution)/shard_map/first_rows/pallas_call | solution.py:247
  120.3 1.5 collective-permute-start.23
  121.7 1.5 collective-permute-done.19.refs_0_
  123.2 2.2 %collective-permute-start.24 = (bf16[96,4096]{1,0:T(8,128)(2,1)}, bf16[96,4096]{1,0:T(8,128)(2,1)}, u32[]{:S(2)}, u32[]{:S(2)}) collective-permute-start(bf16[96,4096]{1,0:T(8,128)(2,1)} %copy-done.8), channel_id=1, source_target_pairs={{0,6},{2,0},{4,2},{6,4},{1,7},{3,1},{5,3},{7,5},{8,14},{10,8},{12,... | collective-permute-start | bytes 2359304 | tf_op jit(solution)/shard_map/ppermute | solution.py:307
  127.8 2.4 %collective-permute-start.26 = (bf16[96,4096]{1,0:T(8,128)(2,1)}, bf16[96,4096]{1,0:T(8,128)(2,1)}, u32[]{:S(2)}, u32[]{:S(2)}) collective-permute-start(bf16[96,4096]{1,0:T(8,128)(2,1)} %collective-permute-done.17.refs_7_), channel_id=1, source_target_pairs={{0,24},{8,0},{16,8},{24,16},{1,25},{9,1},{17,9},{25,17},{2,26},{10... | collective-permute-start | bytes 2359304 | tf_op jit(solution)/shard_map/ppermute | solution.py:307
  131.6 22.7 %next_rows.1 = f32[16,128]{1,0:T(8,128)} custom-call(bf16[96,4096]{1,0:T(8,128)(2,1)} %collective-permute-done.19.refs_0_, bf16[96,4096]{1,0:T(8,128)(2,1)} %collective-permute-done.20.refs_1_, bf16[96,4096]{1,0:T(8,128)(2,1)} %collective-permute-done.21.refs_2_, bf16[96,4096]{1,0:T(8,128)(2,1)} %collective-permute-done.22.refs_3_, ...), custom_call_target="tpu_custom_call" | custom-call | flops 1 | bytes 1 | tf_op jit(solution)/shard_map/next_rows/pallas_call | solution.py:247
  155.5 12.4 %last_rows.1 = f32[16,128]{1,0:T(8,128)S(1)} custom-call(bf16[96,4096]{1,0:T(8,128)(2,1)} %collective-permute-done.23.refs_0_, bf16[96,4096]{1,0:T(8,128)(2,1)} %collective-permute-done.24.refs_1_, bf16[96,4096]{1,0:T(8,128)(2,1)} %collective-permute-done.25.refs_2_, bf16[96,4096]{1,0:T(8,128)(2,1)} %collective-permute-done.26.refs_3_, s32[72]{0:T(128)S(1)} %copy-done.3, ...), custom_call_target="tpu_custom_call" | custom-call | flops 1 | bytes 1 | tf_op jit(solution)/shard_map/last_rows/pallas_call | solution.py:247
  168.0 18.1 %all_to_all.11 = f32[128,1,128]{2,1,0:T(1,128)} all-to-all(f32[128,1,128]{2,1,0:T(1,128)S(1)} %bitcast.18), channel_id=1, replica_groups=mesh['zh'=2,'c'=2,'x'=4,'y'=4,'zl'=2] {'zh','c','x','y','zl'}, dimensions={0} | all-to-all | bytes 131072 | tf_op jit(solution)/shard_map/all_to_all | solution.py:382
  186.1 1.5 influence.1
  (107 shorter events, 20.6 us)
Async XLA Ops:
  6.5 87.5 %copy-start.24 = (s32[2,2]{1,0:T(2,128)S(1)}, s32[2,2]{1,0:T(2,128)}, u32[]{:S(2)}) copy-start(s32[2,2]{1,0:T(2,128)} %param.11) | copy-start | bytes 52
  6.5 87.6 %copy-start.23 = (s32[32,2]{0,1:T(2,128)S(1)}, s32[32,2]{0,1:T(2,128)}, u32[]{:S(2)}) copy-start(s32[32,2]{0,1:T(2,128)} %param.9) | copy-start | bytes 772
  6.5 89.9 %all-gather.3.cloned.1.call-start = ((), (), s32[]{:S(2)}) async-start(), calls=%async_computation.1 | async-start | bytes 2162688 | tf_op jit(solution)/shard_map/all_gather | solution.py:321
  8.2 5.2 %collective-permute-start.1 = (bf16[8,4096]{1,0:T(8,128)(2,1)}, bf16[8,4096]{1,0:T(8,128)(2,1)S(1)}, u32[]{:S(2)}, u32[]{:S(2)}) collective-permute-start(bf16[8,4096]{1,0:T(8,128)(2,1)} %norm_rows.2), channel_id=1, source_target_pairs={{0,32},{32,33},{33,1},{1,0},{2,34},{34,35},{35,3},{3,2},{4,36},{36... | collective-permute-start | bytes 196616 | tf_op jit(solution)/shard_map/ppermute | solution.py:310
  14.0 117.6 %all-gather.5.cloned.1.call-start = ((), (), s32[]{:S(2)}) async-start(), calls=%async_computation.2 | async-start | bytes 4456448 | tf_op jit(solution)/shard_map/all_gather | solution.py:322
  14.1 12.8 %collective-permute-start.2 = (bf16[96,4096]{1,0:T(8,128)(2,1)}, bf16[96,4096]{1,0:T(8,128)(2,1)S(1)}, u32[]{:S(2)}, u32[]{:S(2)}) collective-permute-start(bf16[96,4096]{1,0:T(8,128)(2,1)} %get-tuple-element.35), channel_id=1, source_target_pairs={{0,32},{32,33},{33,1},{1,0},{2,34},{34,35},{35,3},{3,2},{4,36},{36... | collective-permute-start | bytes 2359304 | tf_op jit(solution)/shard_map/ppermute | solution.py:317
  14.8 12.1 %collective-permute-start.3 = (bf16[32,4096]{1,0:T(8,128)(2,1)}, bf16[32,4096]{1,0:T(8,128)(2,1)S(1)}, u32[]{:S(2)}, u32[]{:S(2)}) collective-permute-start(bf16[32,4096]{1,0:T(8,128)(2,1)} %get-tuple-element.36), channel_id=1, source_target_pairs={{0,32},{32,33},{33,1},{1,0},{2,34},{34,35},{35,3},{3,2},{4,36},{36... | collective-permute-start | bytes 786440 | tf_op jit(solution)/shard_map/ppermute | solution.py:317
  16.4 82.3 %copy-start.19 = (f32[1,768]{1,0:T(1,128)}, f32[1,768]{1,0:T(1,128)S(1)}, u32[]{:S(2)}) copy-start(f32[1,768]{1,0:T(1,128)S(1)} %reshape.21.refs_13_) | copy-start | bytes 9220
  16.4 10.5 %collective-permute-start = (f32[1,768]{1,0:T(1,128)S(1)}, f32[1,768]{1,0:T(1,128)S(1)}, u32[]{:S(2)}, u32[]{:S(2)}) collective-permute-start(f32[1,768]{1,0:T(1,128)S(1)} %reshape.21.refs_13_), channel_id=1, source_target_pairs={{0,32},{32,33},{33,1},{1,0},{2,34},{34,35},{35,3},{3,2},{4,36},{36... | collective-permute-start | bytes 9224 | tf_op jit(solution)/shard_map/ppermute | solution.py:317
  26.9 58.9 %collective-permute-start.13 = (bf16[4096,640]{1,0:T(8,128)(2,1)}, bf16[4096,640]{1,0:T(8,128)(2,1)}, u32[]{:S(2)}, u32[]{:S(2)}) collective-permute-start(bf16[4096,640]{1,0:T(8,128)(2,1)} %bitcast.10), channel_id=1, source_target_pairs={{0,32},{32,33},{33,1},{1,0},{2,34},{34,35},{35,3},{3,2},{4,36},{36... | collective-permute-start | bytes 15728648 | tf_op jit(solution)/shard_map/ppermute | solution.py:320
  28.9 11.0 %collective-permute-start.4 = (bf16[48,4096]{1,0:T(8,128)(2,1)S(1)}, bf16[48,4096]{1,0:T(8,128)(2,1)S(1)}, u32[]{:S(2)}, u32[]{:S(2)}) collective-permute-start(bf16[48,4096]{1,0:T(8,128)(2,1)S(1)} %get-tuple-element.62), channel_id=1, source_target_pairs={{0,8},{8,16},{16,24},{24,0},{1,9},{9,17},{17,25},{25,1},{2,10},{10... | collective-permute-start | bytes 1179656 | tf_op jit(solution)/shard_map/ppermute | solution.py:306
  30.2 11.1 %collective-permute-start.9 = (bf16[48,4096]{1,0:T(8,128)(2,1)S(1)}, bf16[48,4096]{1,0:T(8,128)(2,1)S(1)}, u32[]{:S(2)}, u32[]{:S(2)}) collective-permute-start(bf16[48,4096]{1,0:T(8,128)(2,1)S(1)} %get-tuple-element.61), channel_id=1, source_target_pairs={{0,2},{2,4},{4,6},{6,0},{1,3},{3,5},{5,7},{7,1},{8,10},{10,12},{12... | collective-permute-start | bytes 1179656 | tf_op jit(solution)/shard_map/ppermute | solution.py:306
  31.5 10.1 %collective-permute-start.6 = (bf16[48,4096]{1,0:T(8,128)(2,1)S(1)}, bf16[48,4096]{1,0:T(8,128)(2,1)S(1)}, u32[]{:S(2)}, u32[]{:S(2)}) collective-permute-start(bf16[48,4096]{1,0:T(8,128)(2,1)S(1)} %get-tuple-element.62), channel_id=1, source_target_pairs={{0,24},{8,0},{16,8},{24,16},{1,25},{9,1},{17,9},{25,17},{2,26},{10... | collective-permute-start | bytes 1179656 | tf_op jit(solution)/shard_map/ppermute | solution.py:307
  32.9 11.5 %collective-permute-start.10 = (bf16[48,4096]{1,0:T(8,128)(2,1)S(1)}, bf16[48,4096]{1,0:T(8,128)(2,1)S(1)}, u32[]{:S(2)}, u32[]{:S(2)}) collective-permute-start(bf16[48,4096]{1,0:T(8,128)(2,1)S(1)} %get-tuple-element.61), channel_id=1, source_target_pairs={{0,6},{2,0},{4,2},{6,4},{1,7},{3,1},{5,3},{7,5},{8,14},{10,8},{12,... | collective-permute-start | bytes 1179656 | tf_op jit(solution)/shard_map/ppermute | solution.py:307
  40.0 12.4 %collective-permute-start.7 = (bf16[32,4096]{1,0:T(8,128)(2,1)S(1)}, bf16[32,4096]{1,0:T(8,128)(2,1)S(1)}, u32[]{:S(2)}, u32[]{:S(2)}) collective-permute-start(bf16[32,4096]{1,0:T(8,128)(2,1)S(1)} %slice.24), channel_id=1, source_target_pairs={{0,8},{8,16},{16,24},{24,0},{1,9},{9,17},{17,25},{25,1},{2,10},{10... | collective-permute-start | bytes 786440 | tf_op jit(solution)/shard_map/ppermute | solution.py:306
  41.3 11.1 %collective-permute-start.11 = (bf16[32,4096]{1,0:T(8,128)(2,1)S(1)}, bf16[32,4096]{1,0:T(8,128)(2,1)S(1)}, u32[]{:S(2)}, u32[]{:S(2)}) collective-permute-start(bf16[32,4096]{1,0:T(8,128)(2,1)S(1)} %slice.26), channel_id=1, source_target_pairs={{0,2},{2,4},{4,6},{6,0},{1,3},{3,5},{5,7},{7,1},{8,10},{10,12},{12... | collective-permute-start | bytes 786440 | tf_op jit(solution)/shard_map/ppermute | solution.py:306
  41.6 5.6 %collective-permute-start.5 = (f32[1,768]{1,0:T(1,128)S(1)}, f32[1,768]{1,0:T(1,128)S(1)}, u32[]{:S(2)}, u32[]{:S(2)}) collective-permute-start(f32[1,768]{1,0:T(1,128)S(1)} %collective-permute-done.refs_14_), channel_id=1, source_target_pairs={{0,32},{32,0},{1,33},{33,1},{2,34},{34,2},{3,35},{35,3},{4,36},{36... | collective-permute-start | bytes 9224 | tf_op jit(solution)/shard_map/ppermute | solution.py:328
  44.5 5.9 %collective-permute-start.8 = (bf16[16,4096]{1,0:T(8,128)(2,1)S(1)}, bf16[16,4096]{1,0:T(8,128)(2,1)S(1)}, u32[]{:S(2)}, u32[]{:S(2)}) collective-permute-start(bf16[16,4096]{1,0:T(8,128)(2,1)S(1)} %slice.25), channel_id=1, source_target_pairs={{0,24},{8,0},{16,8},{24,16},{1,25},{9,1},{17,9},{25,17},{2,26},{10... | collective-permute-start | bytes 393224 | tf_op jit(solution)/shard_map/ppermute | solution.py:307
  47.2 5.2 %collective-permute-start.12 = (bf16[16,4096]{1,0:T(8,128)(2,1)S(1)}, bf16[16,4096]{1,0:T(8,128)(2,1)S(1)}, u32[]{:S(2)}, u32[]{:S(2)}) collective-permute-start(bf16[16,4096]{1,0:T(8,128)(2,1)S(1)} %slice.27), channel_id=1, source_target_pairs={{0,6},{2,0},{4,2},{6,4},{1,7},{3,1},{5,3},{7,5},{8,14},{10,8},{12,... | collective-permute-start | bytes 393224 | tf_op jit(solution)/shard_map/ppermute | solution.py:307
  57.5 19.1 %collective-permute-start.14 = (bf16[96,4096]{1,0:T(8,128)(2,1)}, bf16[96,4096]{1,0:T(8,128)(2,1)S(1)}, u32[]{:S(2)}, u32[]{:S(2)}) collective-permute-start(bf16[96,4096]{1,0:T(8,128)(2,1)} %get-tuple-element.40.refs_0_), channel_id=1, source_target_pairs={{0,2},{2,4},{4,6},{6,0},{1,3},{3,5},{5,7},{7,1},{8,10},{10,12},{12... | collective-permute-start | bytes 2359304 | tf_op jit(solution)/shard_map/ppermute | solution.py:306
  58.9 18.7 %collective-permute-start.15 = (bf16[96,4096]{1,0:T(8,128)(2,1)}, bf16[96,4096]{1,0:T(8,128)(2,1)S(1)}, u32[]{:S(2)}, u32[]{:S(2)}) collective-permute-start(bf16[96,4096]{1,0:T(8,128)(2,1)} %get-tuple-element.41.refs_1_), channel_id=1, source_target_pairs={{0,6},{2,0},{4,2},{6,4},{1,7},{3,1},{5,3},{7,5},{8,14},{10,8},{12,... | collective-permute-start | bytes 2359304 | tf_op jit(solution)/shard_map/ppermute | solution.py:307
  60.2 20.2 %collective-permute-start.16 = (bf16[96,4096]{1,0:T(8,128)(2,1)}, bf16[96,4096]{1,0:T(8,128)(2,1)S(1)}, u32[]{:S(2)}, u32[]{:S(2)}) collective-permute-start(bf16[96,4096]{1,0:T(8,128)(2,1)} %get-tuple-element.42.refs_2_), channel_id=1, source_target_pairs={{0,8},{8,16},{16,24},{24,0},{1,9},{9,17},{17,25},{25,1},{2,10},{10... | collective-permute-start | bytes 2359304 | tf_op jit(solution)/shard_map/ppermute | solution.py:306
  60.5 19.9 %collective-permute-start.17 = (bf16[96,4096]{1,0:T(8,128)(2,1)}, bf16[96,4096]{1,0:T(8,128)(2,1)}, u32[]{:S(2)}, u32[]{:S(2)}) collective-permute-start(bf16[96,4096]{1,0:T(8,128)(2,1)} %get-tuple-element.43.refs_3_), channel_id=1, source_target_pairs={{0,24},{8,0},{16,8},{24,16},{1,25},{9,1},{17,9},{25,17},{2,26},{10... | collective-permute-start | bytes 2359304 | tf_op jit(solution)/shard_map/ppermute | solution.py:307
  85.8 12.8 %collective-permute-start.18 = (bf16[4096,640]{1,0:T(8,128)(2,1)}, bf16[4096,640]{1,0:T(8,128)(2,1)}, u32[]{:S(2)}, u32[]{:S(2)}) collective-permute-start(bf16[4096,640]{1,0:T(8,128)(2,1)} %collective-permute-done.13.refs_11_.refs_8_.refs_7_), channel_id=1, source_target_pairs={{0,32},{32,0},{1,33},{33,1},{2,34},{34,2},{3,35},{35,3},{4,36},{36... | collective-permute-start | bytes 15728648 | tf_op jit(solution)/shard_map/ppermute | solution.py:341
  90.0 33.2 %collective-permute-start.19 = (bf16[96,4096]{1,0:T(8,128)(2,1)}, bf16[96,4096]{1,0:T(8,128)(2,1)}, u32[]{:S(2)}, u32[]{:S(2)}) collective-permute-start(bf16[96,4096]{1,0:T(8,128)(2,1)} %get-tuple-element.41.refs_1_), channel_id=1, source_target_pairs={{0,2},{2,4},{4,6},{6,0},{1,3},{3,5},{5,7},{7,1},{8,10},{10,12},{12... | collective-permute-start | bytes 2359304 | tf_op jit(solution)/shard_map/ppermute | solution.py:306
  91.4 34.1 %collective-permute-start.20 = (bf16[96,4096]{1,0:T(8,128)(2,1)}, bf16[96,4096]{1,0:T(8,128)(2,1)}, u32[]{:S(2)}, u32[]{:S(2)}) collective-permute-start(bf16[96,4096]{1,0:T(8,128)(2,1)} %get-tuple-element.40.refs_0_), channel_id=1, source_target_pairs={{0,6},{2,0},{4,2},{6,4},{1,7},{3,1},{5,3},{7,5},{8,14},{10,8},{12,... | collective-permute-start | bytes 2359304 | tf_op jit(solution)/shard_map/ppermute | solution.py:307
  92.8 34.9 %collective-permute-start.21 = (bf16[96,4096]{1,0:T(8,128)(2,1)}, bf16[96,4096]{1,0:T(8,128)(2,1)}, u32[]{:S(2)}, u32[]{:S(2)}) collective-permute-start(bf16[96,4096]{1,0:T(8,128)(2,1)} %get-tuple-element.43.refs_3_), channel_id=1, source_target_pairs={{0,8},{8,16},{16,24},{24,0},{1,9},{9,17},{17,25},{25,1},{2,10},{10... | collective-permute-start | bytes 2359304 | tf_op jit(solution)/shard_map/ppermute | solution.py:306
  95.0 35.4 %collective-permute-start.22 = (bf16[96,4096]{1,0:T(8,128)(2,1)}, bf16[96,4096]{1,0:T(8,128)(2,1)}, u32[]{:S(2)}, u32[]{:S(2)}) collective-permute-start(bf16[96,4096]{1,0:T(8,128)(2,1)} %get-tuple-element.42.refs_2_), channel_id=1, source_target_pairs={{0,24},{8,0},{16,8},{24,16},{1,25},{9,1},{17,9},{25,17},{2,26},{10... | collective-permute-start | bytes 2359304 | tf_op jit(solution)/shard_map/ppermute | solution.py:307
  120.3 34.1 %collective-permute-start.23 = (bf16[96,4096]{1,0:T(8,128)(2,1)}, bf16[96,4096]{1,0:T(8,128)(2,1)}, u32[]{:S(2)}, u32[]{:S(2)}) collective-permute-start(bf16[96,4096]{1,0:T(8,128)(2,1)} %copy-done.7), channel_id=1, source_target_pairs={{0,2},{2,4},{4,6},{6,0},{1,3},{3,5},{5,7},{7,1},{8,10},{10,12},{12... | collective-permute-start | bytes 2359304 | tf_op jit(solution)/shard_map/ppermute | solution.py:306
  123.2 31.1 %collective-permute-start.24 = (bf16[96,4096]{1,0:T(8,128)(2,1)}, bf16[96,4096]{1,0:T(8,128)(2,1)}, u32[]{:S(2)}, u32[]{:S(2)}) collective-permute-start(bf16[96,4096]{1,0:T(8,128)(2,1)} %copy-done.8), channel_id=1, source_target_pairs={{0,6},{2,0},{4,2},{6,4},{1,7},{3,1},{5,3},{7,5},{8,14},{10,8},{12,... | collective-permute-start | bytes 2359304 | tf_op jit(solution)/shard_map/ppermute | solution.py:307
  125.5 28.9 %collective-permute-start.25 = (bf16[96,4096]{1,0:T(8,128)(2,1)}, bf16[96,4096]{1,0:T(8,128)(2,1)}, u32[]{:S(2)}, u32[]{:S(2)}) collective-permute-start(bf16[96,4096]{1,0:T(8,128)(2,1)} %copy-done.9), channel_id=1, source_target_pairs={{0,8},{8,16},{16,24},{24,0},{1,9},{9,17},{17,25},{25,1},{2,10},{10... | collective-permute-start | bytes 2359304 | tf_op jit(solution)/shard_map/ppermute | solution.py:306
  127.8 26.6 %collective-permute-start.26 = (bf16[96,4096]{1,0:T(8,128)(2,1)}, bf16[96,4096]{1,0:T(8,128)(2,1)}, u32[]{:S(2)}, u32[]{:S(2)}) collective-permute-start(bf16[96,4096]{1,0:T(8,128)(2,1)} %collective-permute-done.17.refs_7_), channel_id=1, source_target_pairs={{0,24},{8,0},{16,8},{24,16},{1,25},{9,1},{17,9},{25,17},{2,26},{10... | collective-permute-start | bytes 2359304 | tf_op jit(solution)/shard_map/ppermute | solution.py:307
  (24 other events, 455.9 us)
Sparse Core Ops, SparseCore 0:
  14.1 47.1 all-gather.2
  63.5 68.0 all-gather.4

commit v5 on v4

--- a/solution.py
+++ b/solution.py
@@ -370,7 +370,7 @@
     (more,) = rows_call(
         [(b1_low, group((0, 1, far))), (a1_high, group((0, 2, near))),
          (b2_low, group((1, 1, far))), (a2_high, group((1, 2, near))), (some, gathered_runs)],
-        224, "next_rows", (*given, *kept), False,
+        224, "next_rows", (*given, *kept), False, HBM, 48,
     )
     (last,) = rows_call(
         [(a1_far, group((0, 3, near))), (b1_far, group((0, 3, far))),

time: 195 us -> 194 us (level)
    unnamed x55 -> x47, local copies, waits for them, and re-layouts: 3.25 us -> 3.94 us
  transfers between devices with their start and end apart: 29 -> 29, of which waited for: 14 -> 13; matrix products, arithmetic and copies ran while one was open for 1% -> 1% of each run, Pallas kernels for 26% -> 25%
where the time goes in v5:
time: 194 us; the launch traced here: 193 us
  Pallas kernels  64.2 us (33%)
  waiting for transfers between devices  48.3 us (25%)
  starting transfers between devices  42.6 us (22%)
  blocking collectives  18 us (9%)
  between operations  14.4 us (7%)
  local copies, waits for them, and re-layouts  4.9 us (3%)
    pallas_call x3, Pallas kernels, rows_call(): pl.pallas_call(functools.partial(rows_kernel, shapes, block, with_queries...  54.7 us
    ppermute x10, waiting for transfers between devices, local(): low = lambda v, axis: lax.ppermute(v, axis, ring(1))  25.7 us
    ppermute x10, starting transfers between devices, local(): high = lambda v, axis: lax.ppermute(v, axis, ring(-1))  18.3 us
    all_to_all x1, blocking collectives, local(): lax.all_to_all(message, ('zh', 'c', 'x', 'y', 'zl'), split_axis=0, concat...  18 us
    ppermute x10, starting transfers between devices, local(): low = lambda v, axis: lax.ppermute(v, axis, ring(1))  10.2 us
    ppermute x3, waiting for transfers between devices, local(): both, rest, small_first = (turn(both), turn(rest), turn(small))  8.79 us
    ppermute x1, waiting for transfers between devices, local(): weight_first = turn(weight_own)  5.56 us
    ppermute x10, waiting for transfers between devices, local(): high = lambda v, axis: lax.ppermute(v, axis, ring(-1))  4.68 us
  transfers between devices with their start and end apart: 29, of which 13 were waited for; matrix products, arithmetic and copies ran while one was open for 1% of the time, Pallas kernels for 25%

profile of v5, /device:TPU:1, one launch (start us, length us, event | category | flops | bytes accessed | tf_op | source)
XLA Modules:
  0.0 193.1 jit_solution(12506717675343007896)
XLA Ops:
  6.5 1.6 norm_rows.2
  8.2 2.5 %collective-permute-start.1 = (bf16[8,4096]{1,0:T(8,128)(2,1)}, bf16[8,4096]{1,0:T(8,128)(2,1)S(1)}, u32[]{:S(2)}, u32[]{:S(2)}) collective-permute-start(bf16[8,4096]{1,0:T(8,128)(2,1)} %norm_rows.2), channel_id=1, source_target_pairs={{0,32},{32,33},{33,1},{1,0},{2,34},{34,35},{35,3},{3,2},{4,36},{36... | collective-permute-start | bytes 196616 | tf_op jit(solution)/shard_map/ppermute | solution.py:310
  10.6 2.7 %norm_rows.3 = (bf16[96,4096]{1,0:T(8,128)(2,1)}, bf16[32,4096]{1,0:T(8,128)(2,1)}) custom-call(bf16[128,4096]{1,0:T(8,128)(2,1)} %bitcast.16, bf16[1,4096]{1,0:T(2,128)(2,1)} %gain.3), custom_call_target="tpu_custom_call" | custom-call | flops 2097152 | bytes 2097152 | tf_op jit(solution)/shard_map/norm_rows/pallas_call | solution.py:58
  16.4 1.7 collective-permute-start
  18.1 8.8 %collective-permute-done.refs_14_ = f32[1,768]{1,0:T(1,128)S(1)} collective-permute-done((f32[1,768]{1,0:T(1,128)S(1)}, f32[1,768]{1,0:T(1,128)S(1)}, u32[]{:S(2)}, u32[]{:S(2)}) %collective-permute-start) | collective-permute-done | bytes 3104 | tf_op jit(solution)/shard_map/ppermute | solution.py:317
  26.9 1.9 collective-permute-start.13
  31.5 1.5 collective-permute-start.6
  32.9 1.4 collective-permute-start.10
  34.4 5.5 %collective-permute-done.4.refs_0_ = bf16[48,4096]{1,0:T(8,128)(2,1)S(1)} collective-permute-done((bf16[48,4096]{1,0:T(8,128)(2,1)S(1)}, bf16[48,4096]{1,0:T(8,128)(2,1)S(1)}, u32[]{:S(2)}, u32[]{:S(2)}) %collective-permute-start.4) | collective-permute-done | bytes 393248 | tf_op jit(solution)/shard_map/ppermute | solution.py:306
  41.6 2.9 %collective-permute-start.5 = (f32[1,768]{1,0:T(1,128)S(1)}, f32[1,768]{1,0:T(1,128)S(1)}, u32[]{:S(2)}, u32[]{:S(2)}) collective-permute-start(f32[1,768]{1,0:T(1,128)S(1)} %collective-permute-done.refs_14_), channel_id=1, source_target_pairs={{0,32},{32,0},{1,33},{33,1},{2,34},{34,2},{3,35},{35,3},{4,36},{36... | collective-permute-start | bytes 9224 | tf_op jit(solution)/shard_map/ppermute | solution.py:328
  44.5 2.7 %collective-permute-start.8 = (bf16[16,4096]{1,0:T(8,128)(2,1)S(1)}, bf16[16,4096]{1,0:T(8,128)(2,1)S(1)}, u32[]{:S(2)}, u32[]{:S(2)}) collective-permute-start(bf16[16,4096]{1,0:T(8,128)(2,1)S(1)} %slice.25), channel_id=1, source_target_pairs={{0,24},{8,0},{16,8},{24,16},{1,25},{9,1},{17,9},{25,17},{2,26},{10... | collective-permute-start | bytes 393224 | tf_op jit(solution)/shard_map/ppermute | solution.py:307
  47.2 1.4 collective-permute-start.12
  48.7 1.7 collective-permute-done.8.refs_3_
  50.4 2.0 %collective-permute-done.12.refs_7_ = bf16[16,4096]{1,0:T(8,128)(2,1)S(1)} collective-permute-done((bf16[16,4096]{1,0:T(8,128)(2,1)S(1)}, bf16[16,4096]{1,0:T(8,128)(2,1)S(1)}, u32[]{:S(2)}, u32[]{:S(2)}) %collective-permute-start.12) | collective-permute-done | bytes 131104 | tf_op jit(solution)/shard_map/ppermute | solution.py:307
  53.9 3.6 %join_rows.1 = (bf16[96,4096]{1,0:T(8,128)(2,1)}, bf16[96,4096]{1,0:T(8,128)(2,1)}, bf16[96,4096]{1,0:T(8,128)(2,1)}, bf16[96,4096]{1,0:T(8,128)(2,1)}) custom-call(bf16[48,4096]{1,0:T(8,128)(2,1)} %copy-done.5, bf16[48,4096]{1,0:T(8,128)(2,1)} %copy-done.7, bf16[32,4096]{1,0:T(8,128)(2,1)} %copy-done.9, bf16[16,4096]{1,0:T(8,128)(2,1)} %copy-done.12, ...), custom_call_target="tpu_custom_call" | custom-call | bytes 6291456 | tf_op jit(solution)/shard_map/join_rows/pallas_call | solution.py:81
  57.5 1.5 collective-permute-start.14
  60.5 2.4 %collective-permute-start.17 = (bf16[96,4096]{1,0:T(8,128)(2,1)}, bf16[96,4096]{1,0:T(8,128)(2,1)}, u32[]{:S(2)}, u32[]{:S(2)}) collective-permute-start(bf16[96,4096]{1,0:T(8,128)(2,1)} %get-tuple-element.43.refs_3_), channel_id=1, source_target_pairs={{0,24},{8,0},{16,8},{24,16},{1,25},{9,1},{17,9},{25,17},{2,26},{10... | collective-permute-start | bytes 2359304 | tf_op jit(solution)/shard_map/ppermute | solution.py:307
  62.9 13.7 %collective-permute-done.14.refs_4_ = bf16[96,4096]{1,0:T(8,128)(2,1)} collective-permute-done((bf16[96,4096]{1,0:T(8,128)(2,1)}, bf16[96,4096]{1,0:T(8,128)(2,1)}, u32[]{:S(2)}, u32[]{:S(2)}) %collective-permute-start.14) | collective-permute-done | bytes 786464 | tf_op jit(solution)/shard_map/ppermute | solution.py:306
  77.6 2.7 %collective-permute-done.16.refs_6_ = bf16[96,4096]{1,0:T(8,128)(2,1)} collective-permute-done((bf16[96,4096]{1,0:T(8,128)(2,1)}, bf16[96,4096]{1,0:T(8,128)(2,1)}, u32[]{:S(2)}, u32[]{:S(2)}) %collective-permute-start.16) | collective-permute-done | bytes 786464 | tf_op jit(solution)/shard_map/ppermute | solution.py:306
  80.2 5.6 %collective-permute-done.13.refs_11_.refs_8_.refs_7_ = bf16[4096,640]{1,0:T(8,128)(2,1)} collective-permute-done((bf16[4096,640]{1,0:T(8,128)(2,1)}, bf16[4096,640]{1,0:T(8,128)(2,1)}, u32[]{:S(2)}, u32[]{:S(2)}) %collective-permute-start.13) | collective-permute-done | bytes 5242912 | tf_op jit(solution)/shard_map/ppermute | solution.py:320
  85.8 4.2 %collective-permute-start.18 = (bf16[4096,640]{1,0:T(8,128)(2,1)}, bf16[4096,640]{1,0:T(8,128)(2,1)}, u32[]{:S(2)}, u32[]{:S(2)}) collective-permute-start(bf16[4096,640]{1,0:T(8,128)(2,1)} %collective-permute-done.13.refs_11_.refs_8_.refs_7_), channel_id=1, source_target_pairs={{0,32},{32,0},{1,33},{33,1},{2,34},{34,2},{3,35},{35,3},{4,36},{36... | collective-permute-start | bytes 15728648 | tf_op jit(solution)/shard_map/ppermute | solution.py:341
  95.0 1.5 collective-permute-start.22
  96.5 2.2 %collective-permute-done.18.refs_12_.refs_9_.refs_8_ = bf16[4096,640]{1,0:T(8,128)(2,1)} collective-permute-done((bf16[4096,640]{1,0:T(8,128)(2,1)}, bf16[4096,640]{1,0:T(8,128)(2,1)}, u32[]{:S(2)}, u32[]{:S(2)}) %collective-permute-start.18) | collective-permute-done | bytes 5242912 | tf_op jit(solution)/shard_map/ppermute | solution.py:341
  98.7 21.6 %first_rows.1 = (f32[16,128]{1,0:T(8,128)}, bf16[256,1280]{1,0:T(8,128)(2,1)}, f32[1,1280]{1,0:T(1,128)}) custom-call(bf16[96,4096]{1,0:T(8,128)(2,1)} %get-tuple-element.40.refs_0_, bf16[96,4096]{1,0:T(8,128)(2,1)} %get-tuple-element.41.refs_1_, bf16[96,4096]{1,0:T(8,128)(2,1)} %get-tuple-element.42.refs_2_, bf16[96,4096]{1,0:T(8,128)(2,1)} %get-tuple-element.43.refs_3_, ...), custom_call_target="tpu_custom_call" | custom-call | flops 1 | bytes 1 | tf_op jit(solution)/shard_map/first_rows/pallas_call | solution.py:247
  120.2 1.5 collective-permute-start.23
  121.7 1.6 collective-permute-done.19.refs_0_
  123.3 2.2 %collective-permute-start.24 = (bf16[96,4096]{1,0:T(8,128)(2,1)}, bf16[96,4096]{1,0:T(8,128)(2,1)}, u32[]{:S(2)}, u32[]{:S(2)}) collective-permute-start(bf16[96,4096]{1,0:T(8,128)(2,1)} %collective-permute-done.15.refs_5_), channel_id=1, source_target_pairs={{0,6},{2,0},{4,2},{6,4},{1,7},{3,1},{5,3},{7,5},{8,14},{10,8},{12,... | collective-permute-start | bytes 2359304 | tf_op jit(solution)/shard_map/ppermute | solution.py:307
  127.9 2.4 %collective-permute-start.26 = (bf16[96,4096]{1,0:T(8,128)(2,1)}, bf16[96,4096]{1,0:T(8,128)(2,1)}, u32[]{:S(2)}, u32[]{:S(2)}) collective-permute-start(bf16[96,4096]{1,0:T(8,128)(2,1)} %collective-permute-done.17.refs_7_), channel_id=1, source_target_pairs={{0,24},{8,0},{16,8},{24,16},{1,25},{9,1},{17,9},{25,17},{2,26},{10... | collective-permute-start | bytes 2359304 | tf_op jit(solution)/shard_map/ppermute | solution.py:307
  133.5 20.8 %next_rows.1 = f32[16,128]{1,0:T(8,128)S(1)} custom-call(bf16[96,4096]{1,0:T(8,128)(2,1)} %collective-permute-done.19.refs_0_, bf16[96,4096]{1,0:T(8,128)(2,1)} %collective-permute-done.20.refs_1_, bf16[96,4096]{1,0:T(8,128)(2,1)} %collective-permute-done.21.refs_2_, bf16[96,4096]{1,0:T(8,128)(2,1)} %collective-permute-done.22.refs_3_, ...), custom_call_target="tpu_custom_call" | custom-call | flops 1 | bytes 1 | tf_op jit(solution)/shard_map/next_rows/pallas_call | solution.py:247
  154.3 12.4 %last_rows.1 = f32[16,128]{1,0:T(8,128)S(1)} custom-call(bf16[96,4096]{1,0:T(8,128)(2,1)} %collective-permute-done.23.refs_0_, bf16[96,4096]{1,0:T(8,128)(2,1)} %collective-permute-done.24.refs_1_, bf16[96,4096]{1,0:T(8,128)(2,1)} %collective-permute-done.25.refs_2_, bf16[96,4096]{1,0:T(8,128)(2,1)} %collective-permute-done.26.refs_3_, s32[72]{0:T(128)S(1)} %copy-done.3, ...), custom_call_target="tpu_custom_call" | custom-call | flops 1 | bytes 1 | tf_op jit(solution)/shard_map/last_rows/pallas_call | solution.py:247
  166.8 18.0 %all_to_all.11 = f32[128,1,128]{2,1,0:T(1,128)} all-to-all(f32[128,1,128]{2,1,0:T(1,128)S(1)} %bitcast.18), channel_id=1, replica_groups=mesh['zh'=2,'c'=2,'x'=4,'y'=4,'zl'=2] {'zh','c','x','y','zl'}, dimensions={0} | all-to-all | bytes 131072 | tf_op jit(solution)/shard_map/all_to_all | solution.py:382
  184.8 1.5 influence.1
  (99 shorter events, 21.1 us)
Async XLA Ops:
  6.5 87.5 %copy-start.20 = (s32[2,2]{1,0:T(2,128)S(1)}, s32[2,2]{1,0:T(2,128)}, u32[]{:S(2)}) copy-start(s32[2,2]{1,0:T(2,128)} %param.11) | copy-start | bytes 52
  6.5 87.6 %copy-start.19 = (s32[32,2]{0,1:T(2,128)S(1)}, s32[32,2]{0,1:T(2,128)}, u32[]{:S(2)}) copy-start(s32[32,2]{0,1:T(2,128)} %param.9) | copy-start | bytes 772
  6.5 89.9 %all-gather.3.cloned.1.call-start = ((), (), s32[]{:S(2)}) async-start(), calls=%async_computation.1 | async-start | bytes 2162688 | tf_op jit(solution)/shard_map/all_gather | solution.py:321
  8.2 5.2 %collective-permute-start.1 = (bf16[8,4096]{1,0:T(8,128)(2,1)}, bf16[8,4096]{1,0:T(8,128)(2,1)S(1)}, u32[]{:S(2)}, u32[]{:S(2)}) collective-permute-start(bf16[8,4096]{1,0:T(8,128)(2,1)} %norm_rows.2), channel_id=1, source_target_pairs={{0,32},{32,33},{33,1},{1,0},{2,34},{34,35},{35,3},{3,2},{4,36},{36... | collective-permute-start | bytes 196616 | tf_op jit(solution)/shard_map/ppermute | solution.py:310
  14.0 117.7 %all-gather.5.cloned.1.call-start = ((), (), s32[]{:S(2)}) async-start(), calls=%async_computation.2 | async-start | bytes 4456448 | tf_op jit(solution)/shard_map/all_gather | solution.py:322
  14.1 12.8 %collective-permute-start.2 = (bf16[96,4096]{1,0:T(8,128)(2,1)}, bf16[96,4096]{1,0:T(8,128)(2,1)S(1)}, u32[]{:S(2)}, u32[]{:S(2)}) collective-permute-start(bf16[96,4096]{1,0:T(8,128)(2,1)} %get-tuple-element.35), channel_id=1, source_target_pairs={{0,32},{32,33},{33,1},{1,0},{2,34},{34,35},{35,3},{3,2},{4,36},{36... | collective-permute-start | bytes 2359304 | tf_op jit(solution)/shard_map/ppermute | solution.py:317
  14.8 12.1 %collective-permute-start.3 = (bf16[32,4096]{1,0:T(8,128)(2,1)}, bf16[32,4096]{1,0:T(8,128)(2,1)S(1)}, u32[]{:S(2)}, u32[]{:S(2)}) collective-permute-start(bf16[32,4096]{1,0:T(8,128)(2,1)} %get-tuple-element.36), channel_id=1, source_target_pairs={{0,32},{32,33},{33,1},{1,0},{2,34},{34,35},{35,3},{3,2},{4,36},{36... | collective-permute-start | bytes 786440 | tf_op jit(solution)/shard_map/ppermute | solution.py:317
  16.4 82.3 %copy-start.15 = (f32[1,768]{1,0:T(1,128)}, f32[1,768]{1,0:T(1,128)S(1)}, u32[]{:S(2)}) copy-start(f32[1,768]{1,0:T(1,128)S(1)} %reshape.21.refs_13_) | copy-start | bytes 9220
  16.4 10.5 %collective-permute-start = (f32[1,768]{1,0:T(1,128)S(1)}, f32[1,768]{1,0:T(1,128)S(1)}, u32[]{:S(2)}, u32[]{:S(2)}) collective-permute-start(f32[1,768]{1,0:T(1,128)S(1)} %reshape.21.refs_13_), channel_id=1, source_target_pairs={{0,32},{32,33},{33,1},{1,0},{2,34},{34,35},{35,3},{3,2},{4,36},{36... | collective-permute-start | bytes 9224 | tf_op jit(solution)/shard_map/ppermute | solution.py:317
  26.9 58.9 %collective-permute-start.13 = (bf16[4096,640]{1,0:T(8,128)(2,1)}, bf16[4096,640]{1,0:T(8,128)(2,1)}, u32[]{:S(2)}, u32[]{:S(2)}) collective-permute-start(bf16[4096,640]{1,0:T(8,128)(2,1)} %bitcast.10), channel_id=1, source_target_pairs={{0,32},{32,33},{33,1},{1,0},{2,34},{34,35},{35,3},{3,2},{4,36},{36... | collective-permute-start | bytes 15728648 | tf_op jit(solution)/shard_map/ppermute | solution.py:320
  28.9 11.0 %collective-permute-start.4 = (bf16[48,4096]{1,0:T(8,128)(2,1)S(1)}, bf16[48,4096]{1,0:T(8,128)(2,1)S(1)}, u32[]{:S(2)}, u32[]{:S(2)}) collective-permute-start(bf16[48,4096]{1,0:T(8,128)(2,1)S(1)} %get-tuple-element.62), channel_id=1, source_target_pairs={{0,8},{8,16},{16,24},{24,0},{1,9},{9,17},{17,25},{25,1},{2,10},{10... | collective-permute-start | bytes 1179656 | tf_op jit(solution)/shard_map/ppermute | solution.py:306
  30.2 11.1 %collective-permute-start.9 = (bf16[48,4096]{1,0:T(8,128)(2,1)S(1)}, bf16[48,4096]{1,0:T(8,128)(2,1)S(1)}, u32[]{:S(2)}, u32[]{:S(2)}) collective-permute-start(bf16[48,4096]{1,0:T(8,128)(2,1)S(1)} %get-tuple-element.61), channel_id=1, source_target_pairs={{0,2},{2,4},{4,6},{6,0},{1,3},{3,5},{5,7},{7,1},{8,10},{10,12},{12... | collective-permute-start | bytes 1179656 | tf_op jit(solution)/shard_map/ppermute | solution.py:306
  31.5 10.1 %collective-permute-start.6 = (bf16[48,4096]{1,0:T(8,128)(2,1)S(1)}, bf16[48,4096]{1,0:T(8,128)(2,1)S(1)}, u32[]{:S(2)}, u32[]{:S(2)}) collective-permute-start(bf16[48,4096]{1,0:T(8,128)(2,1)S(1)} %get-tuple-element.62), channel_id=1, source_target_pairs={{0,24},{8,0},{16,8},{24,16},{1,25},{9,1},{17,9},{25,17},{2,26},{10... | collective-permute-start | bytes 1179656 | tf_op jit(solution)/shard_map/ppermute | solution.py:307
  32.9 11.5 %collective-permute-start.10 = (bf16[48,4096]{1,0:T(8,128)(2,1)S(1)}, bf16[48,4096]{1,0:T(8,128)(2,1)S(1)}, u32[]{:S(2)}, u32[]{:S(2)}) collective-permute-start(bf16[48,4096]{1,0:T(8,128)(2,1)S(1)} %get-tuple-element.61), channel_id=1, source_target_pairs={{0,6},{2,0},{4,2},{6,4},{1,7},{3,1},{5,3},{7,5},{8,14},{10,8},{12,... | collective-permute-start | bytes 1179656 | tf_op jit(solution)/shard_map/ppermute | solution.py:307
  39.9 12.5 %collective-permute-start.7 = (bf16[32,4096]{1,0:T(8,128)(2,1)S(1)}, bf16[32,4096]{1,0:T(8,128)(2,1)S(1)}, u32[]{:S(2)}, u32[]{:S(2)}) collective-permute-start(bf16[32,4096]{1,0:T(8,128)(2,1)S(1)} %slice.24), channel_id=1, source_target_pairs={{0,8},{8,16},{16,24},{24,0},{1,9},{9,17},{17,25},{25,1},{2,10},{10... | collective-permute-start | bytes 786440 | tf_op jit(solution)/shard_map/ppermute | solution.py:306
  41.3 11.1 %collective-permute-start.11 = (bf16[32,4096]{1,0:T(8,128)(2,1)S(1)}, bf16[32,4096]{1,0:T(8,128)(2,1)S(1)}, u32[]{:S(2)}, u32[]{:S(2)}) collective-permute-start(bf16[32,4096]{1,0:T(8,128)(2,1)S(1)} %slice.26), channel_id=1, source_target_pairs={{0,2},{2,4},{4,6},{6,0},{1,3},{3,5},{5,7},{7,1},{8,10},{10,12},{12... | collective-permute-start | bytes 786440 | tf_op jit(solution)/shard_map/ppermute | solution.py:306
  41.6 5.6 %collective-permute-start.5 = (f32[1,768]{1,0:T(1,128)S(1)}, f32[1,768]{1,0:T(1,128)S(1)}, u32[]{:S(2)}, u32[]{:S(2)}) collective-permute-start(f32[1,768]{1,0:T(1,128)S(1)} %collective-permute-done.refs_14_), channel_id=1, source_target_pairs={{0,32},{32,0},{1,33},{33,1},{2,34},{34,2},{3,35},{35,3},{4,36},{36... | collective-permute-start | bytes 9224 | tf_op jit(solution)/shard_map/ppermute | solution.py:328
  44.5 5.9 %collective-permute-start.8 = (bf16[16,4096]{1,0:T(8,128)(2,1)S(1)}, bf16[16,4096]{1,0:T(8,128)(2,1)S(1)}, u32[]{:S(2)}, u32[]{:S(2)}) collective-permute-start(bf16[16,4096]{1,0:T(8,128)(2,1)S(1)} %slice.25), channel_id=1, source_target_pairs={{0,24},{8,0},{16,8},{24,16},{1,25},{9,1},{17,9},{25,17},{2,26},{10... | collective-permute-start | bytes 393224 | tf_op jit(solution)/shard_map/ppermute | solution.py:307
  47.2 5.2 %collective-permute-start.12 = (bf16[16,4096]{1,0:T(8,128)(2,1)S(1)}, bf16[16,4096]{1,0:T(8,128)(2,1)S(1)}, u32[]{:S(2)}, u32[]{:S(2)}) collective-permute-start(bf16[16,4096]{1,0:T(8,128)(2,1)S(1)} %slice.27), channel_id=1, source_target_pairs={{0,6},{2,0},{4,2},{6,4},{1,7},{3,1},{5,3},{7,5},{8,14},{10,8},{12,... | collective-permute-start | bytes 393224 | tf_op jit(solution)/shard_map/ppermute | solution.py:307
  57.5 19.1 %collective-permute-start.14 = (bf16[96,4096]{1,0:T(8,128)(2,1)}, bf16[96,4096]{1,0:T(8,128)(2,1)}, u32[]{:S(2)}, u32[]{:S(2)}) collective-permute-start(bf16[96,4096]{1,0:T(8,128)(2,1)} %get-tuple-element.40.refs_0_), channel_id=1, source_target_pairs={{0,2},{2,4},{4,6},{6,0},{1,3},{3,5},{5,7},{7,1},{8,10},{10,12},{12... | collective-permute-start | bytes 2359304 | tf_op jit(solution)/shard_map/ppermute | solution.py:306
  59.0 18.6 %collective-permute-start.15 = (bf16[96,4096]{1,0:T(8,128)(2,1)}, bf16[96,4096]{1,0:T(8,128)(2,1)}, u32[]{:S(2)}, u32[]{:S(2)}) collective-permute-start(bf16[96,4096]{1,0:T(8,128)(2,1)} %get-tuple-element.41.refs_1_), channel_id=1, source_target_pairs={{0,6},{2,0},{4,2},{6,4},{1,7},{3,1},{5,3},{7,5},{8,14},{10,8},{12,... | collective-permute-start | bytes 2359304 | tf_op jit(solution)/shard_map/ppermute | solution.py:307
  60.2 20.0 %collective-permute-start.16 = (bf16[96,4096]{1,0:T(8,128)(2,1)}, bf16[96,4096]{1,0:T(8,128)(2,1)}, u32[]{:S(2)}, u32[]{:S(2)}) collective-permute-start(bf16[96,4096]{1,0:T(8,128)(2,1)} %get-tuple-element.42.refs_2_), channel_id=1, source_target_pairs={{0,8},{8,16},{16,24},{24,0},{1,9},{9,17},{17,25},{25,1},{2,10},{10... | collective-permute-start | bytes 2359304 | tf_op jit(solution)/shard_map/ppermute | solution.py:306
  60.5 19.7 %collective-permute-start.17 = (bf16[96,4096]{1,0:T(8,128)(2,1)}, bf16[96,4096]{1,0:T(8,128)(2,1)}, u32[]{:S(2)}, u32[]{:S(2)}) collective-permute-start(bf16[96,4096]{1,0:T(8,128)(2,1)} %get-tuple-element.43.refs_3_), channel_id=1, source_target_pairs={{0,24},{8,0},{16,8},{24,16},{1,25},{9,1},{17,9},{25,17},{2,26},{10... | collective-permute-start | bytes 2359304 | tf_op jit(solution)/shard_map/ppermute | solution.py:307
  85.8 12.8 %collective-permute-start.18 = (bf16[4096,640]{1,0:T(8,128)(2,1)}, bf16[4096,640]{1,0:T(8,128)(2,1)}, u32[]{:S(2)}, u32[]{:S(2)}) collective-permute-start(bf16[4096,640]{1,0:T(8,128)(2,1)} %collective-permute-done.13.refs_11_.refs_8_.refs_7_), channel_id=1, source_target_pairs={{0,32},{32,0},{1,33},{33,1},{2,34},{34,2},{3,35},{35,3},{4,36},{36... | collective-permute-start | bytes 15728648 | tf_op jit(solution)/shard_map/ppermute | solution.py:341
  90.0 33.3 %collective-permute-start.19 = (bf16[96,4096]{1,0:T(8,128)(2,1)}, bf16[96,4096]{1,0:T(8,128)(2,1)}, u32[]{:S(2)}, u32[]{:S(2)}) collective-permute-start(bf16[96,4096]{1,0:T(8,128)(2,1)} %get-tuple-element.41.refs_1_), channel_id=1, source_target_pairs={{0,2},{2,4},{4,6},{6,0},{1,3},{3,5},{5,7},{7,1},{8,10},{10,12},{12... | collective-permute-start | bytes 2359304 | tf_op jit(solution)/shard_map/ppermute | solution.py:306
  91.4 34.2 %collective-permute-start.20 = (bf16[96,4096]{1,0:T(8,128)(2,1)}, bf16[96,4096]{1,0:T(8,128)(2,1)}, u32[]{:S(2)}, u32[]{:S(2)}) collective-permute-start(bf16[96,4096]{1,0:T(8,128)(2,1)} %get-tuple-element.40.refs_0_), channel_id=1, source_target_pairs={{0,6},{2,0},{4,2},{6,4},{1,7},{3,1},{5,3},{7,5},{8,14},{10,8},{12,... | collective-permute-start | bytes 2359304 | tf_op jit(solution)/shard_map/ppermute | solution.py:307
  92.9 35.1 %collective-permute-start.21 = (bf16[96,4096]{1,0:T(8,128)(2,1)}, bf16[96,4096]{1,0:T(8,128)(2,1)}, u32[]{:S(2)}, u32[]{:S(2)}) collective-permute-start(bf16[96,4096]{1,0:T(8,128)(2,1)} %get-tuple-element.43.refs_3_), channel_id=1, source_target_pairs={{0,8},{8,16},{16,24},{24,0},{1,9},{9,17},{17,25},{25,1},{2,10},{10... | collective-permute-start | bytes 2359304 | tf_op jit(solution)/shard_map/ppermute | solution.py:306
  95.0 35.4 %collective-permute-start.22 = (bf16[96,4096]{1,0:T(8,128)(2,1)}, bf16[96,4096]{1,0:T(8,128)(2,1)}, u32[]{:S(2)}, u32[]{:S(2)}) collective-permute-start(bf16[96,4096]{1,0:T(8,128)(2,1)} %get-tuple-element.42.refs_2_), channel_id=1, source_target_pairs={{0,24},{8,0},{16,8},{24,16},{1,25},{9,1},{17,9},{25,17},{2,26},{10... | collective-permute-start | bytes 2359304 | tf_op jit(solution)/shard_map/ppermute | solution.py:307
  120.2 34.0 %collective-permute-start.23 = (bf16[96,4096]{1,0:T(8,128)(2,1)}, bf16[96,4096]{1,0:T(8,128)(2,1)}, u32[]{:S(2)}, u32[]{:S(2)}) collective-permute-start(bf16[96,4096]{1,0:T(8,128)(2,1)} %collective-permute-done.14.refs_4_), channel_id=1, source_target_pairs={{0,2},{2,4},{4,6},{6,0},{1,3},{3,5},{5,7},{7,1},{8,10},{10,12},{12... | collective-permute-start | bytes 2359304 | tf_op jit(solution)/shard_map/ppermute | solution.py:306
  123.3 31.0 %collective-permute-start.24 = (bf16[96,4096]{1,0:T(8,128)(2,1)}, bf16[96,4096]{1,0:T(8,128)(2,1)}, u32[]{:S(2)}, u32[]{:S(2)}) collective-permute-start(bf16[96,4096]{1,0:T(8,128)(2,1)} %collective-permute-done.15.refs_5_), channel_id=1, source_target_pairs={{0,6},{2,0},{4,2},{6,4},{1,7},{3,1},{5,3},{7,5},{8,14},{10,8},{12,... | collective-permute-start | bytes 2359304 | tf_op jit(solution)/shard_map/ppermute | solution.py:307
  125.6 28.7 %collective-permute-start.25 = (bf16[96,4096]{1,0:T(8,128)(2,1)}, bf16[96,4096]{1,0:T(8,128)(2,1)}, u32[]{:S(2)}, u32[]{:S(2)}) collective-permute-start(bf16[96,4096]{1,0:T(8,128)(2,1)} %collective-permute-done.16.refs_6_), channel_id=1, source_target_pairs={{0,8},{8,16},{16,24},{24,0},{1,9},{9,17},{17,25},{25,1},{2,10},{10... | collective-permute-start | bytes 2359304 | tf_op jit(solution)/shard_map/ppermute | solution.py:306
  127.9 26.4 %collective-permute-start.26 = (bf16[96,4096]{1,0:T(8,128)(2,1)}, bf16[96,4096]{1,0:T(8,128)(2,1)}, u32[]{:S(2)}, u32[]{:S(2)}) collective-permute-start(bf16[96,4096]{1,0:T(8,128)(2,1)} %collective-permute-done.17.refs_7_), channel_id=1, source_target_pairs={{0,24},{8,0},{16,8},{24,16},{1,25},{9,1},{17,9},{25,17},{2,26},{10... | collective-permute-start | bytes 2359304 | tf_op jit(solution)/shard_map/ppermute | solution.py:307
  (20 other events, 360.7 us)
Sparse Core Ops, SparseCore 0:
  14.1 47.1 all-gather.2
  63.5 68.1 all-gather.4
